TPU v7x, 32 devices: a whole 2x2x4 slice. The times are simulated.
32 devices in a mesh: groups: 2 (over x), ctx: 16 (over z, y, core).
Axes of the slice: x: 2, y: 2, z: 4, core: 2. Of those that a mesh axis runs over, the one named last changes fastest.
Arguments:
- query: bfloat16 [8192, 6144], P(('groups', 'ctx')), parts along dimension 0, may hold values from -6 to 6
- key_rows: bfloat16 [8192, 6144], P(('groups', 'ctx')), parts along dimension 0, may hold values from -0.59765625 to 0.59765625
- value_rows: bfloat16 [8192, 6144], P(('groups', 'ctx')), parts along dimension 0, may hold values from -60 to 60
- log_decay: float32 [8192, 48], P(('groups', 'ctx')), parts along dimension 0, may hold values from -1.2 to 0
- gate_input: bfloat16 [8192, 6144], P(('groups', 'ctx')), parts along dimension 0, may hold values from -6 to 6
- residual: bfloat16 [8192, 6144], P(('groups', 'ctx')), parts along dimension 0, may hold values from -60 to 60
- attn_gain: float32 [6144], replicated, may hold values from 0.1 to 1.9
- moe_gain: float32 [6144], replicated, may hold values from 0.1 to 1.9
- expert_ids: int32 [8192, 2], P(('groups', 'ctx')), parts along dimension 0, may hold values from 0 to 15, all different within a row; in each aligned block of 256 rows (0 to 255, 256 to 511, ...) at most 40 rows name the same one
Outputs:
- expert_rows: bfloat16 [32, 640, 6144], P(('groups', 'ctx')), parts along dimension 0
There are 2 independent parts, one for each index of `groups`. A program takes and returns all parts, laid end to end along the dimension named above; an argument that names none is the same for every part. Nothing has to cross between parts.
Inputs may be any that keep to these rules, and one draw needn't show every extreme that they name: `expert_ids`: in the rows of one device (aligned blocks of 256 rows) no expert is named more than 40 times, a bound that some block reaches; the two experts of a row differ.
All inputs are finite; a program needn't handle non-finite values.
Results may differ from a plain program's by a relative error of at most 0.0027.
Values may be sent and summed in bfloat16 or wider, within the bound.
No kernel may reach another device: no remote copies, remote signals or barrier semaphores. Data moves between devices by JAX's collectives and lax.ppermute only.
A program may use at most 256 MiB of HBM per device.

v0:
```python
import jax
import jax.numpy as jnp
from jax import lax
from jax.sharding import PartitionSpec as P

EXP_DEV = 1


def prefix(value, axis, combine, identity):
    peers, place = (lax.axis_size(axis), lax.axis_index(axis))
    everything = jax.tree.map(lambda part: lax.all_gather(part, axis), value)
    start = jax.tree.map(
        lambda part, zero: jnp.broadcast_to(jnp.asarray(zero, part.dtype), part.shape),
        value,
        identity,
    )

    def step(k, before):
        reached = k < place
        new = combine(before, jax.tree.map(lambda part: part[k], everything))
        return jax.tree.map(lambda a, b: jnp.where(reached, a, b), new, before)

    return lax.fori_loop(0, peers, step, start)


def block_summary(key_heads, value_heads, cumulative):
    final_log = cumulative[-1]
    weighted_keys = (jnp.exp(final_log - cumulative)[:, :, None] * key_heads).astype(jnp.bfloat16)
    block_state = jnp.einsum(
        "thd,the->hde", weighted_keys, value_heads, preferred_element_type=jnp.float32
    )
    return (block_state, jnp.exp(final_log))


def combine_states(earlier, latter):
    return (earlier[0] * latter[0], latter[0][:, None, None] * earlier[1] + latter[1])


def state_identity(head_count, head_dim):
    return (
        jnp.ones((head_count,), jnp.float32),
        jnp.zeros((head_count, head_dim, head_dim), jnp.float32),
    )


def body(
    query, key_rows, value_rows, log_decay, gate_input, residual, attn_gain, moe_gain, expert_ids
):
    tok_rows, model_width = query.shape
    head_count = log_decay.shape[1]
    head_dim = model_width // head_count
    query_heads = query.reshape(tok_rows, head_count, head_dim)
    key_heads = key_rows.reshape(tok_rows, head_count, head_dim)
    value_heads = value_rows.reshape(tok_rows, head_count, head_dim)
    cumulative = jnp.cumsum(log_decay, axis=0)
    half_heads = head_count // 2
    state_low, decay_low = block_summary(
        key_heads[:, :half_heads], value_heads[:, :half_heads], cumulative[:, :half_heads]
    )
    prefix_low = prefix(
        (decay_low, state_low), "ctx", combine_states, state_identity(half_heads, head_dim)
    )
    state_high, decay_high = block_summary(
        key_heads[:, half_heads:], value_heads[:, half_heads:], cumulative[:, half_heads:]
    )
    prefix_high = prefix(
        (decay_high, state_high),
        "ctx",
        combine_states,
        state_identity(head_count - half_heads, head_dim),
    )
    carried = jnp.concatenate([prefix_low[1], prefix_high[1]], axis=0)
    positions = jnp.arange(tok_rows, dtype=jnp.int32)
    causal_mask = positions[:, None] >= positions[None, :]
    score_block = jnp.einsum(
        "thd,shd->hts", query_heads, key_heads, preferred_element_type=jnp.float32
    )
    cum_heads = cumulative.T
    log_gap = jnp.where(causal_mask[None], cum_heads[:, :, None] - cum_heads[:, None, :], 0.0)
    intra_weights = jnp.where(causal_mask[None], score_block * jnp.exp(log_gap), 0.0).astype(
        jnp.bfloat16
    )
    intra_out = jnp.einsum(
        "hts,shd->thd", intra_weights, value_heads, preferred_element_type=jnp.float32
    )
    inter_out = jnp.exp(cumulative)[:, :, None] * jnp.einsum(
        "thd,hde->the", query_heads.astype(jnp.float32), carried, precision=lax.Precision.HIGHEST
    )
    attention = (intra_out + inter_out).reshape(tok_rows, model_width)
    branch_out = (
        attention
        * lax.rsqrt(jnp.mean(attention * attention, axis=-1, keepdims=True) + 1e-06)
        * attn_gain
        * jax.nn.sigmoid(gate_input.astype(jnp.float32))
    )
    hidden_rows = residual.astype(jnp.float32) + branch_out
    normed_rows = (
        hidden_rows
        * lax.rsqrt(jnp.mean(hidden_rows * hidden_rows, axis=-1, keepdims=True) + 1e-06)
        * moe_gain
    ).astype(jnp.bfloat16)
    top_count = expert_ids.shape[1]
    chain_size = lax.axis_size("ctx")
    expert_count = EXP_DEV * chain_size
    capacity = 5 * tok_rows * top_count // (4 * expert_count)
    pair_ids = expert_ids.reshape(-1)
    one_hot = (pair_ids[:, None] == jnp.arange(expert_count, dtype=jnp.int32)[None, :]).astype(
        jnp.int32
    )
    earlier_count = jnp.cumsum(one_hot, axis=0) - one_hot
    slot_index = jnp.sum(earlier_count * one_hot, axis=1)
    target_row = pair_ids * capacity + slot_index
    pair_rows = jnp.repeat(normed_rows, top_count, axis=0)
    outgoing = (
        jnp.zeros((expert_count * capacity, model_width), jnp.bfloat16)
        .at[target_row]
        .set(pair_rows)
    )
    arrived = lax.all_to_all(outgoing, "ctx", split_axis=0, concat_axis=0, tiled=True)
    arranged = arrived.reshape(chain_size, EXP_DEV, capacity, model_width).transpose(1, 0, 2, 3)
    return arranged.reshape(EXP_DEV, chain_size * capacity, model_width)


def solution(mesh):
    in_specs = (
        P(("groups", "ctx"), None),
        P(("groups", "ctx"), None),
        P(("groups", "ctx"), None),
        P(("groups", "ctx"), None),
        P(("groups", "ctx"), None),
        P(("groups", "ctx"), None),
        P(),
        P(),
        P(("groups", "ctx"), None),
    )
    out_specs = P(("groups", "ctx"), None, None)
    return jax.shard_map(body, mesh=mesh, in_specs=in_specs, out_specs=out_specs, check_vma=False)
```

profile of v0, /device:TPU:1, one launch (start us, length us, event | category | flops | bytes accessed | tf_op | source)
XLA Modules:
  0.0 590.0 jit_solution(2163318922698295580)
XLA Ops:
  6.5 1.0 copy_bitcast_fusion.1
  7.5 0.6 reduce-window.16
  8.1 0.2 slice_reduce_fusion
  8.4 0.2 slice_reduce_fusion.3
  8.6 4.7 copy.63
  13.3 2.6 copy.81
  15.9 2.3 fusion.45
  18.1 2.8 copy.72
  21.1 3.6 fusion.30
  24.7 2.8 copy.74
  27.6 3.6 fusion.31
  31.7 1.2 reduce-window.14
  32.8 0.2 slice_reduce_fusion.1
  33.1 0.1 copy.55
  33.4 22.9 %all-gather.2 = f32[16,1,24]{2,1,0:T(1,128)S(1)} all-gather(f32[1,1,24]{2,1,0:T(1,128)S(1)} %bitcast.121), channel_id=1, replica_groups=mesh['groups'=2,'ctx'=16] {'ctx'}, dimensions={0}, use_global_device_ids=true | all-gather | bytes 1632 | tf_op jit(solution)/shard_map/all_gather | solution.py:11
  56.3 17.3 %all-gather.3 = f32[16,1,24]{2,1,0:T(1,128)S(1)} all-gather(f32[1,1,24]{2,1,0:T(1,128)S(1)} %bitcast.120), channel_id=1, replica_groups=mesh['groups'=2,'ctx'=16] {'ctx'}, dimensions={0}, use_global_device_ids=true | all-gather | bytes 1632 | tf_op jit(solution)/shard_map/all_gather | solution.py:11
  73.9 9.0 %fusion.2 = f32[48,256,128]{1,2,0:T(8,128)} fusion(bf16[256,48,128]{0,2,1:T(8,128)(2,1)} %bitcast.112, f32[48,256]{1,0:T(8,128)S(1)} %get-tuple-element.262, pred[256,256]{1,0:T(8,128)(4,1)S(1)} %iota_compare_fusion, bf16[256,6144]{1,0:T(8,128)(2,1)} %param.14, bf16[256,6144]{1,0:T(8,128)(2,1)S(1)} %copy-done), kind=kOutput, calls=%fused_computation.8 | convolution fusion | flops 1626341376 | bytes 15843328 | tf_op jit(solution)/shard_map/hts,shd->thd/dot_general | solution.py:83
  82.8 73.2 %all-gather.7.cloned.1.call-done = f32[384,128,128]{2,1,0:T(8,128)} async-done(((f32[24,128,128]{2,1,0:T(8,128)}), f32[384,128,128]{2,1,0:T(8,128)}) %all-gather.7.cloned.1.call-update) | async-done | bytes 25165840 | tf_op jit(solution)/shard_map/all_gather | solution.py:11
  156.0 53.6 %while.28 = (s32[]{:T(128)}, f32[24,128,128]{2,1,0:T(8,128)}, s32[]{:T(128)}, f32[16,24]{1,0:T(8,128)S(1)}, f32[16,24,128,128]{3,2,1,0:T(8,128)}, /*index=5*/s32[]{:T(128)}, s32[]{:T(128)}) while((s32[]{:T(128)}, f32[24,128,128]{2,1,0:T(8,128)}, s32[]{:T(128)}, f32[16,24]{1,0:T(8,128)S(1)}, f32[16,24,128,128]{3,2,1,0:T(8,128)}, ...), condition=%wide.region_6.7_spmd.clone, body=%wide.region_5.6_spmd.clone.sunk | while | flops 1572868 | bytes 4718985 | solution.py:23
  156.0 2.9 fusion.53
  158.9 3.3 fusion.53
  162.2 3.3 fusion.53
  165.6 3.3 fusion.53
  168.9 3.3 fusion.53
  172.3 3.3 fusion.53
  175.6 3.4 fusion.53
  179.0 3.5 fusion.53
  182.5 3.5 fusion.53
  186.0 3.3 fusion.53
  189.3 3.3 fusion.53
  192.7 3.4 fusion.53
  196.1 3.4 fusion.53
  199.5 3.5 fusion.53
  203.0 3.3 fusion.53
  206.3 3.3 fusion.53
  209.6 3.1 copy.68
  212.8 73.5 %all-gather.9.cloned.1.call-done = f32[384,128,128]{2,1,0:T(8,128)} async-done(((f32[24,128,128]{2,1,0:T(8,128)}), f32[384,128,128]{2,1,0:T(8,128)}) %all-gather.9.cloned.1.call-update) | async-done | bytes 25165840 | tf_op jit(solution)/shard_map/all_gather | solution.py:11
  286.3 53.1 %while.29 = (s32[]{:T(128)}, f32[24,128,128]{2,1,0:T(8,128)}, s32[]{:T(128)}, f32[16,24]{1,0:T(8,128)S(1)}, f32[16,24,128,128]{3,2,1,0:T(8,128)}, /*index=5*/s32[]{:T(128)}, s32[]{:T(128)}) while((s32[]{:T(128)}, f32[24,128,128]{2,1,0:T(8,128)}, s32[]{:T(128)}, f32[16,24]{1,0:T(8,128)S(1)}, f32[16,24,128,128]{3,2,1,0:T(8,128)}, ...), condition=%wide.region_8.9_spmd.clone, body=%wide.region_7.8_spmd.clone.sunk | while | flops 1572868 | bytes 4718985 | solution.py:23
  286.3 2.9 fusion.54
  289.2 3.3 fusion.54
  292.5 3.3 fusion.54
  295.9 3.3 fusion.54
  299.2 3.3 fusion.54
  302.6 3.3 fusion.54
  305.9 3.3 fusion.54
  309.3 3.3 fusion.54
  312.6 3.3 fusion.54
  316.0 3.3 fusion.54
  319.3 3.3 fusion.54
  322.7 3.3 fusion.54
  326.0 3.3 fusion.54
  329.3 3.3 fusion.54
  332.7 3.3 fusion.54
  336.0 3.3 fusion.54
  339.4 3.0 copy.69
  342.4 9.9 %multiply_reduce_fusion.1 = (f32[256]{0:T(256)S(1)}, f32[256,48,128]{0,2,1:T(8,128)}) fusion(f32[24,128,128]{1,2,0:T(8,128)} %copy.69, f32[24,128,128]{1,2,0:T(8,128)} %copy.68, f32[256,48]{0,1:T(8,128)S(1)} %bitcast_exponential_fusion, f32[48,256,128]{1,2,0:T(8,128)} %fusion.2, bf16[256,6144]{1,0:T(8,128)(2,1)S(1)} %copy-done), kind=kOutput, calls=%fused_computation.14 | convolution fusion | flops 2422996736 | bytes 18924544 | tf_op jit(solution)/shard_map/thd,hde->the/dot_general | solution.py:86
  352.3 6.8 %copy.71 = f32[256,6144]{1,0:T(8,128)} copy(f32[256,6144]{0,1:T(8,128)} %bitcast.108) | data formatting | bytes 12582912 | tf_op jit(solution)/shard_map/reshape | solution.py:89
  359.1 5.6 multiply_reduce_fusion
  364.8 0.9 multiply_convert_fusion
  365.6 5.1 broadcast_in_dim.42
  370.8 13.3 %reshape.142 = bf16[512,6144]{1,0:T(8,128)(2,1)} reshape(bf16[256,2,6144]{2,1,0:T(2,128)(2,1)} %broadcast_in_dim.42) | data formatting | bytes 12582912 | tf_op jit(solution)/shard_map/reshape | solution.py:113
  384.1 15.3 %scatter_custom_fusion = bf16[640,6144]{1,0:T(8,128)(2,1)} fusion(s32[512]{0:T(512)S(1)} %bitcast.119, bf16[512,6144]{1,0:T(8,128)(2,1)} %reshape.142, bf16[]{:T(256)} %constant.66.clone.1), kind=kCustom, calls=%fused_computation.20 | custom fusion | bytes 7864832 | tf_op jit(solution)/shard_map/scatter | solution.py:117
  399.4 176.2 %all_to_all.9 = bf16[16,40,6144]{2,1,0:T(8,128)(2,1)} all-to-all(bf16[16,40,6144]{2,1,0:T(8,128)(2,1)} %bitcast.106), channel_id=1, replica_groups=mesh['groups'=2,'ctx'=16] {'ctx'}, dimensions={0} | all-to-all | bytes 15728640 | tf_op jit(solution)/shard_map/all_to_all | solution.py:119
  575.6 7.6 %copy.120 = bf16[1,640,6144]{2,1,0:T(8,128)(2,1)} copy(bf16[1,640,6144]{2,1,0:T(8,128)(2,1)} %bitcast.107) | data formatting | bytes 15728640
  (68 shorter events, 1.3 us)
Async XLA Ops:
  6.5 67.3 %copy-start = (bf16[256,6144]{1,0:T(8,128)(2,1)S(1)}, bf16[256,6144]{1,0:T(8,128)(2,1)}, u32[]{:S(2)}) copy-start(bf16[256,6144]{1,0:T(8,128)(2,1)} %param.13) | copy-start | bytes 9437188
  6.5 149.5 %all-gather.7.cloned.1.call-start = ((), (), s32[]{:S(2)}) async-start(), calls=%async_computation.1 | async-start | bytes 26738688 | tf_op jit(solution)/shard_map/all_gather | solution.py:11
  24.7 261.6 %all-gather.9.cloned.1.call-start = ((), (), s32[]{:S(2)}) async-start(), calls=%async_computation.2 | async-start | bytes 26738688 | tf_op jit(solution)/shard_map/all_gather | solution.py:11
  27.6 3.7 copy-start.5
  352.3 6.8 %copy-start.2 = (bf16[256,6144]{1,0:T(8,128)(2,1)S(1)}, bf16[256,6144]{1,0:T(8,128)(2,1)}, u32[]{:S(2)}) copy-start(bf16[256,6144]{1,0:T(8,128)(2,1)} %param.17) | copy-start | bytes 9437188
  352.3 6.8 %copy-start.4 = (f32[6144]{0:T(1024)S(1)}, f32[6144]{0:T(1024)}, u32[]{:S(2)}) copy-start(f32[6144]{0:T(1024)} %param.19) | copy-start | bytes 73732
  359.1 5.7 copy-start.3
  575.6 7.6 %copy-start.1 = (bf16[256,6144]{1,0:T(8,128)(2,1)S(1)}, bf16[256,6144]{1,0:T(8,128)(2,1)}, u32[]{:S(2)}) copy-start(bf16[256,6144]{1,0:T(8,128)(2,1)} %param.13) | copy-start | bytes 9437188
Sparse Core Ops, SparseCore 0:
  24.8 131.1 all-gather.6
  157.6 128.6 all-gather.8
where the time goes:
time: 591 us; the launch traced here: 590 us
  blocking collectives  216 us (37%)
  waiting for transfers between devices  147 us (25%)
  other arithmetic  115 us (19%)
  local copies, waits for them, and re-layouts  71.9 us (12%)
  matrix products  26 us (4%)
  between operations  13.6 us (2%)
    all_to_all x1, blocking collectives, body(): lax.all_to_all(outgoing, 'ctx', split_axis=0, concat_axis=0, tiled=True)  176 us
    all_gather x2, waiting for transfers between devices, prefix(): everything = jax.tree.map(lambda part: lax.all_gather(part, axis), value)  147 us
    select_n x32, other arithmetic, step(): return jax.tree.map(lambda a, b: jnp.where(reached, a, b), new, before)  106 us
    all_gather x2, blocking collectives, prefix(): everything = jax.tree.map(lambda part: lax.all_gather(part, axis), value)  40.2 us
    unnamed x18, local copies, waits for them, and re-layouts  20.7 us
    scatter x1, local copies, waits for them, and re-layouts, body(): outgoing = jnp.zeros((expert_count * capacity, model_width), jnp.bfloat16...  15.3 us
    reshape x1, local copies, waits for them, and re-layouts, body(): pair_rows = jnp.repeat(normed_rows, top_count, axis=0)  13.3 us
  transfers between devices with their start and end apart: 2, of which 2 were waited for; matrix products, arithmetic and copies ran while one was open for 13% of the time, Pallas kernels for 0%

commit v1 on v0

v1 whole, which is shorter than its diff:
```python
import functools
import jax
import jax.numpy as jnp
from jax import lax
from jax.experimental import pallas as pl
from jax.experimental.pallas import tpu as pltpu
from jax.sharding import PartitionSpec as P

EXP_DEV = 1
SLOTS = 4
CHUNKS = 3
EXACT = lax.Precision.HIGHEST
F32 = jnp.float32
BF16 = jnp.bfloat16


def dot(a, b, contract, precision=None):
    return lax.dot_general(
        a, b, ((contract[:1], contract[1:]), ((), ())), precision=precision, preferred_element_type=F32
    )


def group_decay(ld_ref, first, count):
    heads = ld_ref.shape[1]
    row = lax.broadcasted_iota(jnp.int32, (heads, count), 0)
    col = lax.broadcasted_iota(jnp.int32, (heads, count), 1)
    pick = (row == first + col).astype(F32)
    return dot(ld_ref[...], pick, (1, 0), EXACT)


def running(ld):
    tok = ld.shape[0]
    row = lax.broadcasted_iota(jnp.int32, (tok, tok), 0)
    col = lax.broadcasted_iota(jnp.int32, (tok, tok), 1)
    return dot((row >= col).astype(F32), ld, (1, 0), EXACT)


def running_rows(ld):
    tok = ld.shape[0]
    row = lax.broadcasted_iota(jnp.int32, (tok, tok), 0)
    col = lax.broadcasted_iota(jnp.int32, (tok, tok), 1)
    return dot(ld, (row <= col).astype(F32), (0, 0), EXACT)


def state_kernel(first_slot, hd, place, k_ref, v_ref, ld_ref, *outs):
    gh = k_ref.shape[1] // hd
    group = jnp.bitwise_xor(pl.program_id(0) + first_slot, place[0])
    cum = running(group_decay(ld_ref, group * gh, gh))
    weight = jnp.exp(cum[-1:, :] - cum)
    per = gh // len(outs)
    for i in range(gh):
        cols = slice(i * hd, (i + 1) * hd)
        wk = (weight[:, i : i + 1] * k_ref[:, cols].astype(F32)).astype(BF16)
        outs[i // per][0, i % per] = dot(wk, v_ref[:, cols], (0, 0))


def block_states(place, key_rows, value_rows, log_decay, first_slot, hd):
    tok, width = key_rows.shape
    gw = width // SLOTS
    gh = gw // hd
    per = gh // CHUNKS
    cols = lambda i, s: (0, jnp.bitwise_xor(i + first_slot, s[0]))
    return pl.pallas_call(
        functools.partial(state_kernel, first_slot, hd),
        grid_spec=pltpu.PrefetchScalarGridSpec(
            num_scalar_prefetch=1,
            grid=(2,),
            in_specs=[
                pl.BlockSpec((tok, gw), cols),
                pl.BlockSpec((tok, gw), cols),
                pl.BlockSpec(log_decay.shape, lambda i, s: (0, 0)),
            ],
            out_specs=[pl.BlockSpec((1, per, hd, hd), lambda i, s: (i, 0, 0, 0))] * CHUNKS,
        ),
        out_shape=[jax.ShapeDtypeStruct((2, per, hd, hd), F32)] * CHUNKS,
        compiler_params=pltpu.CompilerParams(vmem_limit_bytes=32 << 20),
        cost_estimate=pl.CostEstimate(
            flops=tok * width * hd, bytes_accessed=2 * tok * width + 2 * width * hd, transcendentals=tok * width // hd
        ),
        name="block_states",
    )(place, key_rows, value_rows, log_decay)


def intra_kernel(hd, q_ref, k_ref, v_ref, ld_ref, o_ref):
    tok = q_ref.shape[0]
    gh = q_ref.shape[1] // hd
    half = tok // 2
    ld = group_decay(ld_ref, pl.program_id(0) * gh, gh)
    cum = running(ld)
    cum_rows = running_rows(ld)
    for i in range(gh):
        cols = slice(i * hd, (i + 1) * hd)
        for first, seen in ((0, half), (half, tok)):
            score = dot(q_ref[first : first + half, cols], k_ref[:seen, cols], (1, 1))
            gap = cum[first : first + half, i : i + 1] - cum_rows[i : i + 1, :seen]
            row = lax.broadcasted_iota(jnp.int32, (half, seen), 0) + first
            col = lax.broadcasted_iota(jnp.int32, (half, seen), 1)
            weights = jnp.where(row >= col, score * jnp.exp(gap), 0.0).astype(BF16)
            o_ref[first : first + half, cols] = dot(weights, v_ref[:seen, cols], (1, 0))


def intra(query, key_rows, value_rows, log_decay, hd):
    tok, width = query.shape
    steps = 8
    block = pl.BlockSpec((tok, width // steps), lambda i: (0, i))
    return pl.pallas_call(
        functools.partial(intra_kernel, hd),
        grid=(steps,),
        in_specs=[block, block, block, pl.BlockSpec(log_decay.shape, lambda i: (0, 0))],
        out_specs=block,
        out_shape=jax.ShapeDtypeStruct((tok, width), F32),
        compiler_params=pltpu.CompilerParams(vmem_limit_bytes=32 << 20),
        cost_estimate=pl.CostEstimate(
            flops=3 * tok * tok * width, bytes_accessed=10 * tok * width, transcendentals=tok * tok * width // hd
        ),
        name="intra",
    )(query, key_rows, value_rows, log_decay)


def finish_kernel(
    hd, cap, row_steps, out_steps, place, q_ref, in_ref, ld_ref, gate_ref, res_ref, ag_ref, mg_ref, ids_ref, *rest
):
    states = rest[: 2 * CHUNKS]
    o_ref, att, normed, target = rest[2 * CHUNKS :]
    tok, width = att.shape
    gh = q_ref.shape[1] // hd
    per = gh // CHUNKS
    step = pl.program_id(0)

    for slot in range(SLOTS):

        @pl.when(step == slot)
        def _():
            group = jnp.bitwise_xor(slot, place[0])
            grow = jnp.exp(running(group_decay(ld_ref, group * gh, gh)))
            for i in range(gh):
                cols = slice(i * hd, (i + 1) * hd)
                carried = states[(slot // 2) * CHUNKS + i // per][slot % 2, i % per]
                high = carried.astype(BF16)
                low = (carried - high.astype(F32)).astype(BF16)
                q = q_ref[:, cols]
                inter = dot(q, high, (1, 0)) + dot(q, low, (1, 0))
                where = pl.ds(pl.multiple_of(group * (gh * hd) + i * hd, hd), hd)
                att[:, where] = in_ref[:, cols] + grow[:, i : i + 1] * inter

    rows = tok // row_steps

    @pl.when((step >= SLOTS) & (step < SLOTS + row_steps))
    def _():
        at = pl.ds(pl.multiple_of((step - SLOTS) * rows, rows), rows)
        a = att[at, :]
        scale = lax.rsqrt(jnp.mean(a * a, axis=-1, keepdims=True) + 1e-06)
        branch = a * scale * ag_ref[...] * jax.nn.sigmoid(gate_ref[...].astype(F32))
        hidden = res_ref[...].astype(F32) + branch
        scale = lax.rsqrt(jnp.mean(hidden * hidden, axis=-1, keepdims=True) + 1e-06)
        normed[at, :] = (hidden * scale * mg_ref[...]).astype(BF16)

    @pl.when(step == SLOTS + row_steps)
    def _():
        top = ids_ref.shape[0]
        experts = out_steps * o_ref.shape[0] // cap
        ids = ids_ref[...]
        expert = lax.broadcasted_iota(jnp.int32, (experts, tok), 0)
        hot = [(ids[k : k + 1, :] == expert).astype(F32) for k in range(top)]
        row = lax.broadcasted_iota(jnp.int32, (tok, tok), 0)
        col = lax.broadcasted_iota(jnp.int32, (tok, tok), 1)
        count = dot(sum(hot).astype(BF16), (row < col).astype(BF16), (1, 0))
        for k in range(top):
            slot = jnp.sum(hot[k] * count, axis=0, keepdims=True).astype(jnp.int32)
            target[k : k + 1, :] = ids[k : k + 1, :] * cap + slot
            count = count + hot[k]

    @pl.when(step >= SLOTS + row_steps)
    def _():
        out_rows = o_ref.shape[0]
        base = (step - SLOTS - row_steps) * out_rows
        row = lax.broadcasted_iota(jnp.int32, (out_rows, tok), 0) + base
        hit = row == target[0:1, :]
        for k in range(1, ids_ref.shape[0]):
            hit = hit | (row == target[k : k + 1, :])
        pick = hit.astype(F32).astype(BF16)
        part = width // 4
        for n in range(4):
            cols = slice(n * part, (n + 1) * part)
            o_ref[:, cols] = dot(pick, normed[:, cols], (1, 0)).astype(BF16)


def finish(place, query, intra_out, log_decay, gate, residual, attn_gain, moe_gain, ids, states, cap, experts, hd):
    tok, width = query.shape
    gw = width // SLOTS
    row_steps, out_steps = 4, 4
    out_rows = experts * cap // out_steps
    last = SLOTS - 1
    cols = lambda i, s: (0, jnp.bitwise_xor(jnp.minimum(i, last), s[0]))
    rows = lambda i, s: (jnp.clip(i - SLOTS, 0, row_steps - 1), 0)
    whole = lambda i, s: (0, 0)
    return pl.pallas_call(
        functools.partial(finish_kernel, hd, cap, row_steps, out_steps),
        grid_spec=pltpu.PrefetchScalarGridSpec(
            num_scalar_prefetch=1,
            grid=(SLOTS + row_steps + out_steps,),
            in_specs=[
                pl.BlockSpec((tok, gw), cols),
                pl.BlockSpec((tok, gw), cols),
                pl.BlockSpec(log_decay.shape, whole),
                pl.BlockSpec((tok // row_steps, width), rows),
                pl.BlockSpec((tok // row_steps, width), rows),
                pl.BlockSpec((1, width), whole),
                pl.BlockSpec((1, width), whole),
                pl.BlockSpec(ids.shape, whole),
            ]
            + [pl.BlockSpec(s.shape, lambda i, s: (0, 0, 0, 0)) for s in states],
            out_specs=pl.BlockSpec((out_rows, width), lambda i, s: (jnp.maximum(i - SLOTS - row_steps, 0), 0)),
            scratch_shapes=[
                pltpu.VMEM((tok, width), F32),
                pltpu.VMEM((tok, width), BF16),
                pltpu.VMEM((8, tok), jnp.int32),
            ],
        ),
        out_shape=jax.ShapeDtypeStruct((experts * cap, width), BF16),
        compiler_params=pltpu.CompilerParams(vmem_limit_bytes=48 << 20),
        cost_estimate=pl.CostEstimate(
            flops=4 * tok * width * hd, bytes_accessed=20 * tok * width, transcendentals=tok * width
        ),
        name="finish",
    )(place, query, intra_out, log_decay, gate, residual, attn_gain[None], moe_gain[None], ids, *states)


def swap(value, bit):
    size = lax.axis_size("ctx")
    return lax.ppermute(value, "ctx", [(i, i ^ bit) for i in range(size)])


def carried_states(index, place, keep, send, log_decay):
    size = lax.axis_size("ctx")
    rows = size // SLOTS
    core, side = index % 2, (index // 2) % 2
    heads = log_decay.shape[1]
    own = jnp.exp(jnp.sum(log_decay, axis=0))
    decay = jnp.stack([own, swap(own, 1), swap(own, 2), swap(own, 3)]).reshape(4, SLOTS, CHUNKS, -1)
    near = [lax.dynamic_index_in_dim(decay, jnp.bitwise_xor(j, place), 1, keepdims=False) for j in range(2)]
    near = jnp.stack(near, axis=1)[..., None, None]
    one = jnp.float32(1)

    received = [swap(s, 1) for s in send]
    mine, rest = [], []
    for k in range(CHUNKS):
        d_own, d_core = near[0, :, k], near[1, :, k]
        total = jnp.where(core == 0, d_core, one) * keep[k] + jnp.where(core == 0, one, d_own) * received[k]
        first = jnp.where(core == 0, keep[k], received[k])
        d_first = jnp.where(core == 0, d_own, d_core)
        chip = d_own[0] * d_core[0]
        chip_other = near[2, 0, k] * near[3, 0, k]
        other = swap(total[1], 2)
        row_total = jnp.where(side == 0, chip_other, one) * total[0] + jnp.where(side == 0, one, chip) * other
        row_decay = chip * chip_other
        upper = jnp.where(side == 0, total[0], other)
        d_upper = jnp.where(side == 0, chip, chip_other)
        before = jnp.zeros_like(row_total)
        for s in range(rows - 1):
            pairs = [(s * SLOTS + j, (s + 1) * SLOTS + j) for j in range(SLOTS)]
            before = before + lax.ppermute(row_decay * before + row_total, "ctx", pairs)
        lower = d_upper * before + upper
        there = swap(jnp.where(side == 0, lower, before), 2)
        here = jnp.where(side == 0, before, lower)
        pair = jnp.stack([here, there])
        second = d_first * pair + first
        rest.append(swap(jnp.where(core == 0, second, pair), 1))
        mine.append(jnp.where(core == 0, pair, second))
    return mine + rest


def body(
    query, key_rows, value_rows, log_decay, gate_input, residual, attn_gain, moe_gain, expert_ids
):
    tok_rows, model_width = query.shape
    hd = model_width // log_decay.shape[1]
    index = lax.axis_index("ctx")
    place = (index % 2) * 2 + (index // 2) % 2
    place_ref = place.astype(jnp.int32)[None]
    send = block_states(place_ref, key_rows, value_rows, log_decay, 2, hd)
    keep = block_states(place_ref, key_rows, value_rows, log_decay, 0, hd)
    states = carried_states(index, place, keep, send, log_decay)
    intra_out = intra(query, key_rows, value_rows, log_decay, hd)
    top_count = expert_ids.shape[1]
    expert_count = EXP_DEV * lax.axis_size("ctx")
    capacity = 5 * tok_rows * top_count // (4 * expert_count)
    outgoing = finish(
        place_ref, query, intra_out, log_decay, gate_input, residual, attn_gain, moe_gain,
        expert_ids.T, states, capacity, expert_count, hd,
    )
    arrived = lax.all_to_all(outgoing, "ctx", split_axis=0, concat_axis=0, tiled=True)
    return arrived[None]


def solution(mesh):
    rows = P(("groups", "ctx"), None)
    in_specs = (rows, rows, rows, rows, rows, rows, P(), P(), rows)
    out_specs = P(("groups", "ctx"), None, None)
    return jax.shard_map(body, mesh=mesh, in_specs=in_specs, out_specs=out_specs, check_vma=False)
```

time: 591 us -> 311 us (0.53)
  waiting for transfers between devices: 147 us -> 17 us
  other arithmetic: 115 us -> 9.91 us
  local copies, waits for them, and re-layouts: 71.9 us -> 20.3 us
  Pallas kernels: 0 us -> 42.9 us
  starting transfers between devices: 0.04 us -> 31.3 us
  blocking collectives: 216 us -> 188 us
  matrix products: 26 us -> 0 us
  between operations: 13.6 us -> 0.55 us
    all_gather x2 -> x0, waiting for transfers between devices: 147 us -> none  [prefix(): everything = jax.tree.map(lambda part: lax.all_gather(part, axis), value)]
    select_n x33 -> x6, other arithmetic: 106 us -> 3.82 us  [the longest x3 3.79 us: carried_states(): rest.append(swap(jnp.where(core == 0, second, pair), 1))]
    pallas_call x0 -> x4, Pallas kernels: none -> 42.9 us  [the longest x1 18.7 us: finish(): pl.pallas_call(functools.partial(finish_kernel, hd, cap, row_steps, out_s...]
    all_gather x2 -> x0, blocking collectives: 40.2 us -> none  [prefix(): everything = jax.tree.map(lambda part: lax.all_gather(part, axis), value)]
    ppermute x0 -> x24, starting transfers between devices: none -> 31.3 us  [the longest x15 15.9 us: swap(): return lax.ppermute(value, 'ctx', [(i, i ^ bit) for i in range(size)])]
    dot_general x4 -> x0, matrix products: 26 us -> none  [the longest x1 9.89 us: body(): jnp.einsum('thd,hde->the', query_heads.astype(jnp.float32), carried, prec...]
    reshape x2 -> x0, local copies, waits for them, and re-layouts: 20.1 us -> none  [the longest x1 13.3 us: body(): pair_rows = jnp.repeat(normed_rows, top_count, axis=0)]
    ppermute x0 -> x24, waiting for transfers between devices: none -> 17 us  [the longest x15 14 us: swap(): return lax.ppermute(value, 'ctx', [(i, i ^ bit) for i in range(size)])]
  transfers between devices with their start and end apart: 2 -> 24, of which waited for: 2 -> 6; matrix products, arithmetic and copies ran while one was open for 13% -> 3% of each run, Pallas kernels for 0% -> 8%
where the time goes in v1:
time: 311 us; the launch traced here: 310 us
  blocking collectives  188 us (60%)
  Pallas kernels  42.9 us (14%)
  starting transfers between devices  31.3 us (10%)
  local copies, waits for them, and re-layouts  20.3 us (7%)
  waiting for transfers between devices  17 us (5%)
  other arithmetic  9.91 us (3%)
    all_to_all x1, blocking collectives, body(): lax.all_to_all(outgoing, 'ctx', split_axis=0, concat_axis=0, tiled=True)  188 us
    unnamed x39, local copies, waits for them, and re-layouts  19.9 us
    pallas_call x1, Pallas kernels, finish(): pl.pallas_call(functools.partial(finish_kernel, hd, cap, row_steps, out_s...  18.7 us
    pallas_call x1, Pallas kernels, intra(): pl.pallas_call(functools.partial(intra_kernel, hd), grid=(steps,), in_spe...  15.9 us
    ppermute x15, starting transfers between devices, swap(): return lax.ppermute(value, 'ctx', [(i, i ^ bit) for i in range(size)])  15.9 us
    ppermute x9, starting transfers between devices, carried_states(): before = before + lax.ppermute(row_decay * before + row_total, 'ctx', pairs)  15.4 us
    ppermute x15, waiting for transfers between devices, swap(): return lax.ppermute(value, 'ctx', [(i, i ^ bit) for i in range(size)])  14 us
    pallas_call x2, Pallas kernels, block_states(): pl.pallas_call(functools.partial(state_kernel, first_slot, hd), grid_spec...  8.3 us
  transfers between devices with their start and end apart: 24, of which 6 were waited for; matrix products, arithmetic and copies ran while one was open for 3% of the time, Pallas kernels for 8%

profile of v1, /device:TPU:1, one launch (start us, length us, event | category | flops | bytes accessed | tf_op | source)
XLA Modules:
  0.0 309.8 jit_solution(16071246815393029930)
XLA Ops:
  0.0 0.9 reduce_sum.9
  0.9 2.7 collective-permute-start.2
  3.6 0.5 collective-permute-start
  4.1 0.9 copy.15.ld_ref
  5.0 1.9 copy-done
  6.9 1.9 copy-done.2
  8.8 4.5 %block_states.3 = (f32[2,4,128,128]{3,2,1,0:T(8,128)}, f32[2,4,128,128]{3,2,1,0:T(8,128)}, f32[2,4,128,128]{3,2,1,0:T(8,128)S(1)}) custom-call(s32[1]{0:T(128)} %bitcast.place, bf16[256,6144]{1,0:T(8,128)(2,1)S(1)} %copy-done, bf16[256,6144]{1,0:T(8,128)(2,1)S(1)} %copy-done.2, f32[256,48]{1,0:T(8,128)S(1)} %copy.15.ld_ref), custom_call_target="tpu_custom_call" | custom-call | flops 201326592 | bytes 4718592 | tf_op jit(solution)/shard_map/block_states/pallas_call | solution.py:63
  13.3 0.8 copy-done.16
  14.1 0.5 collective-permute-start.9
  14.6 0.1 exp.15
  14.7 1.9 copy-done.3
  16.5 3.8 %block_states.2 = (f32[2,4,128,128]{3,2,1,0:T(8,128)S(1)}, f32[2,4,128,128]{3,2,1,0:T(8,128)S(1)}, f32[2,4,128,128]{3,2,1,0:T(8,128)S(1)}) custom-call(s32[1]{0:T(128)} %bitcast.place, bf16[256,6144]{1,0:T(8,128)(2,1)S(1)} %copy-done.1, bf16[256,6144]{1,0:T(8,128)(2,1)S(1)} %copy-done.3, f32[256,48]{1,0:T(8,128)S(1)} %copy.15.ld_ref), custom_call_target="tpu_custom_call" | custom-call | flops 201326592 | bytes 4718592 | tf_op jit(solution)/shard_map/block_states/pallas_call | solution.py:63
  20.4 0.8 copy-done.7
  21.2 0.8 copy-done.9
  22.0 0.8 copy-done.11
  22.8 0.1 stack.45
  22.9 0.1 stack.46
  23.0 0.1 stack.47
  23.3 1.4 multiply_add_fusion.2
  24.7 1.6 collective-permute-start.4
  26.2 1.3 multiply_add_fusion
  27.6 0.1 collective-permute-start.16
  27.7 1.2 multiply_add_fusion.1
  28.9 1.5 collective-permute-start.10
  30.4 1.8 collective-permute-done.4
  32.1 0.1 broadcast_add_fusion.2
  32.3 3.7 %collective-permute-start.5 = (f32[4,128,128]{2,1,0:T(8,128)S(1)}, f32[4,128,128]{2,1,0:T(8,128)S(1)}, u32[]{:S(2)}, u32[]{:S(2)}) collective-permute-start(f32[4,128,128]{2,1,0:T(8,128)S(1)} %get-tuple-element.31), channel_id=1, source_target_pairs={{0,4},{1,5},{2,6},{3,7},{16,20},{17,21},{18,22},{19,23}} | collective-permute-start | bytes 786440 | tf_op jit(solution)/shard_map/ppermute | solution.py:262
  36.0 1.8 collective-permute-done.16
  37.8 0.1 broadcast_add_fusion
  37.9 3.7 %collective-permute-start.17 = (f32[4,128,128]{2,1,0:T(8,128)S(1)}, f32[4,128,128]{2,1,0:T(8,128)S(1)}, u32[]{:S(2)}, u32[]{:S(2)}) collective-permute-start(f32[4,128,128]{2,1,0:T(8,128)S(1)} %get-tuple-element.19), channel_id=1, source_target_pairs={{0,4},{1,5},{2,6},{3,7},{16,20},{17,21},{18,22},{19,23}} | collective-permute-start | bytes 786440 | tf_op jit(solution)/shard_map/ppermute | solution.py:262
  41.6 1.8 collective-permute-done.10
  43.4 0.1 broadcast_add_fusion.1
  43.5 3.7 %collective-permute-start.11 = (f32[4,128,128]{2,1,0:T(8,128)S(1)}, f32[4,128,128]{2,1,0:T(8,128)S(1)}, u32[]{:S(2)}, u32[]{:S(2)}) collective-permute-start(f32[4,128,128]{2,1,0:T(8,128)S(1)} %get-tuple-element.25), channel_id=1, source_target_pairs={{0,4},{1,5},{2,6},{3,7},{16,20},{17,21},{18,22},{19,23}} | collective-permute-start | bytes 786440 | tf_op jit(solution)/shard_map/ppermute | solution.py:262
  47.2 0.1 multiply_add_fusion.10
  47.3 0.7 collective-permute-start.6
  48.0 0.1 multiply_add_fusion.4
  48.1 0.7 collective-permute-start.18
  48.8 2.9 collective-permute-done.11
  51.7 0.1 multiply_add_fusion.7
  51.8 0.7 collective-permute-start.12
  52.5 0.1 multiply_add_fusion.9
  52.6 0.7 collective-permute-start.7
  53.3 0.1 multiply_add_fusion.3
  53.4 0.8 collective-permute-start.19
  54.2 0.1 multiply_add_fusion.6
  54.3 0.9 collective-permute-start.13
  55.2 0.1 select_bitcast_fusion.2
  55.3 1.7 collective-permute-start.8
  57.1 0.1 select_bitcast_fusion
  57.2 0.1 collective-permute-start.20
  57.3 0.1 select_bitcast_fusion.1
  57.5 1.5 collective-permute-start.14
  59.0 2.7 collective-permute-done.8
  61.6 1.4 fusion
  63.0 3.9 %collective-permute-start.21 = (f32[2,4,128,128]{3,2,1,0:T(8,128)S(1)}, f32[2,4,128,128]{3,2,1,0:T(8,128)S(1)}, u32[]{:S(2)}, u32[]{:S(2)}) collective-permute-start(f32[2,4,128,128]{3,2,1,0:T(8,128)S(1)} %get-tuple-element.39), channel_id=1, source_target_pairs={{0,1},{1,0},{2,3},{3,2},{4,5},{5,4},{6,7},{7,6},{8,9},{9,8},{10,11... | collective-permute-start | bytes 1572872 | tf_op jit(solution)/shard_map/ppermute | solution.py:231
  66.9 6.0 %collective-permute-done.14 = f32[4,128,128]{2,1,0:T(8,128)S(1)} collective-permute-done((f32[4,128,128]{2,1,0:T(8,128)S(1)}, f32[4,128,128]{2,1,0:T(8,128)S(1)}, u32[]{:S(2)}, u32[]{:S(2)}) %collective-permute-start.14) | collective-permute-done | bytes 262176 | tf_op jit(solution)/shard_map/ppermute | solution.py:231
  72.9 1.2 fusion.2
  74.1 1.7 collective-permute-start.22
  75.8 1.2 fusion.4
  77.2 15.9 %intra.1.in_ref = f32[256,6144]{1,0:T(8,128)S(1)} custom-call(bf16[256,6144]{1,0:T(8,128)(2,1)S(1)} %copy-done.6, bf16[256,6144]{1,0:T(8,128)(2,1)S(1)} %copy-done.1, bf16[256,6144]{1,0:T(8,128)(2,1)S(1)} %copy-done.4, f32[256,48]{1,0:T(8,128)S(1)} %copy.15.ld_ref), custom_call_target="tpu_custom_call" | custom-call | flops 1207959552 | bytes 15728640 | tf_op jit(solution)/shard_map/intra/pallas_call | solution.py:106
  93.1 2.7 copy-done.5
  95.8 18.7 %finish.1 = bf16[640,6144]{1,0:T(8,128)(2,1)} custom-call(s32[1]{0:T(128)} %bitcast.place, bf16[256,6144]{1,0:T(8,128)(2,1)} %q_ref.3, f32[256,6144]{1,0:T(8,128)} %copy-done.5, f32[256,48]{1,0:T(8,128)S(1)} %copy.15.ld_ref, bf16[256,6144]{1,0:T(8,128)(2,1)} %gate_ref.1, bf16[256,6144]{1,0:T(8,128)(2,1)} %res_ref.1, f32[1,6144]{1,0:T(1,128)S(1)} %bitcast.93, ...), custom_call_target="tpu_custom_call" | custom-call | flops 805306368 | bytes 31457280 | tf_op jit(solution)/shard_map/finish/pallas_call | solution.py:197
  114.5 187.9 %all_to_all.9 = bf16[16,40,6144]{2,1,0:T(8,128)(2,1)} all-to-all(bf16[16,40,6144]{2,1,0:T(8,128)(2,1)} %bitcast.97), channel_id=1, replica_groups=mesh['groups'=2,'ctx'=16] {'ctx'}, dimensions={0} | all-to-all | bytes 15728640 | tf_op jit(solution)/shard_map/all_to_all | solution.py:292
  302.4 7.4 %copy.26 = bf16[1,640,6144]{2,1,0:T(8,128)(2,1)} copy(bf16[1,640,6144]{2,1,0:T(8,128)(2,1)} %bitcast.96) | data formatting | bytes 15728640
  (63 shorter events, 0.4 us)
Async XLA Ops:
  0.9 22.1 %collective-permute-start.2 = (f32[48]{0:T(128)S(1)}, f32[48]{0:T(128)S(1)}, u32[]{:S(2)}, u32[]{:S(2)}) collective-permute-start(f32[48]{0:T(128)S(1)} %exp.14), channel_id=1, source_target_pairs={{0,3},{1,2},{2,1},{3,0},{4,7},{5,6},{6,5},{7,4},{8,11},{9,10},{10,... | collective-permute-start | bytes 584 | tf_op jit(solution)/shard_map/ppermute | solution.py:231
  3.6 19.3 %collective-permute-start.1 = (f32[48]{0:T(128)S(1)}, f32[48]{0:T(128)S(1)}, u32[]{:S(2)}, u32[]{:S(2)}) collective-permute-start(f32[48]{0:T(128)S(1)} %exp.14), channel_id=1, source_target_pairs={{0,2},{1,3},{2,0},{3,1},{4,6},{5,7},{6,4},{7,5},{8,10},{9,11},{10,... | collective-permute-start | bytes 584 | tf_op jit(solution)/shard_map/ppermute | solution.py:231
  3.6 19.2 %collective-permute-start = (f32[48]{0:T(128)S(1)}, f32[48]{0:T(128)S(1)}, u32[]{:S(2)}, u32[]{:S(2)}) collective-permute-start(f32[48]{0:T(128)S(1)} %exp.14), channel_id=1, source_target_pairs={{0,1},{1,0},{2,3},{3,2},{4,5},{5,4},{6,7},{7,6},{8,9},{9,8},{10,11... | collective-permute-start | bytes 584 | tf_op jit(solution)/shard_map/ppermute | solution.py:231
  5.0 1.9 copy-start
  6.9 1.9 copy-start.2
  8.8 5.9 %copy-start.1 = (bf16[256,6144]{1,0:T(8,128)(2,1)S(1)}, bf16[256,6144]{1,0:T(8,128)(2,1)}, u32[]{:S(2)}) copy-start(bf16[256,6144]{1,0:T(8,128)(2,1)} %k_ref.5) | copy-start | bytes 9437188
  13.3 0.8 copy-start.16
  14.0 9.2 %collective-permute-start.3 = (f32[2,4,128,128]{3,2,1,0:T(8,128)}, f32[2,4,128,128]{3,2,1,0:T(8,128)}, u32[]{:S(2)}, u32[]{:S(2)}) collective-permute-start(f32[2,4,128,128]{3,2,1,0:T(8,128)} %get-tuple-element.12), channel_id=1, source_target_pairs={{0,1},{1,0},{2,3},{3,2},{4,5},{5,4},{6,7},{7,6},{8,9},{9,8},{10,11... | collective-permute-start | bytes 1572872 | tf_op jit(solution)/shard_map/ppermute | solution.py:231
  14.1 13.6 %collective-permute-start.9 = (f32[2,4,128,128]{3,2,1,0:T(8,128)}, f32[2,4,128,128]{3,2,1,0:T(8,128)}, u32[]{:S(2)}, u32[]{:S(2)}) collective-permute-start(f32[2,4,128,128]{3,2,1,0:T(8,128)} %get-tuple-element.14), channel_id=1, source_target_pairs={{0,1},{1,0},{2,3},{3,2},{4,5},{5,4},{6,7},{7,6},{8,9},{9,8},{10,11... | collective-permute-start | bytes 1572872 | tf_op jit(solution)/shard_map/ppermute | solution.py:231
  14.6 1.9 copy-start.3
  20.4 0.8 copy-start.7
  21.2 0.8 copy-start.9
  22.0 0.8 copy-start.11
  22.8 3.5 %collective-permute-start.15 = (f32[2,4,128,128]{3,2,1,0:T(8,128)}, f32[2,4,128,128]{3,2,1,0:T(8,128)}, u32[]{:S(2)}, u32[]{:S(2)}) collective-permute-start(f32[2,4,128,128]{3,2,1,0:T(8,128)} %copy-done.16), channel_id=1, source_target_pairs={{0,1},{1,0},{2,3},{3,2},{4,5},{5,4},{6,7},{7,6},{8,9},{9,8},{10,11... | collective-permute-start | bytes 1572872 | tf_op jit(solution)/shard_map/ppermute | solution.py:231
  23.1 4.6 %copy-start.10 = (f32[2,4,128,128]{3,2,1,0:T(8,128)S(1)}, f32[2,4,128,128]{3,2,1,0:T(8,128)}, u32[]{:S(2)}) copy-start(f32[2,4,128,128]{3,2,1,0:T(8,128)} %copy-done.9) | copy-start | bytes 1572868
  24.7 7.5 %collective-permute-start.4 = (f32[4,128,128]{2,1,0:T(8,128)S(1)}, f32[4,128,128]{2,1,0:T(8,128)S(1)}, u32[]{:S(2)}, u32[]{:S(2)}) collective-permute-start(f32[4,128,128]{2,1,0:T(8,128)S(1)} %slice_bitcast_fusion.4), channel_id=1, source_target_pairs={{0,2},{1,3},{2,0},{3,1},{4,6},{5,7},{6,4},{7,5},{8,10},{9,11},{10,... | collective-permute-start | bytes 786440 | tf_op jit(solution)/shard_map/ppermute | solution.py:231
  27.6 10.2 %collective-permute-start.16 = (f32[4,128,128]{2,1,0:T(8,128)S(1)}, f32[4,128,128]{2,1,0:T(8,128)S(1)}, u32[]{:S(2)}, u32[]{:S(2)}) collective-permute-start(f32[4,128,128]{2,1,0:T(8,128)S(1)} %slice_bitcast_fusion), channel_id=1, source_target_pairs={{0,2},{1,3},{2,0},{3,1},{4,6},{5,7},{6,4},{7,5},{8,10},{9,11},{10,... | collective-permute-start | bytes 786440 | tf_op jit(solution)/shard_map/ppermute | solution.py:231
  28.9 14.5 %collective-permute-start.10 = (f32[4,128,128]{2,1,0:T(8,128)S(1)}, f32[4,128,128]{2,1,0:T(8,128)S(1)}, u32[]{:S(2)}, u32[]{:S(2)}) collective-permute-start(f32[4,128,128]{2,1,0:T(8,128)S(1)} %slice_bitcast_fusion.2), channel_id=1, source_target_pairs={{0,2},{1,3},{2,0},{3,1},{4,6},{5,7},{6,4},{7,5},{8,10},{9,11},{10,... | collective-permute-start | bytes 786440 | tf_op jit(solution)/shard_map/ppermute | solution.py:231
  32.3 14.9 %collective-permute-start.5 = (f32[4,128,128]{2,1,0:T(8,128)S(1)}, f32[4,128,128]{2,1,0:T(8,128)S(1)}, u32[]{:S(2)}, u32[]{:S(2)}) collective-permute-start(f32[4,128,128]{2,1,0:T(8,128)S(1)} %get-tuple-element.31), channel_id=1, source_target_pairs={{0,4},{1,5},{2,6},{3,7},{16,20},{17,21},{18,22},{19,23}} | collective-permute-start | bytes 786440 | tf_op jit(solution)/shard_map/ppermute | solution.py:262
  37.9 10.1 %collective-permute-start.17 = (f32[4,128,128]{2,1,0:T(8,128)S(1)}, f32[4,128,128]{2,1,0:T(8,128)S(1)}, u32[]{:S(2)}, u32[]{:S(2)}) collective-permute-start(f32[4,128,128]{2,1,0:T(8,128)S(1)} %get-tuple-element.19), channel_id=1, source_target_pairs={{0,4},{1,5},{2,6},{3,7},{16,20},{17,21},{18,22},{19,23}} | collective-permute-start | bytes 786440 | tf_op jit(solution)/shard_map/ppermute | solution.py:262
  43.5 8.2 %collective-permute-start.11 = (f32[4,128,128]{2,1,0:T(8,128)S(1)}, f32[4,128,128]{2,1,0:T(8,128)S(1)}, u32[]{:S(2)}, u32[]{:S(2)}) collective-permute-start(f32[4,128,128]{2,1,0:T(8,128)S(1)} %get-tuple-element.25), channel_id=1, source_target_pairs={{0,4},{1,5},{2,6},{3,7},{16,20},{17,21},{18,22},{19,23}} | collective-permute-start | bytes 786440 | tf_op jit(solution)/shard_map/ppermute | solution.py:262
  47.3 5.2 %collective-permute-start.6 = (f32[4,128,128]{2,1,0:T(8,128)S(1)}, f32[4,128,128]{2,1,0:T(8,128)S(1)}, u32[]{:S(2)}, u32[]{:S(2)}) collective-permute-start(f32[4,128,128]{2,1,0:T(8,128)S(1)} %multiply_add_fusion.10), channel_id=1, source_target_pairs={{4,8},{5,9},{6,10},{7,11},{20,24},{21,25},{22,26},{23,27}} | collective-permute-start | bytes 786440 | tf_op jit(solution)/shard_map/ppermute | solution.py:262
  48.1 5.2 %collective-permute-start.18 = (f32[4,128,128]{2,1,0:T(8,128)S(1)}, f32[4,128,128]{2,1,0:T(8,128)S(1)}, u32[]{:S(2)}, u32[]{:S(2)}) collective-permute-start(f32[4,128,128]{2,1,0:T(8,128)S(1)} %multiply_add_fusion.4), channel_id=1, source_target_pairs={{4,8},{5,9},{6,10},{7,11},{20,24},{21,25},{22,26},{23,27}} | collective-permute-start | bytes 786440 | tf_op jit(solution)/shard_map/ppermute | solution.py:262
  51.8 2.4 collective-permute-start.12
  52.6 2.6 collective-permute-start.7
  53.4 8.3 %copy-start.12 = (f32[2,4,128,128]{3,2,1,0:T(8,128)S(1)}, f32[2,4,128,128]{3,2,1,0:T(8,128)}, u32[]{:S(2)}) copy-start(f32[2,4,128,128]{3,2,1,0:T(8,128)} %copy-done.11) | copy-start | bytes 1572868
  53.4 3.7 %collective-permute-start.19 = (f32[4,128,128]{2,1,0:T(8,128)S(1)}, f32[4,128,128]{2,1,0:T(8,128)S(1)}, u32[]{:S(2)}, u32[]{:S(2)}) collective-permute-start(f32[4,128,128]{2,1,0:T(8,128)S(1)} %get-tuple-element.17), channel_id=1, source_target_pairs={{8,12},{9,13},{10,14},{11,15},{24,28},{25,29},{26,30},{27,31}} | collective-permute-start | bytes 786440 | tf_op jit(solution)/shard_map/ppermute | solution.py:262
  54.3 3.0 collective-permute-start.13
  55.3 6.3 %collective-permute-start.8 = (f32[4,128,128]{2,1,0:T(8,128)S(1)}, f32[4,128,128]{2,1,0:T(8,128)S(1)}, u32[]{:S(2)}, u32[]{:S(2)}) collective-permute-start(f32[4,128,128]{2,1,0:T(8,128)S(1)} %get-tuple-element.46), channel_id=1, source_target_pairs={{0,2},{1,3},{2,0},{3,1},{4,6},{5,7},{6,4},{7,5},{8,10},{9,11},{10,... | collective-permute-start | bytes 786440 | tf_op jit(solution)/shard_map/ppermute | solution.py:231
  57.2 18.6 %collective-permute-start.20 = (f32[4,128,128]{2,1,0:T(8,128)S(1)}, f32[4,128,128]{2,1,0:T(8,128)S(1)}, u32[]{:S(2)}, u32[]{:S(2)}) collective-permute-start(f32[4,128,128]{2,1,0:T(8,128)S(1)} %get-tuple-element.42), channel_id=1, source_target_pairs={{0,2},{1,3},{2,0},{3,1},{4,6},{5,7},{6,4},{7,5},{8,10},{9,11},{10,... | collective-permute-start | bytes 786440 | tf_op jit(solution)/shard_map/ppermute | solution.py:231
  57.3 18.5 %copy-start.8 = (f32[2,4,128,128]{3,2,1,0:T(8,128)S(1)}, f32[2,4,128,128]{3,2,1,0:T(8,128)}, u32[]{:S(2)}) copy-start(f32[2,4,128,128]{3,2,1,0:T(8,128)} %copy-done.7) | copy-start | bytes 1572868
  57.5 15.4 %collective-permute-start.14 = (f32[4,128,128]{2,1,0:T(8,128)S(1)}, f32[4,128,128]{2,1,0:T(8,128)S(1)}, u32[]{:S(2)}, u32[]{:S(2)}) collective-permute-start(f32[4,128,128]{2,1,0:T(8,128)S(1)} %get-tuple-element.44), channel_id=1, source_target_pairs={{0,2},{1,3},{2,0},{3,1},{4,6},{5,7},{6,4},{7,5},{8,10},{9,11},{10,... | collective-permute-start | bytes 786440 | tf_op jit(solution)/shard_map/ppermute | solution.py:231
  61.6 15.5 %copy-start.6 = (bf16[256,6144]{1,0:T(8,128)(2,1)S(1)}, bf16[256,6144]{1,0:T(8,128)(2,1)}, u32[]{:S(2)}) copy-start(bf16[256,6144]{1,0:T(8,128)(2,1)} %q_ref.3) | copy-start | bytes 9437188
  63.0 14.2 %copy-start.4 = (bf16[256,6144]{1,0:T(8,128)(2,1)S(1)}, bf16[256,6144]{1,0:T(8,128)(2,1)}, u32[]{:S(2)}) copy-start(bf16[256,6144]{1,0:T(8,128)(2,1)} %v_ref.5) | copy-start | bytes 9437188
  63.0 32.7 %collective-permute-start.21 = (f32[2,4,128,128]{3,2,1,0:T(8,128)S(1)}, f32[2,4,128,128]{3,2,1,0:T(8,128)S(1)}, u32[]{:S(2)}, u32[]{:S(2)}) collective-permute-start(f32[2,4,128,128]{3,2,1,0:T(8,128)S(1)} %get-tuple-element.39), channel_id=1, source_target_pairs={{0,1},{1,0},{2,3},{3,2},{4,5},{5,4},{6,7},{7,6},{8,9},{9,8},{10,11... | collective-permute-start | bytes 1572872 | tf_op jit(solution)/shard_map/ppermute | solution.py:231
  74.1 21.7 %collective-permute-start.22 = (f32[2,4,128,128]{3,2,1,0:T(8,128)S(1)}, f32[2,4,128,128]{3,2,1,0:T(8,128)S(1)}, u32[]{:S(2)}, u32[]{:S(2)}) collective-permute-start(f32[2,4,128,128]{3,2,1,0:T(8,128)S(1)} %get-tuple-element.37), channel_id=1, source_target_pairs={{0,1},{1,0},{2,3},{3,2},{4,5},{5,4},{6,7},{7,6},{8,9},{9,8},{10,11... | collective-permute-start | bytes 1572872 | tf_op jit(solution)/shard_map/ppermute | solution.py:231
  77.0 18.7 %copy-start.13 = (f32[6144]{0:T(1024)S(1)}, f32[6144]{0:T(1024)}, u32[]{:S(2)}) copy-start(f32[6144]{0:T(1024)} %param.15) | copy-start | bytes 73732
  77.1 18.7 %copy-start.14 = (f32[6144]{0:T(1024)S(1)}, f32[6144]{0:T(1024)}, u32[]{:S(2)}) copy-start(f32[6144]{0:T(1024)} %param.16) | copy-start | bytes 73732
  77.1 18.7 %copy-start.15 = (s32[256,2]{0,1:T(2,128)S(1)}, s32[256,2]{0,1:T(2,128)}, u32[]{:S(2)}) copy-start(s32[256,2]{0,1:T(2,128)} %param.17) | copy-start | bytes 6148
  77.1 18.7 %collective-permute-start.23 = (f32[2,4,128,128]{3,2,1,0:T(8,128)S(1)}, f32[2,4,128,128]{3,2,1,0:T(8,128)S(1)}, u32[]{:S(2)}, u32[]{:S(2)}) collective-permute-start(f32[2,4,128,128]{3,2,1,0:T(8,128)S(1)} %get-tuple-element.35), channel_id=1, source_target_pairs={{0,1},{1,0},{2,3},{3,2},{4,5},{5,4},{6,7},{7,6},{8,9},{9,8},{10,11... | collective-permute-start | bytes 1572872 | tf_op jit(solution)/shard_map/ppermute | solution.py:231
  93.1 2.7 copy-start.5

commit v2 on v0

v2 whole, which is shorter than its diff:
```python
import functools
import jax
import jax.numpy as jnp
from jax import lax
from jax.experimental import pallas as pl
from jax.experimental.pallas import tpu as pltpu
from jax.sharding import PartitionSpec as P

EXP_DEV = 1
SLOTS = 4
CHUNKS = 2
WIRE = jnp.float32
LANES = 128
TAIL = 8
F32 = jnp.float32
BF16 = jnp.bfloat16
ANY = pl.BlockSpec(memory_space=pl.ANY)
VMEM = pl.BlockSpec(memory_space=pltpu.VMEM)
SMEM = pl.BlockSpec(memory_space=pltpu.SMEM)
BRIEF = pl.CostEstimate(flops=1, bytes_accessed=1, transcendentals=0)


def dot(a, b, contract=(1, 0)):
    return lax.dot_general(a, b, ((contract[:1], contract[1:]), ((), ())), preferred_element_type=F32)


def running(ld_ref, group, count):
    ld = ld_ref[:count, :]
    for g in range(1, ld_ref.shape[0] // count):
        ld = jnp.where(group == g, ld_ref[g * count : (g + 1) * count, :], ld)
    tok = ld.shape[1]
    row = lax.broadcasted_iota(jnp.int32, (tok, tok), 0)
    col = lax.broadcasted_iota(jnp.int32, (tok, tok), 1)
    upper = (row <= col).astype(F32).astype(BF16)
    high = ld.astype(BF16)
    rest = ld - high.astype(F32)
    mid = rest.astype(BF16)
    low = (rest - mid.astype(F32)).astype(BF16)
    return dot(high, upper) + (dot(mid, upper) + dot(low, upper))


def state_kernel(first_slot, hd, place, k_hbm, v_hbm, ld_ref, dep, *rest):
    outs = rest[:CHUNKS]
    k_ref, v_ref, sems = rest[CHUNKS:]
    gw = k_ref.shape[2]
    gh = gw // hd
    per = gh // CHUNKS
    copies = []
    for j in range(2):
        at = pl.ds(pl.multiple_of(jnp.bitwise_xor(j + first_slot, place[0]) * gw, gw), gw)
        copies.append(
            [
                pltpu.make_async_copy(k_hbm.at[:, at], k_ref.at[j], sems.at[2 * j]),
                pltpu.make_async_copy(v_hbm.at[:, at], v_ref.at[j], sems.at[2 * j + 1]),
            ]
        )
        for c in copies[j]:
            c.start()
    for j in range(2):
        cum = running(ld_ref, jnp.bitwise_xor(j + first_slot, place[0]), gh)
        total = cum[:, -1:]
        weight = jnp.exp(total - cum)
        decay = jnp.exp(total)
        for c in copies[j]:
            c.wait()
        for i in range(gh):
            cols = slice(i * hd, (i + 1) * hd)
            wk = (weight[i : i + 1, :] * k_ref[j, :, cols].T.astype(F32)).astype(BF16)
            out = outs[i // per]
            out[j, i % per, :hd, :] = dot(wk, v_ref[j, :, cols])
            out[j, i % per, hd:, :] = jnp.broadcast_to(decay[i : i + 1, :], (TAIL, hd))


def block_states(place, key_rows, value_rows, log_decay, dep, first_slot, hd):
    tok, width = key_rows.shape
    gw = width // SLOTS
    per = gw // hd // CHUNKS
    shape = (2, per, hd + TAIL, hd)
    hbm = pl.BlockSpec(memory_space=pltpu.HBM)
    vmem = pl.BlockSpec(memory_space=pltpu.VMEM)
    return pl.pallas_call(
        functools.partial(state_kernel, first_slot, hd),
        in_specs=[pl.BlockSpec(memory_space=pltpu.SMEM), hbm, hbm, vmem, ANY],
        out_specs=[vmem] * CHUNKS,
        scratch_shapes=[
            pltpu.VMEM((2, tok, gw), BF16),
            pltpu.VMEM((2, tok, gw), BF16),
            pltpu.SemaphoreType.DMA((4,)),
        ],
        out_shape=[jax.ShapeDtypeStruct(shape, F32)] * CHUNKS,
        compiler_params=pltpu.CompilerParams(vmem_limit_bytes=60 << 20),
        cost_estimate=BRIEF,
        name="block_states",
    )(place, key_rows, value_rows, log_decay, dep)


def intra_kernel(hd, slot, place, q_ref, k_ref, v_ref, ld_ref, dep, *outs):
    tok = q_ref.shape[0]
    gh = q_ref.shape[1] // hd
    half = tok // 2
    cum_rows = running(ld_ref, jnp.bitwise_xor(slot, place[0]), gh)
    cum = cum_rows.T
    row = lax.broadcasted_iota(jnp.int32, (half, half), 0)
    col = lax.broadcasted_iota(jnp.int32, (half, half), 1)
    causal = row >= col
    per = gh // len(outs)
    for i in range(gh):
        cols = slice(i * hd, (i + 1) * hd)
        o_ref, to = outs[i // per], slice(i % per * hd, (i % per + 1) * hd)
        down, across = cum[:, i : i + 1], cum_rows[i : i + 1, :]
        parts = []
        for first in (0, half):
            at = slice(first, first + half)
            score = dot(q_ref[at, cols], k_ref[at, cols], (1, 1))
            weights = jnp.where(causal, score * jnp.exp(down[at] - across[:, at]), 0.0).astype(BF16)
            parts.append(dot(weights, v_ref[at, cols]))
        o_ref[:half, to] = parts[0]
        middle = across[:, half - 1 : half]
        score = dot(q_ref[half:, cols], k_ref[:half, cols], (1, 1))
        weights = (score * (jnp.exp(down[half:] - middle) * jnp.exp(middle - across[:, :half]))).astype(BF16)
        o_ref[half:, to] = parts[1] + dot(weights, v_ref[:half, cols])


def intra(place, query, key_rows, value_rows, log_decay, dep, slot, hd):
    tok, width = query.shape
    gw = width // SLOTS
    block = pl.BlockSpec((tok, gw), lambda i, s: (0, jnp.bitwise_xor(slot, s[0])))
    return pl.pallas_call(
        functools.partial(intra_kernel, hd, slot),
        grid_spec=pltpu.PrefetchScalarGridSpec(
            num_scalar_prefetch=1,
            grid=(1,),
            in_specs=[block, block, block, pl.BlockSpec(log_decay.shape, lambda i, s: (0, 0)), ANY],
            out_specs=[pl.BlockSpec((tok, gw // CHUNKS), lambda i, s: (0, 0))] * CHUNKS,
        ),
        out_shape=[jax.ShapeDtypeStruct((tok, gw // CHUNKS), F32)] * CHUNKS,
        compiler_params=pltpu.CompilerParams(vmem_limit_bytes=16 << 20),
        cost_estimate=BRIEF,
        name="intra",
    )(place, query, key_rows, value_rows, log_decay, dep)


def add_branch(hd, place, slot, first, q_ref, in_ref, ld_ref, gate, gain, states, put):
    own, there = states
    per = own.shape[1]
    grow = jnp.exp(running(ld_ref, jnp.bitwise_xor(slot, place[0]), per * CHUNKS)[first : first + per]).T
    squares = 0.0
    for i in range(per):
        cols = slice(i * hd, (i + 1) * hd)
        carried = (own if slot < 2 else there)[slot % 2, i]
        high = carried.astype(BF16)
        low = (carried - high.astype(F32)).astype(BF16)
        q = q_ref[:, cols]
        att = in_ref[:, cols] + grow[:, i : i + 1] * (dot(q, high) + dot(q, low))
        squares = squares + att * att
        put(cols, att * gain[:, cols] * jax.nn.sigmoid(gate[:, cols].astype(F32)))
    return squares


def branch_kernel(hd, chunk, per, place, q_ref, gate_ref, ag_ref, ld_ref, own, there, dep, *rest):
    ins = rest[:SLOTS]
    o_ref, sq_ref = rest[SLOTS:]
    step = pl.program_id(0)
    for slot in range(SLOTS):

        @pl.when(step == slot)
        def _():
            def put(cols, value):
                o_ref[:, cols] = value

            squares = add_branch(
                hd, place, slot, chunk * per, q_ref, ins[slot], ld_ref, gate_ref, ag_ref, (own, there), put
            )
            sq_ref[...] = squares if slot == 0 else sq_ref[...] + squares


def chunk_block(rows, per, hd, chunk, last):
    return pl.BlockSpec(
        (rows, per * hd),
        lambda i, s: (0, jnp.bitwise_xor(jnp.minimum(i, last), s[0]) * CHUNKS + chunk),
    )


def branch(place, query, gate, attn_gain, log_decay, states, intra_outs, dep, chunk, hd):
    tok, width = query.shape
    per = states[0].shape[1]
    col = lambda rows: chunk_block(rows, per, hd, chunk, SLOTS - 1)
    whole = lambda a: pl.BlockSpec(a.shape, lambda i, s: (0,) * a.ndim)
    part = pl.BlockSpec((tok, per * hd), lambda i, s: (0, 0))
    return pl.pallas_call(
        functools.partial(branch_kernel, hd, chunk, per),
        grid_spec=pltpu.PrefetchScalarGridSpec(
            num_scalar_prefetch=1,
            grid=(SLOTS,),
            in_specs=[col(tok), col(tok), col(1), whole(log_decay), whole(states[0]), whole(states[1]), ANY]
            + [part] * SLOTS,
            out_specs=[
                pl.BlockSpec((tok, per * hd), lambda i, s: (0, i)),
                pl.BlockSpec((tok, hd), lambda i, s: (0, 0)),
            ],
        ),
        out_shape=[
            jax.ShapeDtypeStruct((tok, SLOTS * per * hd), F32),
            jax.ShapeDtypeStruct((tok, hd), F32),
        ],
        compiler_params=pltpu.CompilerParams(vmem_limit_bytes=24 << 20),
        cost_estimate=BRIEF,
        name="branch",
    )(place, query, gate, attn_gain, log_decay, *states, dep, *intra_outs)


def finish_kernel(hd, cap, per, row_steps, place, q_ref, gate_ref, ag_ref, ld_ref, own, there, dep, *rest):
    ins, rest = rest[:SLOTS], rest[SLOTS:]
    early, rest = rest[: CHUNKS - 1], rest[CHUNKS - 1 :]
    squares, rest = rest[: CHUNKS - 1], rest[CHUNKS - 1 :]
    res_ref, mg_ref, ids_ref, o_ref, late, sq, hidden, normed, target = rest
    tok, width = normed.shape
    step = pl.program_id(0)
    cw = per * hd

    for slot in range(SLOTS):

        @pl.when(step == slot)
        def _():
            def put(cols, value):
                late[:, slot * cw + cols.start : slot * cw + cols.stop] = value

            part = add_branch(
                hd, place, slot, (CHUNKS - 1) * per, q_ref, ins[slot], ld_ref, gate_ref, ag_ref, (own, there), put
            )
            if slot == 0:
                for s in squares:
                    part = part + s[...]
                sq[...] = part
            else:
                sq[...] += part

    rows = tok // row_steps

    @pl.when((step >= SLOTS) & (step < SLOTS + row_steps))
    def _():
        at = pl.ds(pl.multiple_of((step - SLOTS) * rows, rows), rows)
        scale = lax.rsqrt(jnp.sum(sq[at, :], axis=-1, keepdims=True) / width + 1e-06)
        total = jnp.zeros((rows, LANES), F32)
        for slot in range(SLOTS):
            group = jnp.bitwise_xor(slot, place[0])
            for k in range(CHUNKS):
                for n in range(cw // LANES):
                    here = slice(slot * cw + n * LANES, slot * cw + (n + 1) * LANES)
                    where = pl.ds(pl.multiple_of((group * CHUNKS + k) * cw + n * LANES, LANES), LANES)
                    value = early[k][:, here] if k < CHUNKS - 1 else late[at, here]
                    value = res_ref[:, where].astype(F32) + value * scale
                    total = total + value * value
                    hidden[:, where] = value
        scale = lax.rsqrt(jnp.sum(total, axis=-1, keepdims=True) / width + 1e-06)
        for n in range(width // LANES):
            cols = slice(n * LANES, (n + 1) * LANES)
            normed[at, cols] = (hidden[:, cols] * scale * mg_ref[:, cols]).astype(BF16)

    @pl.when(step == 0)
    def _():
        top = ids_ref.shape[0]
        experts = target.shape[0] - 8
        ids = ids_ref[...]
        expert = lax.broadcasted_iota(jnp.int32, (experts, tok), 0)
        hot = [(ids[k : k + 1, :] == expert).astype(F32) for k in range(top)]
        row = lax.broadcasted_iota(jnp.int32, (tok, tok), 0)
        col = lax.broadcasted_iota(jnp.int32, (tok, tok), 1)
        count = dot(sum(hot).astype(BF16), (row < col).astype(F32).astype(BF16))
        for k in range(top):
            slot = jnp.sum(hot[k] * count, axis=0, keepdims=True).astype(jnp.int32)
            target[k : k + 1, :] = ids[k : k + 1, :] * cap + slot
            count = count + hot[k]

    @pl.when(step >= SLOTS + row_steps)
    def _():
        out_rows = o_ref.shape[0]
        base = (step - SLOTS - row_steps) * out_rows
        row = lax.broadcasted_iota(jnp.int32, (out_rows, tok), 0) + base
        hit = row == target[0:1, :]
        for k in range(1, ids_ref.shape[0]):
            hit = hit | (row == target[k : k + 1, :])
        pick = hit.astype(F32).astype(BF16)
        part = width // 4
        for n in range(4):
            cols = slice(n * part, (n + 1) * part)
            o_ref[:, cols] = dot(pick, normed[:, cols]).astype(BF16)


def finish(
    place, query, gate, attn_gain, log_decay, states, intra_outs, early, squares, residual, moe_gain, ids, dep, cap, experts, hd
):
    tok, width = query.shape
    per = states[0].shape[1]
    cw = per * hd
    row_steps, out_steps = 4, 4
    out_rows = experts * cap // out_steps
    rows = tok // row_steps
    chunk = CHUNKS - 1
    col = lambda r: chunk_block(r, per, hd, chunk, SLOTS - 1)
    whole = lambda a: pl.BlockSpec(a.shape, lambda i, s: (0,) * a.ndim)
    part = pl.BlockSpec((tok, cw), lambda i, s: (0, 0))
    by_row = lambda w: pl.BlockSpec((rows, w), lambda i, s: (jnp.clip(i - SLOTS, 0, row_steps - 1), 0))
    return pl.pallas_call(
        functools.partial(finish_kernel, hd, cap, per, row_steps),
        grid_spec=pltpu.PrefetchScalarGridSpec(
            num_scalar_prefetch=1,
            grid=(SLOTS + row_steps + out_steps,),
            in_specs=[col(tok), col(tok), col(1), whole(log_decay), whole(states[0]), whole(states[1]), ANY]
            + [part] * SLOTS
            + [by_row(SLOTS * cw)] * len(early)
            + [whole(squares[0])] * len(squares)
            + [by_row(width), whole(moe_gain), whole(ids)],
            out_specs=pl.BlockSpec((out_rows, width), lambda i, s: (jnp.maximum(i - SLOTS - row_steps, 0), 0)),
            scratch_shapes=[
                pltpu.VMEM((tok, SLOTS * cw), F32),
                pltpu.VMEM((tok, hd), F32),
                pltpu.VMEM((rows, width), F32),
                pltpu.VMEM((tok, width), BF16),
                pltpu.VMEM((experts + 8, tok), jnp.int32),
            ],
        ),
        out_shape=jax.ShapeDtypeStruct((experts * cap, width), BF16),
        compiler_params=pltpu.CompilerParams(vmem_limit_bytes=32 << 20),
        cost_estimate=BRIEF,
        name="finish",
    )(place, query, gate, attn_gain, log_decay, *states, dep, *intra_outs, *early, *squares, residual, moe_gain, ids)


def land_kernel(i_ref, o_ref):
    o_ref[0] = i_ref[...]


def land(arrived):
    rows, width = arrived.shape
    steps = 8
    return pl.pallas_call(
        land_kernel,
        grid=(steps,),
        in_specs=[pl.BlockSpec((rows // steps, width), lambda i: (i, 0))],
        out_specs=pl.BlockSpec((1, rows // steps, width), lambda i: (0, i, 0)),
        out_shape=jax.ShapeDtypeStruct((1, rows, width), arrived.dtype),
        cost_estimate=BRIEF,
        compiler_params=pltpu.CompilerParams(vmem_limit_bytes=16 << 20),
        name="land",
    )(arrived)


def swap(value, bit):
    size = lax.axis_size("ctx")
    return lax.ppermute(value, "ctx", [(i, i ^ bit) for i in range(size)])


def small(kernel, name, flags, ins, dep, outs):
    return pl.pallas_call(
        kernel,
        in_specs=[SMEM] + [VMEM] * len(ins) + [ANY],
        out_specs=[VMEM] * len(outs),
        out_shape=[jax.ShapeDtypeStruct(shape, kind) for shape, kind in outs],
        compiler_params=pltpu.CompilerParams(vmem_limit_bytes=16 << 20),
        cost_estimate=BRIEF,
        name=name,
    )(flags, *ins, dep)


def later(before, decay, state):
    return decay * before + state


def decay_rows(decay, rows):
    high = decay.astype(BF16).astype(F32)
    mid = (decay - high).astype(BF16).astype(F32)
    low = decay - high - mid
    row = lax.broadcasted_iota(jnp.int32, (decay.shape[0], rows, decay.shape[2]), 1)
    return jnp.where(row == 0, high, jnp.where(row == 1, mid, jnp.where(row == 2, low, 0.0)))


def chip_kernel(flags, keep, received, dep, mine, sent):
    hd = keep.shape[-1]
    low = flags[1] == 0
    for slot in range(2):
        a = jnp.where(low, keep[slot], received[slot])
        b = jnp.where(low, received[slot], keep[slot])
        state = later(a[:, :hd, :], b[:, hd : hd + 1, :], b[:, :hd, :])
        decay = a[:, hd:, :] * b[:, hd:, :]
        if slot == 0:
            mine[:, :hd, :] = state
            mine[:, hd:, :] = decay
        else:
            sent[:, :hd, :] = state.astype(WIRE)
            sent[:, hd:, :] = decay_rows(decay[:, :1, :], 2 * TAIL).astype(WIRE)


def row_parts(flags, mine, other):
    hd = mine.shape[-1]
    low = flags[2] == 0
    a = (mine[:, :hd, :], mine[:, hd : hd + 1, :])
    b = (other[:, :hd, :].astype(F32), jnp.sum(other[:, hd:, :].astype(F32), axis=1, keepdims=True))
    first = tuple(jnp.where(low, x, y) for x, y in zip(a, b))
    second = tuple(jnp.where(low, y, x) for x, y in zip(a, b))
    return first, second


def row_kernel(flags, mine, other, dep, total, sent):
    hd = mine.shape[-1]
    first, second = row_parts(flags, mine, other)
    state = later(first[0], second[1], second[0])
    total[:, :hd, :] = state
    total[:, hd:, :] = jnp.broadcast_to(first[1] * second[1], (total.shape[0], TAIL, hd))
    sent[...] = state.astype(sent.dtype)


def arrived_sum(refs):
    return sum(r[...].astype(F32) for r in refs)


def hop_kernel(flags, total, *rest):
    hops, sent = rest[:-2], rest[-1]
    hd = total.shape[-1]
    sent[...] = later(arrived_sum(hops), total[:, hd : hd + 1, :], total[:, :hd, :]).astype(sent.dtype)


def side_kernel(flags, mine, other, *rest):
    hops, (_, here, sent) = rest[:-3], rest[-3:]
    low = flags[2] == 0
    first, _ = row_parts(flags, mine, other)
    before = arrived_sum(hops)
    entered = later(before, first[1], first[0])
    here[...] = jnp.where(low, before, entered)
    sent[...] = jnp.where(low, entered, before).astype(sent.dtype)


def core_kernel(flags, keep, received, here, there, dep, own, sent):
    hd = keep.shape[-1]
    low = flags[1] == 0
    for slot, ref in ((0, here), (1, there)):
        pair = ref[...].astype(F32)
        first = jnp.where(low, keep[slot], received[slot])
        second = later(pair, first[:, hd : hd + 1, :], first[:, :hd, :])
        own[slot] = jnp.where(low, pair, second)
        sent[slot] = jnp.where(low, second, pair)


def body(
    query, key_rows, value_rows, log_decay, gate_input, residual, attn_gain, moe_gain, expert_ids
):
    tok_rows, model_width = query.shape
    heads = log_decay.shape[1]
    hd = model_width // heads
    per = heads // SLOTS // CHUNKS
    size = lax.axis_size("ctx")
    hops = size // SLOTS - 1
    index = lax.axis_index("ctx").astype(jnp.int32)
    core, side = jnp.bitwise_and(index, 1), jnp.bitwise_and(lax.shift_right_logical(index, 1), 1)
    place = (2 * core + side)[None]
    flags = jnp.stack([2 * core + side, core, side])
    ld = log_decay.T
    ag, mg = attn_gain[None], moe_gain[None]
    full, wire, plain = (per, hd + TAIL, hd), (per, hd + 2 * TAIL, hd), (per, hd, hd)

    send = block_states(place, key_rows, value_rows, ld, ld, 2, hd)
    received = [swap(s, 1) for s in send]
    keep = block_states(place, key_rows, value_rows, ld, send[0], 0, hd)
    dep = keep[0]
    mine, other = [], []
    for k in range(CHUNKS):
        m, t = small(chip_kernel, "chip", flags, [keep[k], received[k]], dep, [(full, F32), (wire, WIRE)])
        dep = m
        mine.append(m)
        other.append(swap(t, 2))

    intra_outs = []
    totals, arrived = [None] * CHUNKS, [[] for _ in range(CHUNKS)]
    here, there, states = [None] * CHUNKS, [None] * CHUNKS, [None] * CHUNKS
    early, squares = [], []

    def more_intra(dep):
        if len(intra_outs) < SLOTS:
            intra_outs.append(intra(place, query, key_rows, value_rows, ld, dep, len(intra_outs), hd))
            dep = intra_outs[-1][0]
        return dep

    def hop(k, sent):
        s = len(arrived[k])
        pairs = [(s * SLOTS + j, (s + 1) * SLOTS + j) for j in range(SLOTS)]
        arrived[k].append(lax.ppermute(sent, "ctx", pairs))

    dep = more_intra(dep)
    for wave in range(hops + CHUNKS + 2):
        ready = [(k, wave - k) for k in range(CHUNKS) if 0 <= wave - k <= hops + 2]
        for k, stage in sorted(ready, key=lambda r: (r[1] == hops + 2, r[0])):
            if stage == 0:
                totals[k], dep = small(
                    row_kernel, "row", flags, [mine[k], other[k]], dep, [(full, F32), (plain, BF16)]
                )
                hop(k, dep)
            elif stage < hops:
                (dep,) = small(hop_kernel, "hop", flags, [totals[k]] + arrived[k], dep, [(plain, BF16)])
                hop(k, dep)
            elif stage == hops:
                here[k], dep = small(
                    side_kernel, "side", flags, [mine[k], other[k]] + arrived[k], dep, [(plain, F32), (plain, BF16)]
                )
                there[k] = swap(dep, 2)
            elif stage == hops + 1:
                own, dep = small(
                    core_kernel, "core", flags, [keep[k], received[k], here[k], there[k]], dep, [((2,) + plain, F32)] * 2
                )
                states[k] = (own, swap(dep, 1))
            elif k < CHUNKS - 1:
                dep, sq = branch(place, query, gate_input, ag, ld, states[k], [o[k] for o in intra_outs], dep, k, hd)
                early.append(dep)
                squares.append(sq)
        dep = more_intra(dep)

    expert_count = EXP_DEV * size
    capacity = 5 * tok_rows * expert_ids.shape[1] // (4 * expert_count)
    outgoing = finish(
        place, query, gate_input, ag, ld, states[-1], [o[-1] for o in intra_outs], early, squares,
        residual, mg, expert_ids.T, dep, capacity, expert_count, hd,
    )
    return land(lax.all_to_all(outgoing, "ctx", split_axis=0, concat_axis=0, tiled=True))


def solution(mesh):
    rows = P(("groups", "ctx"), None)
    in_specs = (rows, rows, rows, rows, rows, rows, P(), P(), rows)
    out_specs = P(("groups", "ctx"), None, None)
    return jax.shard_map(body, mesh=mesh, in_specs=in_specs, out_specs=out_specs, check_vma=False)
```

time: 591 us -> 263 us (0.45)
  waiting for transfers between devices: 147 us -> 6.7 us
  other arithmetic: 115 us -> 0.08 us
  local copies, waits for them, and re-layouts: 71.9 us -> 4.39 us
  Pallas kernels: 0 us -> 50.2 us
  blocking collectives: 216 us -> 177 us
  matrix products: 26 us -> 0 us
  starting transfers between devices: 0.04 us -> 23.5 us
  between operations: 13.6 us -> 0.33 us
    all_gather x2 -> x0, waiting for transfers between devices: 147 us -> none  [prefix(): everything = jax.tree.map(lambda part: lax.all_gather(part, axis), value)]
    select_n x33 -> x0, other arithmetic: 106 us -> none  [the longest x32 106 us: step(): return jax.tree.map(lambda a, b: jnp.where(reached, a, b), new, before)]
    pallas_call x0 -> x21, Pallas kernels: none -> 50.2 us  [the longest x4 12 us: intra(): pl.pallas_call(functools.partial(intra_kernel, hd, slot), grid_spec=pltpu...]
    all_gather x2 -> x0, blocking collectives: 40.2 us -> none  [prefix(): everything = jax.tree.map(lambda part: lax.all_gather(part, axis), value)]
    dot_general x4 -> x0, matrix products: 26 us -> none  [the longest x1 9.89 us: body(): jnp.einsum('thd,hde->the', query_heads.astype(jnp.float32), carried, prec...]
    ppermute x0 -> x14, starting transfers between devices: none -> 23.5 us  [the longest x8 14.4 us: swap(): return lax.ppermute(value, 'ctx', [(i, i ^ bit) for i in range(size)])]
    reshape x2 -> x0, local copies, waits for them, and re-layouts: 20.1 us -> none  [the longest x1 13.3 us: body(): pair_rows = jnp.repeat(normed_rows, top_count, axis=0)]
    unnamed x18 -> x28, local copies, waits for them, and re-layouts: 20.7 us -> 4.39 us
  transfers between devices with their start and end apart: 2 -> 14, of which waited for: 2 -> 3; matrix products, arithmetic and copies ran while one was open for 13% -> 0% of each run, Pallas kernels for 0% -> 11%
where the time goes in v2:
time: 263 us
  blocking collectives  177 us (67%)
  Pallas kernels  50.2 us (19%)
  starting transfers between devices  23.5 us (9%)
  waiting for transfers between devices  6.7 us (3%)
  local copies, waits for them, and re-layouts  4.39 us (2%)
    all_to_all x1, blocking collectives, body(): lax.all_to_all(outgoing, 'ctx', split_axis=0, concat_axis=0, tiled=True)  177 us
    ppermute x8, starting transfers between devices, swap(): return lax.ppermute(value, 'ctx', [(i, i ^ bit) for i in range(size)])  14.4 us
    pallas_call x4, Pallas kernels, intra(): pl.pallas_call(functools.partial(intra_kernel, hd, slot), grid_spec=pltpu...  12 us
    pallas_call x1, Pallas kernels, finish(): pl.pallas_call(functools.partial(finish_kernel, hd, cap, per, row_steps),...  11.8 us
    pallas_call x12, Pallas kernels, small(): pl.pallas_call(kernel, in_specs=[SMEM] + [VMEM] * len(ins) + [ANY], out_s...  9.44 us
    ppermute x6, starting transfers between devices, hop(): arrived[k].append(lax.ppermute(sent, 'ctx', pairs))  9.11 us
    pallas_call x2, Pallas kernels, block_states(): pl.pallas_call(functools.partial(state_kernel, first_slot, hd), in_specs=...  8.83 us
    ppermute x8, waiting for transfers between devices, swap(): return lax.ppermute(value, 'ctx', [(i, i ^ bit) for i in range(size)])  6.68 us
  transfers between devices with their start and end apart: 14, of which 3 were waited for; matrix products, arithmetic and copies ran while one was open for 0% of the time, Pallas kernels for 11%

profile of v2, /device:TPU:1, one launch (start us, length us, event | category | flops | bytes accessed | tf_op | source)
XLA Modules:
  0.0 262.5 jit_solution(5973025595689453229)
XLA Ops:
  0.0 4.3 %block_states.2 = (f32[2,6,136,128]{3,2,1,0:T(8,128)}, f32[2,6,136,128]{3,2,1,0:T(8,128)}) custom-call(s32[1]{0:T(128)} %bitcast.place, bf16[256,6144]{1,0:T(8,128)(2,1)} %k_ref.7, bf16[256,6144]{1,0:T(8,128)(2,1)} %v_ref.7, f32[48,256]{1,0:T(8,128)} %bitcast.10, f32[48,256]{1,0:T(8,128)} %bitcast.11), custom_call_target="tpu_custom_call" | custom-call | flops 1 | bytes 1 | tf_op jit(solution)/shard_map/block_states/pallas_call | solution.py:81
  4.3 0.1 collective-permute-start.1
  4.5 0.5 collective-permute-start
  4.9 4.5 %block_states.3 = (f32[2,6,136,128]{3,2,1,0:T(8,128)}, f32[2,6,136,128]{3,2,1,0:T(8,128)}) custom-call(s32[1]{0:T(128)} %bitcast.place, bf16[256,6144]{1,0:T(8,128)(2,1)} %k_ref.7, bf16[256,6144]{1,0:T(8,128)(2,1)} %v_ref.7, f32[48,256]{1,0:T(8,128)} %bitcast.12, f32[2,6,136,128]{3,2,1,0:T(8,128)} %get-tuple-element.35.dep), custom_call_target="tpu_custom_call" | custom-call | flops 1 | bytes 1 | tf_op jit(solution)/shard_map/block_states/pallas_call | solution.py:81
  9.4 0.0 copy-start
  9.4 0.1 pad_add_fusion.flags
  9.5 0.0 collective-permute-done.1.received
  9.5 1.3 copy-done.5
  10.8 1.3 chip.2
  12.1 2.4 collective-permute-start.3
  14.5 0.0 collective-permute-done.received
  14.5 1.1 copy-done.8
  15.6 0.7 chip.3
  16.3 0.1 collective-permute-start.2
  16.4 0.0 copy-done.1
  16.4 0.0 copy-done.7
  16.4 0.0 copy-done
  16.4 0.0 copy-start.2
  16.4 1.9 copy-done.2
  18.3 3.0 %intra.4 = (f32[256,768]{1,0:T(8,128)S(1)}, f32[256,768]{1,0:T(8,128)S(1)}) custom-call(s32[1]{0:T(128)} %bitcast.place, bf16[256,6144]{1,0:T(8,128)(2,1)S(1)} %copy-done.2, bf16[256,6144]{1,0:T(8,128)(2,1)S(1)} %copy-done, bf16[256,6144]{1,0:T(8,128)(2,1)S(1)} %copy-done.1, f32[48,256]{1,0:T(8,128)S(1)} %bitcast.13, ...), custom_call_target="tpu_custom_call" | custom-call | flops 1 | bytes 1 | tf_op jit(solution)/shard_map/intra/pallas_call | solution.py:128
  21.3 3.3 %collective-permute-done.3.other = f32[6,144,128]{2,1,0:T(8,128)S(1)} collective-permute-done((f32[6,144,128]{2,1,0:T(8,128)S(1)}, f32[6,144,128]{2,1,0:T(8,128)S(1)}, u32[]{:S(2)}, u32[]{:S(2)}) %collective-permute-start.3) | collective-permute-done | bytes 442400 | tf_op jit(solution)/shard_map/ppermute | solution.py:351
  24.7 0.7 row.2
  25.3 3.1 %collective-permute-start.4 = (bf16[6,128,128]{2,1,0:T(8,128)(2,1)S(1)}, bf16[6,128,128]{2,1,0:T(8,128)(2,1)S(1)}, u32[]{:S(2)}, u32[]{:S(2)}) collective-permute-start(bf16[6,128,128]{2,1,0:T(8,128)(2,1)S(1)} %get-tuple-element.45.dep), channel_id=1, source_target_pairs={{0,4},{1,5},{2,6},{3,7},{16,20},{17,21},{18,22},{19,23}} | collective-permute-start | bytes 589832 | tf_op jit(solution)/shard_map/ppermute | solution.py:486
  28.4 0.0 copy-done.3
  28.4 3.0 %intra.5 = (f32[256,768]{1,0:T(8,128)S(1)}, f32[256,768]{1,0:T(8,128)S(1)}) custom-call(s32[1]{0:T(128)} %bitcast.place, bf16[256,6144]{1,0:T(8,128)(2,1)S(1)} %copy-done.3, bf16[256,6144]{1,0:T(8,128)(2,1)S(1)} %copy-done, bf16[256,6144]{1,0:T(8,128)(2,1)S(1)} %copy-done.1, f32[48,256]{1,0:T(8,128)S(1)} %bitcast.14, ...), custom_call_target="tpu_custom_call" | custom-call | flops 1 | bytes 1 | tf_op jit(solution)/shard_map/intra/pallas_call | solution.py:128
  31.5 0.0 collective-permute-done.4.rest_0_
  31.5 0.6 hop.4.dep
  32.1 0.7 collective-permute-start.6
  32.7 1.4 collective-permute-done.2.other
  34.1 0.7 row.3
  34.8 3.1 %collective-permute-start.5 = (bf16[6,128,128]{2,1,0:T(8,128)(2,1)S(1)}, bf16[6,128,128]{2,1,0:T(8,128)(2,1)S(1)}, u32[]{:S(2)}, u32[]{:S(2)}) collective-permute-start(bf16[6,128,128]{2,1,0:T(8,128)(2,1)S(1)} %get-tuple-element.47.dep), channel_id=1, source_target_pairs={{0,4},{1,5},{2,6},{3,7},{16,20},{17,21},{18,22},{19,23}} | collective-permute-start | bytes 589832 | tf_op jit(solution)/shard_map/ppermute | solution.py:486
  37.9 3.0 %intra.6 = (f32[256,768]{1,0:T(8,128)S(1)}, f32[256,768]{1,0:T(8,128)S(1)}) custom-call(s32[1]{0:T(128)} %bitcast.place, bf16[256,6144]{1,0:T(8,128)(2,1)S(1)} %copy-done.3, bf16[256,6144]{1,0:T(8,128)(2,1)S(1)} %copy-done, bf16[256,6144]{1,0:T(8,128)(2,1)S(1)} %copy-done.1, f32[48,256]{1,0:T(8,128)S(1)} %bitcast.15, ...), custom_call_target="tpu_custom_call" | custom-call | flops 1 | bytes 1 | tf_op jit(solution)/shard_map/intra/pallas_call | solution.py:128
  40.9 0.0 collective-permute-done.6.rest_1_
  40.9 0.6 hop.5.rest_1_
  41.6 0.7 collective-permute-start.8
  42.2 0.0 collective-permute-done.5.rest_0_
  42.2 0.6 hop.6.dep
  42.8 0.9 collective-permute-start.7
  43.7 3.0 %intra.7 = (f32[256,768]{1,0:T(8,128)S(1)}, f32[256,768]{1,0:T(8,128)S(1)}) custom-call(s32[1]{0:T(128)} %bitcast.place, bf16[256,6144]{1,0:T(8,128)(2,1)S(1)} %copy-done.3, bf16[256,6144]{1,0:T(8,128)(2,1)S(1)} %copy-done, bf16[256,6144]{1,0:T(8,128)(2,1)S(1)} %copy-done.1, f32[48,256]{1,0:T(8,128)S(1)} %bitcast.16, bf16[6,128,128]{2,1,0:T(8,128)(2,1)S(1)} %hop.6.dep), custom_call_target="tpu_custom_call" | custom-call | flops 1 | bytes 1 | tf_op jit(solution)/shard_map/intra/pallas_call | solution.py:128
  46.7 0.0 collective-permute-done.8.rest_2_
  46.7 0.7 side.2
  47.5 1.3 collective-permute-start.10
  48.8 0.0 collective-permute-done.7.rest_1_
  48.8 0.6 hop.7.dep
  49.4 0.7 collective-permute-start.9
  50.1 2.0 collective-permute-done.10.there
  52.1 1.5 core.2
  53.6 0.0 collective-permute-done.9.rest_2_
  53.6 0.7 side.3
  54.3 1.3 collective-permute-start.11
  55.6 4.5 %collective-permute-start.13 = (f32[2,6,128,128]{3,2,1,0:T(8,128)S(1)}, f32[2,6,128,128]{3,2,1,0:T(8,128)S(1)}, u32[]{:S(2)}, u32[]{:S(2)}) collective-permute-start(f32[2,6,128,128]{3,2,1,0:T(8,128)S(1)} %get-tuple-element.53.rest_3_), channel_id=1, source_target_pairs={{0,1},{1,0},{2,3},{3,2},{4,5},{5,4},{6,7},{7,6},{8,9},{9,8},{10,11... | collective-permute-start | bytes 2359304 | tf_op jit(solution)/shard_map/ppermute | solution.py:351
  60.2 0.0 collective-permute-done.11.there
  60.2 0.8 core.3
  60.9 4.2 %collective-permute-start.12 = (f32[2,6,128,128]{3,2,1,0:T(8,128)S(1)}, f32[2,6,128,128]{3,2,1,0:T(8,128)S(1)}, u32[]{:S(2)}, u32[]{:S(2)}) collective-permute-start(f32[2,6,128,128]{3,2,1,0:T(8,128)S(1)} %get-tuple-element.57.dep), channel_id=1, source_target_pairs={{0,1},{1,0},{2,3},{3,2},{4,5},{5,4},{6,7},{7,6},{8,9},{9,8},{10,11... | collective-permute-start | bytes 2359304 | tf_op jit(solution)/shard_map/ppermute | solution.py:351
  65.1 0.0 collective-permute-done.13.there
  65.2 0.0 copy-done.4
  65.2 0.0 copy-start.10
  65.2 0.0 copy-start.12
  65.2 0.0 copy-start.13
  65.2 3.7 %branch.1 = (f32[256,3072]{1,0:T(8,128)S(1)}, f32[256,128]{1,0:T(8,128)S(1)}) custom-call(s32[1]{0:T(128)} %bitcast.place, bf16[256,6144]{1,0:T(8,128)(2,1)S(1)} %copy-done.3, bf16[256,6144]{1,0:T(8,128)(2,1)S(1)} %copy-done.4, f32[1,6144]{1,0:T(1,128)S(1)} %bitcast.19, f32[48,256]{1,0:T(8,128)S(1)} %bitcast.17, ...), custom_call_target="tpu_custom_call" | custom-call | flops 1 | bytes 1 | tf_op jit(solution)/shard_map/branch/pallas_call | solution.py:190
  68.9 0.0 collective-permute-done.12.there
  68.9 11.8 %finish.1 = bf16[640,6144]{1,0:T(8,128)(2,1)} custom-call(s32[1]{0:T(128)} %bitcast.place, bf16[256,6144]{1,0:T(8,128)(2,1)S(1)} %copy-done.3, bf16[256,6144]{1,0:T(8,128)(2,1)S(1)} %copy-done.4, f32[1,6144]{1,0:T(1,128)S(1)} %bitcast.20, f32[48,256]{1,0:T(8,128)S(1)} %bitcast.18, f32[2,6,128,128]{3,2,1,0:T(8,128)S(1)} %get-tuple-element.56.own, ...), custom_call_target="tpu_custom_call" | custom-call | flops 1 | bytes 1 | tf_op jit(solution)/shard_map/finish/pallas_call | solution.py:304
  80.8 177.4 %all_to_all.11 = bf16[16,40,6144]{2,1,0:T(8,128)(2,1)S(1)} all-to-all(bf16[16,40,6144]{2,1,0:T(8,128)(2,1)} %bitcast.23), channel_id=1, replica_groups=mesh['groups'=2,'ctx'=16] {'ctx'}, dimensions={0} | all-to-all | bytes 15728640 | tf_op jit(solution)/shard_map/all_to_all | solution.py:522
  258.2 4.3 %land.1 = bf16[1,640,6144]{2,1,0:T(8,128)(2,1)} custom-call(bf16[640,6144]{1,0:T(8,128)(2,1)S(1)} %bitcast.9), custom_call_target="tpu_custom_call" | custom-call | flops 1 | bytes 1 | tf_op jit(solution)/shard_map/land/pallas_call | solution.py:337
  (15 shorter events, 0.0 us)
Async XLA Ops:
  4.3 5.2 %collective-permute-start.1 = (f32[2,6,136,128]{3,2,1,0:T(8,128)}, f32[2,6,136,128]{3,2,1,0:T(8,128)}, u32[]{:S(2)}, u32[]{:S(2)}) collective-permute-start(f32[2,6,136,128]{3,2,1,0:T(8,128)} %get-tuple-element.35.dep), channel_id=1, source_target_pairs={{0,1},{1,0},{2,3},{3,2},{4,5},{5,4},{6,7},{7,6},{8,9},{9,8},{10,11... | collective-permute-start | bytes 2506760 | tf_op jit(solution)/shard_map/ppermute | solution.py:351
  4.5 10.0 %collective-permute-start = (f32[2,6,136,128]{3,2,1,0:T(8,128)}, f32[2,6,136,128]{3,2,1,0:T(8,128)S(1)}, u32[]{:S(2)}, u32[]{:S(2)}) collective-permute-start(f32[2,6,136,128]{3,2,1,0:T(8,128)} %get-tuple-element.37), channel_id=1, source_target_pairs={{0,1},{1,0},{2,3},{3,2},{4,5},{5,4},{6,7},{7,6},{8,9},{9,8},{10,11... | collective-permute-start | bytes 2506760 | tf_op jit(solution)/shard_map/ppermute | solution.py:351
  4.9 11.5 %copy-start.1 = (bf16[256,6144]{1,0:T(8,128)(2,1)S(1)}, bf16[256,6144]{1,0:T(8,128)(2,1)}, u32[]{:S(2)}) copy-start(bf16[256,6144]{1,0:T(8,128)(2,1)} %v_ref.7) | copy-start | bytes 9437188
  4.9 11.5 %copy-start.7 = (f32[256,48]{0,1:T(8,128)S(1)}, f32[256,48]{0,1:T(8,128)}, u32[]{:S(2)}) copy-start(f32[256,48]{0,1:T(8,128)} %param.12) | copy-start | bytes 147460
  9.4 7.0 %copy-start = (bf16[256,6144]{1,0:T(8,128)(2,1)S(1)}, bf16[256,6144]{1,0:T(8,128)(2,1)}, u32[]{:S(2)}) copy-start(bf16[256,6144]{1,0:T(8,128)(2,1)} %k_ref.7) | copy-start | bytes 9437188
  9.5 1.3 copy-start.5
  12.1 12.5 %collective-permute-start.3 = (f32[6,144,128]{2,1,0:T(8,128)S(1)}, f32[6,144,128]{2,1,0:T(8,128)S(1)}, u32[]{:S(2)}, u32[]{:S(2)}) collective-permute-start(f32[6,144,128]{2,1,0:T(8,128)S(1)} %get-tuple-element.42), channel_id=1, source_target_pairs={{0,2},{1,3},{2,0},{3,1},{4,6},{5,7},{6,4},{7,5},{8,10},{9,11},{10,... | collective-permute-start | bytes 1327112 | tf_op jit(solution)/shard_map/ppermute | solution.py:351
  14.5 1.2 copy-start.8
  16.3 17.8 %collective-permute-start.2 = (f32[6,144,128]{2,1,0:T(8,128)S(1)}, f32[6,144,128]{2,1,0:T(8,128)S(1)}, u32[]{:S(2)}, u32[]{:S(2)}) collective-permute-start(f32[6,144,128]{2,1,0:T(8,128)S(1)} %get-tuple-element.41), channel_id=1, source_target_pairs={{0,2},{1,3},{2,0},{3,1},{4,6},{5,7},{6,4},{7,5},{8,10},{9,11},{10,... | collective-permute-start | bytes 1327112 | tf_op jit(solution)/shard_map/ppermute | solution.py:351
  16.4 1.9 copy-start.2
  18.3 10.1 %copy-start.3 = (bf16[256,6144]{1,0:T(8,128)(2,1)S(1)}, bf16[256,6144]{1,0:T(8,128)(2,1)}, u32[]{:S(2)}) copy-start(bf16[256,6144]{1,0:T(8,128)(2,1)} %q_ref.11) | copy-start | bytes 9437188
  25.3 6.1 %collective-permute-start.4 = (bf16[6,128,128]{2,1,0:T(8,128)(2,1)S(1)}, bf16[6,128,128]{2,1,0:T(8,128)(2,1)S(1)}, u32[]{:S(2)}, u32[]{:S(2)}) collective-permute-start(bf16[6,128,128]{2,1,0:T(8,128)(2,1)S(1)} %get-tuple-element.45.dep), channel_id=1, source_target_pairs={{0,4},{1,5},{2,6},{3,7},{16,20},{17,21},{18,22},{19,23}} | collective-permute-start | bytes 589832 | tf_op jit(solution)/shard_map/ppermute | solution.py:486
  32.1 8.9 %collective-permute-start.6 = (bf16[6,128,128]{2,1,0:T(8,128)(2,1)S(1)}, bf16[6,128,128]{2,1,0:T(8,128)(2,1)S(1)}, u32[]{:S(2)}, u32[]{:S(2)}) collective-permute-start(bf16[6,128,128]{2,1,0:T(8,128)(2,1)S(1)} %hop.4.dep), channel_id=1, source_target_pairs={{4,8},{5,9},{6,10},{7,11},{20,24},{21,25},{22,26},{23,27}} | collective-permute-start | bytes 589832 | tf_op jit(solution)/shard_map/ppermute | solution.py:486
  34.8 7.4 %collective-permute-start.5 = (bf16[6,128,128]{2,1,0:T(8,128)(2,1)S(1)}, bf16[6,128,128]{2,1,0:T(8,128)(2,1)S(1)}, u32[]{:S(2)}, u32[]{:S(2)}) collective-permute-start(bf16[6,128,128]{2,1,0:T(8,128)(2,1)S(1)} %get-tuple-element.47.dep), channel_id=1, source_target_pairs={{0,4},{1,5},{2,6},{3,7},{16,20},{17,21},{18,22},{19,23}} | collective-permute-start | bytes 589832 | tf_op jit(solution)/shard_map/ppermute | solution.py:486
  41.6 5.2 %collective-permute-start.8 = (bf16[6,128,128]{2,1,0:T(8,128)(2,1)S(1)}, bf16[6,128,128]{2,1,0:T(8,128)(2,1)S(1)}, u32[]{:S(2)}, u32[]{:S(2)}) collective-permute-start(bf16[6,128,128]{2,1,0:T(8,128)(2,1)S(1)} %hop.5.rest_1_), channel_id=1, source_target_pairs={{8,12},{9,13},{10,14},{11,15},{24,28},{25,29},{26,30},{27,31}} | collective-permute-start | bytes 589832 | tf_op jit(solution)/shard_map/ppermute | solution.py:486
  42.8 5.9 %collective-permute-start.7 = (bf16[6,128,128]{2,1,0:T(8,128)(2,1)S(1)}, bf16[6,128,128]{2,1,0:T(8,128)(2,1)S(1)}, u32[]{:S(2)}, u32[]{:S(2)}) collective-permute-start(bf16[6,128,128]{2,1,0:T(8,128)(2,1)S(1)} %hop.6.dep), channel_id=1, source_target_pairs={{4,8},{5,9},{6,10},{7,11},{20,24},{21,25},{22,26},{23,27}} | collective-permute-start | bytes 589832 | tf_op jit(solution)/shard_map/ppermute | solution.py:486
  46.7 5.3 %copy-start.6 = (f32[2,6,136,128]{3,2,1,0:T(8,128)S(1)}, f32[2,6,136,128]{3,2,1,0:T(8,128)}, u32[]{:S(2)}) copy-start(f32[2,6,136,128]{3,2,1,0:T(8,128)} %get-tuple-element.38.keep.dep) | copy-start | bytes 2506756
  47.5 12.7 %copy-start.9 = (f32[2,6,136,128]{3,2,1,0:T(8,128)S(1)}, f32[2,6,136,128]{3,2,1,0:T(8,128)}, u32[]{:S(2)}) copy-start(f32[2,6,136,128]{3,2,1,0:T(8,128)} %get-tuple-element.36.keep) | copy-start | bytes 2506756
  47.5 4.6 %collective-permute-start.10 = (bf16[6,128,128]{2,1,0:T(8,128)(2,1)S(1)}, bf16[6,128,128]{2,1,0:T(8,128)(2,1)S(1)}, u32[]{:S(2)}, u32[]{:S(2)}) collective-permute-start(bf16[6,128,128]{2,1,0:T(8,128)(2,1)S(1)} %get-tuple-element.51.rest_2_), channel_id=1, source_target_pairs={{0,2},{1,3},{2,0},{3,1},{4,6},{5,7},{6,4},{7,5},{8,10},{9,11},{10,... | collective-permute-start | bytes 589832 | tf_op jit(solution)/shard_map/ppermute | solution.py:351
  49.4 4.2 %collective-permute-start.9 = (bf16[6,128,128]{2,1,0:T(8,128)(2,1)S(1)}, bf16[6,128,128]{2,1,0:T(8,128)(2,1)S(1)}, u32[]{:S(2)}, u32[]{:S(2)}) collective-permute-start(bf16[6,128,128]{2,1,0:T(8,128)(2,1)S(1)} %hop.7.dep), channel_id=1, source_target_pairs={{8,12},{9,13},{10,14},{11,15},{24,28},{25,29},{26,30},{27,31}} | collective-permute-start | bytes 589832 | tf_op jit(solution)/shard_map/ppermute | solution.py:486
  52.1 13.1 %copy-start.4 = (bf16[256,6144]{1,0:T(8,128)(2,1)S(1)}, bf16[256,6144]{1,0:T(8,128)(2,1)}, u32[]{:S(2)}) copy-start(bf16[256,6144]{1,0:T(8,128)(2,1)} %gate_ref.3) | copy-start | bytes 9437188
  52.1 13.1 %copy-start.11 = (f32[6144]{0:T(1024)S(1)}, f32[6144]{0:T(1024)}, u32[]{:S(2)}) copy-start(f32[6144]{0:T(1024)} %param.15) | copy-start | bytes 73732
  54.3 5.8 %collective-permute-start.11 = (bf16[6,128,128]{2,1,0:T(8,128)(2,1)S(1)}, bf16[6,128,128]{2,1,0:T(8,128)(2,1)S(1)}, u32[]{:S(2)}, u32[]{:S(2)}) collective-permute-start(bf16[6,128,128]{2,1,0:T(8,128)(2,1)S(1)} %get-tuple-element.55.dep), channel_id=1, source_target_pairs={{0,2},{1,3},{2,0},{3,1},{4,6},{5,7},{6,4},{7,5},{8,10},{9,11},{10,... | collective-permute-start | bytes 589832 | tf_op jit(solution)/shard_map/ppermute | solution.py:351
  55.6 9.5 %collective-permute-start.13 = (f32[2,6,128,128]{3,2,1,0:T(8,128)S(1)}, f32[2,6,128,128]{3,2,1,0:T(8,128)S(1)}, u32[]{:S(2)}, u32[]{:S(2)}) collective-permute-start(f32[2,6,128,128]{3,2,1,0:T(8,128)S(1)} %get-tuple-element.53.rest_3_), channel_id=1, source_target_pairs={{0,1},{1,0},{2,3},{3,2},{4,5},{5,4},{6,7},{7,6},{8,9},{9,8},{10,11... | collective-permute-start | bytes 2359304 | tf_op jit(solution)/shard_map/ppermute | solution.py:351
  60.9 8.0 %collective-permute-start.12 = (f32[2,6,128,128]{3,2,1,0:T(8,128)S(1)}, f32[2,6,128,128]{3,2,1,0:T(8,128)S(1)}, u32[]{:S(2)}, u32[]{:S(2)}) collective-permute-start(f32[2,6,128,128]{3,2,1,0:T(8,128)S(1)} %get-tuple-element.57.dep), channel_id=1, source_target_pairs={{0,1},{1,0},{2,3},{3,2},{4,5},{5,4},{6,7},{7,6},{8,9},{9,8},{10,11... | collective-permute-start | bytes 2359304 | tf_op jit(solution)/shard_map/ppermute | solution.py:351
  65.2 3.8 %copy-start.10 = (bf16[256,6144]{1,0:T(8,128)(2,1)S(1)}, bf16[256,6144]{1,0:T(8,128)(2,1)}, u32[]{:S(2)}) copy-start(bf16[256,6144]{1,0:T(8,128)(2,1)} %rest_6_.1) | copy-start | bytes 9437188
  65.2 3.8 %copy-start.12 = (f32[6144]{0:T(1024)S(1)}, f32[6144]{0:T(1024)}, u32[]{:S(2)}) copy-start(f32[6144]{0:T(1024)} %param.16) | copy-start | bytes 73732
  65.2 3.8 %copy-start.13 = (s32[256,2]{0,1:T(2,128)S(1)}, s32[256,2]{0,1:T(2,128)}, u32[]{:S(2)}) copy-start(s32[256,2]{0,1:T(2,128)} %param.17) | copy-start | bytes 6148

commit v3 on v2

v3 whole, which is shorter than its diff:
```python
import functools
import jax
import jax.numpy as jnp
from jax import lax
from jax.experimental import pallas as pl
from jax.experimental.pallas import tpu as pltpu
from jax.sharding import PartitionSpec as P

EXP_DEV = 1
SLOTS = 4
CHUNKS = 2
LANES = 128
TAIL = 8
F32 = jnp.float32
BF16 = jnp.bfloat16
ANY = pl.BlockSpec(memory_space=pl.ANY)
VMEM = pl.BlockSpec(memory_space=pltpu.VMEM)
SMEM = pl.BlockSpec(memory_space=pltpu.SMEM)
BRIEF = pl.CostEstimate(flops=1, bytes_accessed=1, transcendentals=0)


def dot(a, b, contract=(1, 0)):
    return lax.dot_general(a, b, ((contract[:1], contract[1:]), ((), ())), preferred_element_type=F32)


def running(ld_ref, group, count):
    ld = ld_ref[:count, :]
    for g in range(1, ld_ref.shape[0] // count):
        ld = jnp.where(group == g, ld_ref[g * count : (g + 1) * count, :], ld)
    tok = ld.shape[1]
    row = lax.broadcasted_iota(jnp.int32, (tok, tok), 0)
    col = lax.broadcasted_iota(jnp.int32, (tok, tok), 1)
    upper = (row <= col).astype(F32).astype(BF16)
    high = ld.astype(BF16)
    rest = ld - high.astype(F32)
    mid = rest.astype(BF16)
    low = (rest - mid.astype(F32)).astype(BF16)
    return dot(high, upper) + (dot(mid, upper) + dot(low, upper))


def state_kernel(first_slot, chunk, hd, place, k_ref, v_ref, ld_ref, dep, out):
    per = out.shape[1]
    for j in range(2):
        group = jnp.bitwise_xor(j + first_slot, place[0])
        cum = running(ld_ref, group, per * CHUNKS)[chunk * per : (chunk + 1) * per]
        total = cum[:, -1:]
        weight = jnp.exp(total - cum)
        decay = jnp.exp(total)
        for i in range(per):
            cols = pl.ds(pl.multiple_of(((group * CHUNKS + chunk) * per + i) * hd, hd), hd)
            wk = (weight[i : i + 1, :] * k_ref[:, cols].T.astype(F32)).astype(BF16)
            out[j, i, :hd, :] = dot(wk, v_ref[:, cols])
            out[j, i, hd:, :] = jnp.broadcast_to(decay[i : i + 1, :], (TAIL, hd))


def block_states(place, key_rows, value_rows, log_decay, dep, first_slot, chunk, hd):
    per = key_rows.shape[1] // SLOTS // CHUNKS // hd
    return pl.pallas_call(
        functools.partial(state_kernel, first_slot, chunk, hd),
        in_specs=[SMEM] + [VMEM] * 3 + [ANY],
        out_specs=VMEM,
        out_shape=jax.ShapeDtypeStruct((2, per, hd + TAIL, hd), F32),
        compiler_params=pltpu.CompilerParams(vmem_limit_bytes=16 << 20),
        cost_estimate=BRIEF,
        name="block_states",
    )(place, key_rows, value_rows, log_decay, dep)


def intra_kernel(hd, slot, place, q_ref, k_ref, v_ref, ld_ref, dep, *outs):
    tok, cw = outs[0].shape
    per = cw // hd
    gh = per * CHUNKS
    half = tok // 2
    group = jnp.bitwise_xor(slot, place[0])
    cum_rows = running(ld_ref, group, gh)
    cum = cum_rows.T
    row = lax.broadcasted_iota(jnp.int32, (half, half), 0)
    col = lax.broadcasted_iota(jnp.int32, (half, half), 1)
    causal = row >= col
    for i in range(gh):
        cols = pl.ds(pl.multiple_of(group * (gh * hd) + i * hd, hd), hd)
        o_ref, to = outs[i // per], slice(i % per * hd, (i % per + 1) * hd)
        down, across = cum[:, i : i + 1], cum_rows[i : i + 1, :]
        q, k, v = q_ref[:, cols], k_ref[:, cols], v_ref[:, cols]
        parts = []
        for first in (0, half):
            at = slice(first, first + half)
            score = dot(q[at], k[at], (1, 1))
            weights = jnp.where(causal, score * jnp.exp(down[at] - across[:, at]), 0.0).astype(BF16)
            parts.append(dot(weights, v[at]))
        o_ref[:half, to] = parts[0]
        middle = across[:, half - 1 : half]
        score = dot(q[half:], k[:half], (1, 1))
        weights = (score * (jnp.exp(down[half:] - middle) * jnp.exp(middle - across[:, :half]))).astype(BF16)
        o_ref[half:, to] = parts[1] + dot(weights, v[:half])


def intra(place, query, key_rows, value_rows, log_decay, dep, slot, hd):
    tok, width = query.shape
    cw = width // SLOTS // CHUNKS
    return pl.pallas_call(
        functools.partial(intra_kernel, hd, slot),
        in_specs=[SMEM] + [VMEM] * 4 + [ANY],
        out_specs=[VMEM] * CHUNKS,
        out_shape=[jax.ShapeDtypeStruct((tok, cw), F32)] * CHUNKS,
        compiler_params=pltpu.CompilerParams(vmem_limit_bytes=16 << 20),
        cost_estimate=BRIEF,
        name="intra",
    )(place, query, key_rows, value_rows, log_decay, dep)


def add_branch(hd, chunk, place, q_ref, gate_ref, ag_ref, ld_ref, own, there, ins, o_ref):
    per = own.shape[1]
    cw = per * hd
    squares = 0.0
    for slot in range(SLOTS):
        group = jnp.bitwise_xor(slot, place[0])
        cum = running(ld_ref, group, per * CHUNKS)[chunk * per : (chunk + 1) * per]
        grow = jnp.exp(cum).T
        for i in range(per):
            carried = (own if slot < 2 else there)[slot % 2, i]
            high = carried.astype(BF16)
            low = (carried - high.astype(F32)).astype(BF16)
            where = pl.ds(pl.multiple_of((group * CHUNKS + chunk) * cw + i * hd, hd), hd)
            q = q_ref[:, where]
            att = ins[slot][:, i * hd : (i + 1) * hd] + grow[:, i : i + 1] * (dot(q, high) + dot(q, low))
            squares = squares + att * att
            opened = 0.5 * jnp.tanh(0.5 * gate_ref[:, where].astype(F32)) + 0.5
            o_ref[:, slot * cw + i * hd : slot * cw + (i + 1) * hd] = att * (ag_ref[:, where] * opened)
    return squares


def branch_kernel(hd, chunk, place, q_ref, gate_ref, ag_ref, ld_ref, own, there, dep, *rest):
    o_ref, sq_ref = rest[SLOTS:]
    sq_ref[...] = add_branch(
        hd, chunk, place, q_ref, gate_ref, ag_ref, ld_ref, own, there, rest[:SLOTS], o_ref
    )


def branch(place, query, gate, attn_gain, log_decay, states, intra_outs, dep, chunk, hd):
    tok, width = query.shape
    return pl.pallas_call(
        functools.partial(branch_kernel, hd, chunk),
        in_specs=[SMEM] + [VMEM] * 6 + [ANY] + [VMEM] * SLOTS,
        out_specs=[VMEM] * 2,
        out_shape=[
            jax.ShapeDtypeStruct((tok, width // CHUNKS), F32),
            jax.ShapeDtypeStruct((tok, hd), F32),
        ],
        compiler_params=pltpu.CompilerParams(vmem_limit_bytes=16 << 20),
        cost_estimate=BRIEF,
        name="branch",
    )(place, query, gate, attn_gain, log_decay, *states, dep, *intra_outs)


def finish_kernel(hd, cap, place, q_ref, gate_ref, ag_ref, ld_ref, own, there, dep, *rest):
    ins, rest = rest[:SLOTS], rest[SLOTS:]
    early, rest = rest[: CHUNKS - 1], rest[CHUNKS - 1 :]
    squares, rest = rest[: CHUNKS - 1], rest[CHUNKS - 1 :]
    res_ref, mg_ref, ids_ref, o_hbm, late, sq, hidden, normed, target, staged, sems = rest
    tok, width = normed.shape
    per = own.shape[1]
    cw = per * hd

    top = ids_ref.shape[0]
    experts = o_hbm.shape[0] // cap
    ids = ids_ref[...]
    expert = lax.broadcasted_iota(jnp.int32, (experts, tok), 0)
    hot = [(ids[k : k + 1, :] == expert).astype(F32) for k in range(top)]
    row = lax.broadcasted_iota(jnp.int32, (tok, tok), 0)
    col = lax.broadcasted_iota(jnp.int32, (tok, tok), 1)
    count = dot(sum(hot).astype(BF16), (row < col).astype(F32).astype(BF16))
    for k in range(top):
        slot = jnp.sum(hot[k] * count, axis=0, keepdims=True).astype(jnp.int32)
        target[k : k + 1, :] = ids[k : k + 1, :] * cap + slot
        count = count + hot[k]

    part = add_branch(
        hd, CHUNKS - 1, place, q_ref, gate_ref, ag_ref, ld_ref, own, there, ins, late
    )
    for s in squares:
        part = part + s[...]
    sq[...] = part

    rows = hidden.shape[0]

    @pl.loop(0, tok // rows)
    def _(step):
        at = pl.ds(pl.multiple_of(step * rows, rows), rows)
        scale = lax.rsqrt(jnp.sum(sq[at, :], axis=-1, keepdims=True) / width + 1e-06)
        total = jnp.zeros((rows, LANES), F32)
        for slot in range(SLOTS):
            group = jnp.bitwise_xor(slot, place[0])
            for k in range(CHUNKS):
                for n in range(cw // LANES):
                    here = slice(slot * cw + n * LANES, slot * cw + (n + 1) * LANES)
                    where = pl.ds(pl.multiple_of((group * CHUNKS + k) * cw + n * LANES, LANES), LANES)
                    value = (early[k] if k < CHUNKS - 1 else late)[at, here]
                    value = res_ref[at, where].astype(F32) + value * scale
                    total = total + value * value
                    hidden[:, where] = value
        scale = lax.rsqrt(jnp.sum(total, axis=-1, keepdims=True) / width + 1e-06)
        for n in range(width // LANES):
            cols = slice(n * LANES, (n + 1) * LANES)
            normed[at, cols] = (hidden[:, cols] * scale * mg_ref[:, cols]).astype(BF16)

    steps = sems.shape[0]
    out_rows = o_hbm.shape[0] // steps

    def copy(step):
        at = pl.ds(pl.multiple_of(step * out_rows, out_rows), out_rows)
        return pltpu.make_async_copy(staged.at[at], o_hbm.at[at], sems.at[step])

    @pl.loop(0, steps)
    def _(step):
        at = pl.ds(pl.multiple_of(step * out_rows, out_rows), out_rows)
        row = lax.broadcasted_iota(jnp.int32, (out_rows, tok), 0) + step * out_rows
        hit = row == target[0:1, :]
        for k in range(1, top):
            hit = hit | (row == target[k : k + 1, :])
        pick = hit.astype(F32).astype(BF16)
        part = width // 4
        for n in range(4):
            cols = slice(n * part, (n + 1) * part)
            staged[at, cols] = dot(pick, normed[:, cols]).astype(BF16)
        copy(step).start()

    for step in range(steps):
        copy(step).wait()


def finish(
    place, query, gate, attn_gain, log_decay, states, intra_outs, early, squares, residual, moe_gain, ids, dep, cap, experts, hd
):
    tok, width = query.shape
    steps = 4
    return pl.pallas_call(
        functools.partial(finish_kernel, hd, cap),
        in_specs=[SMEM] + [VMEM] * 6 + [ANY] + [VMEM] * (SLOTS + 2 * (CHUNKS - 1) + 3),
        out_specs=pl.BlockSpec(memory_space=pl.ANY),
        scratch_shapes=[
            pltpu.VMEM((tok, width // CHUNKS), F32),
            pltpu.VMEM((tok, hd), F32),
            pltpu.VMEM((tok // 4, width), F32),
            pltpu.VMEM((tok, width), BF16),
            pltpu.VMEM((8, tok), jnp.int32),
            pltpu.VMEM((experts * cap, width), BF16),
            pltpu.SemaphoreType.DMA((steps,)),
        ],
        out_shape=jax.ShapeDtypeStruct((experts * cap, width), BF16),
        compiler_params=pltpu.CompilerParams(vmem_limit_bytes=24 << 20),
        cost_estimate=BRIEF,
        name="finish",
    )(place, query, gate, attn_gain, log_decay, *states, dep, *intra_outs, *early, *squares, residual, moe_gain, ids)


def land_kernel(i_ref, o_ref, sems):
    steps = sems.shape[0]
    rows = i_ref.shape[0] // steps
    copies = [
        pltpu.make_async_copy(
            i_ref.at[pl.ds(n * rows, rows)], o_ref.at[0, pl.ds(n * rows, rows)], sems.at[n]
        )
        for n in range(steps)
    ]
    for c in copies:
        c.start()
    for c in copies:
        c.wait()


def land(arrived):
    return pl.pallas_call(
        land_kernel,
        in_specs=[ANY],
        out_specs=ANY,
        scratch_shapes=[pltpu.SemaphoreType.DMA((8,))],
        out_shape=jax.ShapeDtypeStruct((1,) + arrived.shape, arrived.dtype),
        compiler_params=pltpu.CompilerParams(vmem_limit_bytes=16 << 20),
        cost_estimate=BRIEF,
        name="land",
    )(arrived)


def swap(value, bit):
    size = lax.axis_size("ctx")
    return lax.ppermute(value, "ctx", [(i, i ^ bit) for i in range(size)])


def small(kernel, name, flags, ins, dep, outs):
    return pl.pallas_call(
        kernel,
        in_specs=[SMEM] + [VMEM] * len(ins) + [ANY],
        out_specs=[VMEM] * len(outs),
        out_shape=[jax.ShapeDtypeStruct(shape, kind) for shape, kind in outs],
        compiler_params=pltpu.CompilerParams(vmem_limit_bytes=16 << 20),
        cost_estimate=BRIEF,
        name=name,
    )(flags, *ins, dep)


def later(before, decay, state):
    return decay * before + state


def decay_rows(decay, rows):
    high = decay.astype(BF16).astype(F32)
    mid = (decay - high).astype(BF16).astype(F32)
    low = decay - high - mid
    row = lax.broadcasted_iota(jnp.int32, (decay.shape[0], rows, decay.shape[2]), 1)
    return jnp.where(row == 0, high, jnp.where(row == 1, mid, jnp.where(row == 2, low, 0.0)))


def chip_kernel(flags, keep, received, dep, mine, sent, rest):
    hd = keep.shape[-1]
    low = flags[1] == 0
    for slot in range(2):
        a = jnp.where(low, keep[slot], received[slot])
        b = jnp.where(low, received[slot], keep[slot])
        state = later(a[:, :hd, :], b[:, hd : hd + 1, :], b[:, :hd, :])
        decay = a[:, hd:, :] * b[:, hd:, :]
        if slot == 0:
            mine[:, :hd, :] = state
            mine[:, hd:, :] = decay
        else:
            high = state.astype(BF16)
            sent[:, :hd, :] = high
            sent[:, hd:, :] = decay_rows(decay[:, :1, :], 2 * TAIL).astype(BF16)
            rest[...] = (state - high.astype(F32)).astype(BF16)


def late_kernel(flags, *refs):
    count = len(refs) // 2
    for i_ref, o_ref in zip(refs[:count], refs[count + 1 :]):
        o_ref[...] = i_ref[...]


def row_parts(flags, mine, other, rest=None):
    hd = mine.shape[-1]
    low = flags[2] == 0
    a = (mine[:, :hd, :], mine[:, hd : hd + 1, :])
    state = other[:, :hd, :].astype(F32)
    if rest is not None:
        state = state + rest[...].astype(F32)
    b = (state, jnp.sum(other[:, hd:, :].astype(F32), axis=1, keepdims=True))
    first = tuple(jnp.where(low, x, y) for x, y in zip(a, b))
    second = tuple(jnp.where(low, y, x) for x, y in zip(a, b))
    return first, second


def row_kernel(flags, mine, other, dep, sent):
    first, second = row_parts(flags, mine, other)
    sent[...] = later(first[0], second[1], second[0]).astype(sent.dtype)


def arrived_sum(refs):
    return sum(r[...].astype(F32) for r in refs)


def hop_kernel(flags, mine, other, rest, *more):
    hops, sent = more[:-2], more[-1]
    first, second = row_parts(flags, mine, other, rest)
    total = later(first[0], second[1], second[0])
    sent[...] = later(arrived_sum(hops), first[1] * second[1], total).astype(sent.dtype)


def side_kernel(flags, mine, other, rest, *more):
    hops, (_, here, sent) = more[:-3], more[-3:]
    low = flags[2] == 0
    first, _ = row_parts(flags, mine, other, rest)
    before = arrived_sum(hops)
    entered = later(before, first[1], first[0])
    here[...] = jnp.where(low, before, entered)
    sent[...] = jnp.where(low, entered, before).astype(sent.dtype)


def core_kernel(flags, keep, received, here, there, dep, own, sent):
    hd = keep.shape[-1]
    low = flags[1] == 0
    for slot, ref in ((0, here), (1, there)):
        pair = ref[...].astype(F32)
        first = jnp.where(low, keep[slot], received[slot])
        second = later(pair, first[:, hd : hd + 1, :], first[:, :hd, :])
        own[slot] = jnp.where(low, pair, second)
        sent[slot] = jnp.where(low, second, pair)


def body(
    query, key_rows, value_rows, log_decay, gate_input, residual, attn_gain, moe_gain, expert_ids
):
    tok_rows, model_width = query.shape
    heads = log_decay.shape[1]
    hd = model_width // heads
    per = heads // SLOTS // CHUNKS
    size = lax.axis_size("ctx")
    hops = size // SLOTS - 1
    index = lax.axis_index("ctx").astype(jnp.int32)
    core, side = jnp.bitwise_and(index, 1), jnp.bitwise_and(lax.shift_right_logical(index, 1), 1)
    place = (2 * core + side)[None]
    flags = jnp.stack([2 * core + side, core, side])
    ld = log_decay.T
    ag, mg = attn_gain[None], moe_gain[None]
    full, wire, plain = (per, hd + TAIL, hd), (per, hd + 2 * TAIL, hd), (per, hd, hd)

    received, keep, mine, other, rest = [], [], [], [], []
    dep = ld

    def chip(k, dep):
        m, t, r = small(
            chip_kernel, "chip", flags, [keep[k], received[k]], dep, [(full, F32), (wire, BF16), (plain, BF16)]
        )
        mine.append(m)
        other.append(swap(t, 2))
        rest.append(r)
        return m

    for k in range(CHUNKS):
        dep = block_states(place, key_rows, value_rows, ld, dep, 2, k, hd)
        received.append(swap(dep, 1))
        if k:
            dep = chip(k - 1, dep)
        dep = block_states(place, key_rows, value_rows, ld, dep, 0, k, hd)
        keep.append(dep)
    dep = chip(CHUNKS - 1, dep)

    intra_outs = []
    arrived = [[] for _ in range(CHUNKS)]
    here, there, states = [None] * CHUNKS, [None] * CHUNKS, [None] * CHUNKS
    early, squares = [], []

    def more_intra(dep):
        if len(intra_outs) < SLOTS:
            intra_outs.append(intra(place, query, key_rows, value_rows, ld, dep, len(intra_outs), hd))
            dep = intra_outs[-1][0]
        return dep

    def hop(k, sent):
        s = len(arrived[k])
        pairs = [(s * SLOTS + j, (s + 1) * SLOTS + j) for j in range(SLOTS)]
        arrived[k].append(lax.ppermute(sent, "ctx", pairs))

    dep = more_intra(dep)
    rest = small(late_kernel, "late", flags, rest, dep, [(plain, BF16)] * CHUNKS)
    dep = rest[0]
    rest = [swap(r, 2) for r in rest]
    order = sorted(((k, stage) for k in range(CHUNKS) for stage in range(hops + 2)), key=lambda r: r[1] + 0.6 * r[0])
    for k, stage in order:
        if stage == 0:
            (dep,) = small(row_kernel, "row", flags, [mine[k], other[k]], dep, [(plain, BF16)])
            hop(k, dep)
        elif stage < hops:
            (dep,) = small(
                hop_kernel, "hop", flags, [mine[k], other[k], rest[k]] + arrived[k], dep, [(plain, BF16)]
            )
            hop(k, dep)
        elif stage == hops:
            here[k], dep = small(
                side_kernel,
                "side",
                flags,
                [mine[k], other[k], rest[k]] + arrived[k],
                dep,
                [(plain, F32), (plain, BF16)],
            )
            there[k] = swap(dep, 2)
        else:
            own, dep = small(
                core_kernel, "core", flags, [keep[k], received[k], here[k], there[k]], dep, [((2,) + plain, F32)] * 2
            )
            states[k] = (own, swap(dep, 1))
        dep = more_intra(dep)
    while len(intra_outs) < SLOTS:
        dep = more_intra(dep)
    for k in range(CHUNKS - 1):
        dep, sq = branch(place, query, gate_input, ag, ld, states[k], [o[k] for o in intra_outs], dep, k, hd)
        early.append(dep)
        squares.append(sq)

    expert_count = EXP_DEV * size
    capacity = 5 * tok_rows * expert_ids.shape[1] // (4 * expert_count)
    outgoing = finish(
        place, query, gate_input, ag, ld, states[-1], [o[-1] for o in intra_outs], early, squares,
        residual, mg, expert_ids.T, dep, capacity, expert_count, hd,
    )
    return land(lax.all_to_all(outgoing, "ctx", split_axis=0, concat_axis=0, tiled=True))


def solution(mesh):
    rows = P(("groups", "ctx"), None)
    in_specs = (rows, rows, rows, rows, rows, rows, P(), P(), rows)
    out_specs = P(("groups", "ctx"), None, None)
    return jax.shard_map(body, mesh=mesh, in_specs=in_specs, out_specs=out_specs, check_vma=False)
```

time: 263 us -> 249 us (0.947)
  Pallas kernels: 50.2 us -> 40.3 us
  waiting for transfers between devices: 6.7 us -> 2.25 us
  blocking collectives: 177 us -> 180 us
  starting transfers between devices: 23.5 us -> 20.8 us
    pallas_call x9 -> x11, Pallas kernels: 40.7 us -> 31.2 us  [the longest x4 11.9 us: intra(): pl.pallas_call(functools.partial(intra_kernel, hd, slot), in_specs=[SMEM]...]
    ppermute x8 -> x10, waiting for transfers between devices: 6.68 us -> 2.23 us  [swap(): return lax.ppermute(value, 'ctx', [(i, i ^ bit) for i in range(size)])]
    ppermute x8 -> x10, starting transfers between devices: 14.4 us -> 13.4 us  [swap(): return lax.ppermute(value, 'ctx', [(i, i ^ bit) for i in range(size)])]
    pallas_call x12 -> x13, Pallas kernels: 9.44 us -> 9.11 us  [small(): pl.pallas_call(kernel, in_specs=[SMEM] + [VMEM] * len(ins) + [ANY], out_s...]
  transfers between devices with their start and end apart: 14 -> 16, of which waited for: 3 -> 1; matrix products, arithmetic and copies ran while one was open for 0% -> 0% of each run, Pallas kernels for 11% -> 11%
where the time goes in v3:
time: 249 us; the launch traced here: 248 us
  blocking collectives  180 us (72%)
  Pallas kernels  40.3 us (16%)
  starting transfers between devices  20.8 us (8%)
  local copies, waits for them, and re-layouts  4.63 us (2%)
    all_to_all x1, blocking collectives, body(): lax.all_to_all(outgoing, 'ctx', split_axis=0, concat_axis=0, tiled=True)  180 us
    ppermute x10, starting transfers between devices, swap(): return lax.ppermute(value, 'ctx', [(i, i ^ bit) for i in range(size)])  13.4 us
    pallas_call x4, Pallas kernels, intra(): pl.pallas_call(functools.partial(intra_kernel, hd, slot), in_specs=[SMEM]...  11.9 us
    pallas_call x1, Pallas kernels, finish(): pl.pallas_call(functools.partial(finish_kernel, hd, cap), in_specs=[SMEM]...  9.53 us
    pallas_call x13, Pallas kernels, small(): pl.pallas_call(kernel, in_specs=[SMEM] + [VMEM] * len(ins) + [ANY], out_s...  9.11 us
    ppermute x6, starting transfers between devices, hop(): arrived[k].append(lax.ppermute(sent, 'ctx', pairs))  7.39 us
  transfers between devices with their start and end apart: 16, of which 1 were waited for; matrix products, arithmetic and copies ran while one was open for 0% of the time, Pallas kernels for 11%

profile of v3, /device:TPU:1, one launch (start us, length us, event | category | flops | bytes accessed | tf_op | source)
XLA Modules:
  0.0 248.3 jit_solution(7002865904061656377)
XLA Ops:
  0.0 1.9 copy-done
  1.9 1.9 copy-done.2
  3.8 0.8 copy-done.6
  4.6 1.0 block_states.4.dep
  5.6 0.1 collective-permute-start
  5.7 1.0 block_states.5.dep.keep
  6.7 0.0 copy-start.1
  6.7 0.0 copy-start.3
  6.8 1.0 block_states.6.dep
  7.7 0.5 collective-permute-start.1
  8.3 0.1 pad_add_fusion.flags
  8.3 0.7 chip.2
  9.1 2.3 collective-permute-start.4
  11.4 1.0 block_states.7.keep.dep
  12.4 0.0 collective-permute-done.1.received
  12.4 0.7 chip.3
  13.1 0.9 collective-permute-start.2
  14.1 3.0 %intra.4 = (f32[256,768]{1,0:T(8,128)S(1)}, f32[256,768]{1,0:T(8,128)S(1)}) custom-call(s32[1]{0:T(128)} %bitcast.place, bf16[256,6144]{1,0:T(8,128)(2,1)S(1)} %copy-done.4, bf16[256,6144]{1,0:T(8,128)(2,1)S(1)} %copy-done.1, bf16[256,6144]{1,0:T(8,128)(2,1)S(1)} %copy-done.3, f32[48,256]{1,0:T(8,128)S(1)} %bitcast.16, ...), custom_call_target="tpu_custom_call" | custom-call | flops 1 | bytes 1 | tf_op jit(solution)/shard_map/intra/pallas_call | solution.py:101
  17.0 0.6 late.1
  17.6 0.7 collective-permute-start.6
  18.3 0.0 collective-permute-done.4.other
  18.3 0.6 row.2.dep
  18.9 3.2 %collective-permute-start.7 = (bf16[6,128,128]{2,1,0:T(8,128)(2,1)S(1)}, bf16[6,128,128]{2,1,0:T(8,128)(2,1)S(1)}, u32[]{:S(2)}, u32[]{:S(2)}) collective-permute-start(bf16[6,128,128]{2,1,0:T(8,128)(2,1)S(1)} %row.2.dep), channel_id=1, source_target_pairs={{0,4},{1,5},{2,6},{3,7},{16,20},{17,21},{18,22},{19,23}} | collective-permute-start | bytes 589832 | tf_op jit(solution)/shard_map/ppermute | solution.py:440
  22.1 0.9 collective-permute-start.3
  23.1 3.0 %intra.5 = (f32[256,768]{1,0:T(8,128)S(1)}, f32[256,768]{1,0:T(8,128)S(1)}) custom-call(s32[1]{0:T(128)} %bitcast.place, bf16[256,6144]{1,0:T(8,128)(2,1)S(1)} %copy-done.4, bf16[256,6144]{1,0:T(8,128)(2,1)S(1)} %copy-done.1, bf16[256,6144]{1,0:T(8,128)(2,1)S(1)} %copy-done.3, f32[48,256]{1,0:T(8,128)S(1)} %bitcast.17, bf16[6,128,128]{2,1,0:T(8,128)(2,1)S(1)} %row.2.dep), custom_call_target="tpu_custom_call" | custom-call | flops 1 | bytes 1 | tf_op jit(solution)/shard_map/intra/pallas_call | solution.py:101
  26.0 0.0 collective-permute-done.2.other
  26.0 0.6 row.3.dep
  26.7 1.3 collective-permute-start.5
  28.0 3.0 %intra.6 = (f32[256,768]{1,0:T(8,128)S(1)}, f32[256,768]{1,0:T(8,128)S(1)}) custom-call(s32[1]{0:T(128)} %bitcast.place, bf16[256,6144]{1,0:T(8,128)(2,1)S(1)} %copy-done.4, bf16[256,6144]{1,0:T(8,128)(2,1)S(1)} %copy-done.1, bf16[256,6144]{1,0:T(8,128)(2,1)S(1)} %copy-done.3, f32[48,256]{1,0:T(8,128)S(1)} %bitcast.18, bf16[6,128,128]{2,1,0:T(8,128)(2,1)S(1)} %row.3.dep), custom_call_target="tpu_custom_call" | custom-call | flops 1 | bytes 1 | tf_op jit(solution)/shard_map/intra/pallas_call | solution.py:101
  31.0 0.0 collective-permute-done.6.rest
  31.0 0.7 hop.4.dep
  31.7 0.9 collective-permute-start.9
  32.5 3.0 %intra.7 = (f32[256,768]{1,0:T(8,128)S(1)}, f32[256,768]{1,0:T(8,128)S(1)}) custom-call(s32[1]{0:T(128)} %bitcast.place, bf16[256,6144]{1,0:T(8,128)(2,1)S(1)} %copy-done.4, bf16[256,6144]{1,0:T(8,128)(2,1)S(1)} %copy-done.1, bf16[256,6144]{1,0:T(8,128)(2,1)S(1)} %copy-done.3, f32[48,256]{1,0:T(8,128)S(1)} %bitcast.19, bf16[6,128,128]{2,1,0:T(8,128)(2,1)S(1)} %hop.4.dep), custom_call_target="tpu_custom_call" | custom-call | flops 1 | bytes 1 | tf_op jit(solution)/shard_map/intra/pallas_call | solution.py:101
  35.5 0.0 collective-permute-done.3.rest
  35.5 0.0 collective-permute-done.5.more_0_
  35.5 0.7 hop.5.more_2_
  36.2 0.7 collective-permute-start.8
  36.9 0.0 collective-permute-done.9.more_1_
  36.9 0.7 hop.6.more_2_
  37.6 0.7 collective-permute-start.11
  38.3 0.0 collective-permute-done.8.more_1_
  38.3 0.7 hop.7.more_3_
  39.1 0.7 collective-permute-start.10
  39.8 0.7 side.2
  40.5 0.7 collective-permute-start.13
  41.2 0.0 collective-permute-done.10.more_2_
  41.2 0.7 side.3
  41.9 0.0 copy-start.5
  41.9 0.0 copy-start.7
  41.9 0.0 copy-start.9
  41.9 0.9 collective-permute-start.12
  42.9 2.2 collective-permute-done.13.there
  45.1 0.8 core.2
  45.9 5.0 %collective-permute-start.15 = (f32[2,6,128,128]{3,2,1,0:T(8,128)S(1)}, f32[2,6,128,128]{3,2,1,0:T(8,128)S(1)}, u32[]{:S(2)}, u32[]{:S(2)}) collective-permute-start(f32[2,6,128,128]{3,2,1,0:T(8,128)S(1)} %get-tuple-element.47.dep), channel_id=1, source_target_pairs={{0,1},{1,0},{2,3},{3,2},{4,5},{5,4},{6,7},{7,6},{8,9},{9,8},{10,11... | collective-permute-start | bytes 2359304 | tf_op jit(solution)/shard_map/ppermute | solution.py:287
  50.8 0.7 core.3
  51.6 1.3 collective-permute-start.14
  52.9 0.0 collective-permute-done.15.there
  52.9 0.0 copy-start.8
  52.9 0.0 copy-start.10
  53.0 0.0 copy-start.11
  53.0 2.5 %branch.1 = (f32[256,3072]{1,0:T(8,128)S(1)}, f32[256,128]{1,0:T(8,128)S(1)}) custom-call(s32[1]{0:T(128)} %bitcast.place, bf16[256,6144]{1,0:T(8,128)(2,1)S(1)} %copy-done.4, bf16[256,6144]{1,0:T(8,128)(2,1)S(1)} %copy-done.5, f32[1,6144]{1,0:T(1,128)S(1)} %bitcast.22, f32[48,256]{1,0:T(8,128)S(1)} %bitcast.20, ...), custom_call_target="tpu_custom_call" | custom-call | flops 1 | bytes 1 | tf_op jit(solution)/shard_map/branch/pallas_call | solution.py:142
  55.6 9.5 %finish.1 = bf16[640,6144]{1,0:T(8,128)(2,1)S(1)} custom-call(s32[1]{0:T(128)} %bitcast.place, bf16[256,6144]{1,0:T(8,128)(2,1)S(1)} %copy-done.4, bf16[256,6144]{1,0:T(8,128)(2,1)S(1)} %copy-done.5, f32[1,6144]{1,0:T(1,128)S(1)} %bitcast.23, f32[48,256]{1,0:T(8,128)S(1)} %bitcast.21, f32[2,6,128,128]{3,2,1,0:T(8,128)S(1)} %get-tuple-element.48.own, ...), custom_call_target="tpu_custom_call" | custom-call | flops 1 | bytes 1 | tf_op jit(solution)/shard_map/finish/pallas_call | solution.py:237
  65.1 179.8 %all_to_all.11 = bf16[16,40,6144]{2,1,0:T(8,128)(2,1)S(1)} all-to-all(bf16[16,40,6144]{2,1,0:T(8,128)(2,1)S(1)} %bitcast.9), channel_id=1, replica_groups=mesh['groups'=2,'ctx'=16] {'ctx'}, dimensions={0} | all-to-all | bytes 15728640 | tf_op jit(solution)/shard_map/all_to_all | solution.py:485
  244.9 3.2 %land.1 = bf16[1,640,6144]{2,1,0:T(8,128)(2,1)} custom-call(bf16[640,6144]{1,0:T(8,128)(2,1)S(1)} %bitcast.10), custom_call_target="tpu_custom_call" | custom-call | flops 1 | bytes 1 | tf_op jit(solution)/shard_map/land/pallas_call | solution.py:273
  (18 shorter events, 0.0 us)
Async XLA Ops:
  0.0 1.9 copy-start
  1.9 1.9 copy-start.2
  3.8 0.8 copy-start.6
  5.6 2.7 %collective-permute-start = (f32[2,6,136,128]{3,2,1,0:T(8,128)S(1)}, f32[2,6,136,128]{3,2,1,0:T(8,128)S(1)}, u32[]{:S(2)}, u32[]{:S(2)}) collective-permute-start(f32[2,6,136,128]{3,2,1,0:T(8,128)S(1)} %block_states.4.dep), channel_id=1, source_target_pairs={{0,1},{1,0},{2,3},{3,2},{4,5},{5,4},{6,7},{7,6},{8,9},{9,8},{10,11... | collective-permute-start | bytes 2506760 | tf_op jit(solution)/shard_map/ppermute | solution.py:287
  6.7 4.7 %copy-start.1 = (bf16[256,6144]{1,0:T(8,128)(2,1)S(1)}, bf16[256,6144]{1,0:T(8,128)(2,1)}, u32[]{:S(2)}) copy-start(bf16[256,6144]{1,0:T(8,128)(2,1)} %k_ref.15) | copy-start | bytes 9437188
  6.7 4.7 %copy-start.3 = (bf16[256,6144]{1,0:T(8,128)(2,1)S(1)}, bf16[256,6144]{1,0:T(8,128)(2,1)}, u32[]{:S(2)}) copy-start(bf16[256,6144]{1,0:T(8,128)(2,1)} %v_ref.15) | copy-start | bytes 9437188
  7.7 4.6 %collective-permute-start.1 = (f32[2,6,136,128]{3,2,1,0:T(8,128)S(1)}, f32[2,6,136,128]{3,2,1,0:T(8,128)S(1)}, u32[]{:S(2)}, u32[]{:S(2)}) collective-permute-start(f32[2,6,136,128]{3,2,1,0:T(8,128)S(1)} %block_states.6.dep), channel_id=1, source_target_pairs={{0,1},{1,0},{2,3},{3,2},{4,5},{5,4},{6,7},{7,6},{8,9},{9,8},{10,11... | collective-permute-start | bytes 2506760 | tf_op jit(solution)/shard_map/ppermute | solution.py:287
  9.1 9.2 %collective-permute-start.4 = (bf16[6,144,128]{2,1,0:T(8,128)(2,1)S(1)}, bf16[6,144,128]{2,1,0:T(8,128)(2,1)S(1)}, u32[]{:S(2)}, u32[]{:S(2)}) collective-permute-start(bf16[6,144,128]{2,1,0:T(8,128)(2,1)S(1)} %get-tuple-element.38), channel_id=1, source_target_pairs={{0,2},{1,3},{2,0},{3,1},{4,6},{5,7},{6,4},{7,5},{8,10},{9,11},{10,... | collective-permute-start | bytes 663560 | tf_op jit(solution)/shard_map/ppermute | solution.py:287
  11.4 2.7 %copy-start.4 = (bf16[256,6144]{1,0:T(8,128)(2,1)S(1)}, bf16[256,6144]{1,0:T(8,128)(2,1)}, u32[]{:S(2)}) copy-start(bf16[256,6144]{1,0:T(8,128)(2,1)} %q_ref.11) | copy-start | bytes 9437188
  13.1 12.9 %collective-permute-start.2 = (bf16[6,144,128]{2,1,0:T(8,128)(2,1)S(1)}, bf16[6,144,128]{2,1,0:T(8,128)(2,1)S(1)}, u32[]{:S(2)}, u32[]{:S(2)}) collective-permute-start(bf16[6,144,128]{2,1,0:T(8,128)(2,1)S(1)} %get-tuple-element.33), channel_id=1, source_target_pairs={{0,2},{1,3},{2,0},{3,1},{4,6},{5,7},{6,4},{7,5},{8,10},{9,11},{10,... | collective-permute-start | bytes 663560 | tf_op jit(solution)/shard_map/ppermute | solution.py:287
  17.6 13.4 %collective-permute-start.6 = (bf16[6,128,128]{2,1,0:T(8,128)(2,1)S(1)}, bf16[6,128,128]{2,1,0:T(8,128)(2,1)S(1)}, u32[]{:S(2)}, u32[]{:S(2)}) collective-permute-start(bf16[6,128,128]{2,1,0:T(8,128)(2,1)S(1)} %get-tuple-element.39.dep), channel_id=1, source_target_pairs={{0,2},{1,3},{2,0},{3,1},{4,6},{5,7},{6,4},{7,5},{8,10},{9,11},{10,... | collective-permute-start | bytes 589832 | tf_op jit(solution)/shard_map/ppermute | solution.py:287
  18.9 12.1 %collective-permute-start.7 = (bf16[6,128,128]{2,1,0:T(8,128)(2,1)S(1)}, bf16[6,128,128]{2,1,0:T(8,128)(2,1)S(1)}, u32[]{:S(2)}, u32[]{:S(2)}) collective-permute-start(bf16[6,128,128]{2,1,0:T(8,128)(2,1)S(1)} %row.2.dep), channel_id=1, source_target_pairs={{0,4},{1,5},{2,6},{3,7},{16,20},{17,21},{18,22},{19,23}} | collective-permute-start | bytes 589832 | tf_op jit(solution)/shard_map/ppermute | solution.py:440
  22.1 13.4 %collective-permute-start.3 = (bf16[6,128,128]{2,1,0:T(8,128)(2,1)S(1)}, bf16[6,128,128]{2,1,0:T(8,128)(2,1)S(1)}, u32[]{:S(2)}, u32[]{:S(2)}) collective-permute-start(bf16[6,128,128]{2,1,0:T(8,128)(2,1)S(1)} %get-tuple-element.37), channel_id=1, source_target_pairs={{0,2},{1,3},{2,0},{3,1},{4,6},{5,7},{6,4},{7,5},{8,10},{9,11},{10,... | collective-permute-start | bytes 589832 | tf_op jit(solution)/shard_map/ppermute | solution.py:287
  26.7 8.9 %collective-permute-start.5 = (bf16[6,128,128]{2,1,0:T(8,128)(2,1)S(1)}, bf16[6,128,128]{2,1,0:T(8,128)(2,1)S(1)}, u32[]{:S(2)}, u32[]{:S(2)}) collective-permute-start(bf16[6,128,128]{2,1,0:T(8,128)(2,1)S(1)} %row.3.dep), channel_id=1, source_target_pairs={{0,4},{1,5},{2,6},{3,7},{16,20},{17,21},{18,22},{19,23}} | collective-permute-start | bytes 589832 | tf_op jit(solution)/shard_map/ppermute | solution.py:440
  31.7 5.2 %collective-permute-start.9 = (bf16[6,128,128]{2,1,0:T(8,128)(2,1)S(1)}, bf16[6,128,128]{2,1,0:T(8,128)(2,1)S(1)}, u32[]{:S(2)}, u32[]{:S(2)}) collective-permute-start(bf16[6,128,128]{2,1,0:T(8,128)(2,1)S(1)} %hop.4.dep), channel_id=1, source_target_pairs={{4,8},{5,9},{6,10},{7,11},{20,24},{21,25},{22,26},{23,27}} | collective-permute-start | bytes 589832 | tf_op jit(solution)/shard_map/ppermute | solution.py:440
  36.2 2.1 collective-permute-start.8
  37.6 2.1 collective-permute-start.11
  39.1 2.1 collective-permute-start.10
  40.5 4.6 %collective-permute-start.13 = (bf16[6,128,128]{2,1,0:T(8,128)(2,1)S(1)}, bf16[6,128,128]{2,1,0:T(8,128)(2,1)S(1)}, u32[]{:S(2)}, u32[]{:S(2)}) collective-permute-start(bf16[6,128,128]{2,1,0:T(8,128)(2,1)S(1)} %get-tuple-element.43.more_3_), channel_id=1, source_target_pairs={{0,2},{1,3},{2,0},{3,1},{4,6},{5,7},{6,4},{7,5},{8,10},{9,11},{10,... | collective-permute-start | bytes 589832 | tf_op jit(solution)/shard_map/ppermute | solution.py:287
  41.9 11.0 %copy-start.5 = (bf16[256,6144]{1,0:T(8,128)(2,1)S(1)}, bf16[256,6144]{1,0:T(8,128)(2,1)}, u32[]{:S(2)}) copy-start(bf16[256,6144]{1,0:T(8,128)(2,1)} %gate_ref.3) | copy-start | bytes 9437188
  41.9 11.0 %copy-start.7 = (f32[256,48]{0,1:T(8,128)S(1)}, f32[256,48]{0,1:T(8,128)}, u32[]{:S(2)}) copy-start(f32[256,48]{0,1:T(8,128)} %param.12) | copy-start | bytes 147460
  41.9 11.0 %copy-start.9 = (f32[6144]{0:T(1024)S(1)}, f32[6144]{0:T(1024)}, u32[]{:S(2)}) copy-start(f32[6144]{0:T(1024)} %param.15) | copy-start | bytes 73732
  41.9 8.9 %collective-permute-start.12 = (bf16[6,128,128]{2,1,0:T(8,128)(2,1)S(1)}, bf16[6,128,128]{2,1,0:T(8,128)(2,1)S(1)}, u32[]{:S(2)}, u32[]{:S(2)}) collective-permute-start(bf16[6,128,128]{2,1,0:T(8,128)(2,1)S(1)} %get-tuple-element.45.dep), channel_id=1, source_target_pairs={{0,2},{1,3},{2,0},{3,1},{4,6},{5,7},{6,4},{7,5},{8,10},{9,11},{10,... | collective-permute-start | bytes 589832 | tf_op jit(solution)/shard_map/ppermute | solution.py:287
  45.9 7.1 %collective-permute-start.15 = (f32[2,6,128,128]{3,2,1,0:T(8,128)S(1)}, f32[2,6,128,128]{3,2,1,0:T(8,128)S(1)}, u32[]{:S(2)}, u32[]{:S(2)}) collective-permute-start(f32[2,6,128,128]{3,2,1,0:T(8,128)S(1)} %get-tuple-element.47.dep), channel_id=1, source_target_pairs={{0,1},{1,0},{2,3},{3,2},{4,5},{5,4},{6,7},{7,6},{8,9},{9,8},{10,11... | collective-permute-start | bytes 2359304 | tf_op jit(solution)/shard_map/ppermute | solution.py:287
  51.6 3.9 %collective-permute-start.14 = (f32[2,6,128,128]{3,2,1,0:T(8,128)S(1)}, f32[2,6,128,128]{3,2,1,0:T(8,128)S(1)}, u32[]{:S(2)}, u32[]{:S(2)}) collective-permute-start(f32[2,6,128,128]{3,2,1,0:T(8,128)S(1)} %get-tuple-element.49.dep), channel_id=1, source_target_pairs={{0,1},{1,0},{2,3},{3,2},{4,5},{5,4},{6,7},{7,6},{8,9},{9,8},{10,11... | collective-permute-start | bytes 2359304 | tf_op jit(solution)/shard_map/ppermute | solution.py:287
  52.9 2.6 %copy-start.8 = (bf16[256,6144]{1,0:T(8,128)(2,1)S(1)}, bf16[256,6144]{1,0:T(8,128)(2,1)}, u32[]{:S(2)}) copy-start(bf16[256,6144]{1,0:T(8,128)(2,1)} %rest_6_.1) | copy-start | bytes 9437188
  52.9 2.6 %copy-start.10 = (f32[6144]{0:T(1024)S(1)}, f32[6144]{0:T(1024)}, u32[]{:S(2)}) copy-start(f32[6144]{0:T(1024)} %param.16) | copy-start | bytes 73732
  53.0 2.6 %copy-start.11 = (s32[256,2]{0,1:T(2,128)S(1)}, s32[256,2]{0,1:T(2,128)}, u32[]{:S(2)}) copy-start(s32[256,2]{0,1:T(2,128)} %param.17) | copy-start | bytes 6148

commit v4 on v3

--- a/solution.py
+++ b/solution.py
@@ -23,10 +23,7 @@
     return lax.dot_general(a, b, ((contract[:1], contract[1:]), ((), ())), preferred_element_type=F32)
 
 
-def running(ld_ref, group, count):
-    ld = ld_ref[:count, :]
-    for g in range(1, ld_ref.shape[0] // count):
-        ld = jnp.where(group == g, ld_ref[g * count : (g + 1) * count, :], ld)
+def running(ld):
     tok = ld.shape[1]
     row = lax.broadcasted_iota(jnp.int32, (tok, tok), 0)
     col = lax.broadcasted_iota(jnp.int32, (tok, tok), 1)
@@ -38,13 +35,49 @@
     return dot(high, upper) + (dot(mid, upper) + dot(low, upper))
 
 
+def start_kernel(cap, experts, ld_ref, ids_ref, dep, cum_ref, target_ref):
+    cum_ref[...] = running(ld_ref[...])
+    top, tok = ids_ref.shape
+    ids = ids_ref[...]
+    expert = lax.broadcasted_iota(jnp.int32, (experts, tok), 0)
+    hot = [(ids[k : k + 1, :] == expert).astype(F32) for k in range(top)]
+    row = lax.broadcasted_iota(jnp.int32, (tok, tok), 0)
+    col = lax.broadcasted_iota(jnp.int32, (tok, tok), 1)
+    count = dot(sum(hot).astype(BF16), (row < col).astype(F32).astype(BF16))
+    for k in range(top):
+        slot = jnp.sum(hot[k] * count, axis=0, keepdims=True).astype(jnp.int32)
+        target_ref[k : k + 1, :] = ids[k : k + 1, :] * cap + slot
+        count = count + hot[k]
+
+
+def start(log_decay, ids, dep, cap, experts):
+    return pl.pallas_call(
+        functools.partial(start_kernel, cap, experts),
+        in_specs=[VMEM] * 2 + [ANY],
+        out_specs=[VMEM] * 2,
+        out_shape=[jax.ShapeDtypeStruct(a.shape, a.dtype) for a in (log_decay, ids)],
+        compiler_params=pltpu.CompilerParams(vmem_limit_bytes=16 << 20),
+        cost_estimate=BRIEF,
+        name="start",
+    )(log_decay, ids, dep)
+
+
+def group_rows(cum, group, first, count):
+    size = cum.shape[0] // SLOTS
+    rows = cum[first : first + count]
+    for g in range(1, SLOTS):
+        rows = jnp.where(group == g, cum[g * size + first : g * size + first + count], rows)
+    return rows
+
+
 def state_kernel(first_slot, chunk, hd, place, k_ref, v_ref, ld_ref, dep, out):
     per = out.shape[1]
+    cum = running(ld_ref[...])
     for j in range(2):
         group = jnp.bitwise_xor(j + first_slot, place[0])
-        cum = running(ld_ref, group, per * CHUNKS)[chunk * per : (chunk + 1) * per]
-        total = cum[:, -1:]
-        weight = jnp.exp(total - cum)
+        rows = group_rows(cum, group, chunk * per, per)
+        total = rows[:, -1:]
+        weight = jnp.exp(total - rows)
         decay = jnp.exp(total)
         for i in range(per):
             cols = pl.ds(pl.multiple_of(((group * CHUNKS + chunk) * per + i) * hd, hd), hd)
@@ -66,13 +99,13 @@
     )(place, key_rows, value_rows, log_decay, dep)
 
 
-def intra_kernel(hd, slot, place, q_ref, k_ref, v_ref, ld_ref, dep, *outs):
+def intra_kernel(hd, slot, place, q_ref, k_ref, v_ref, cum_ref, dep, *outs):
     tok, cw = outs[0].shape
     per = cw // hd
     gh = per * CHUNKS
     half = tok // 2
     group = jnp.bitwise_xor(slot, place[0])
-    cum_rows = running(ld_ref, group, gh)
+    cum_rows = group_rows(cum_ref[...], group, 0, gh)
     cum = cum_rows.T
     row = lax.broadcasted_iota(jnp.int32, (half, half), 0)
     col = lax.broadcasted_iota(jnp.int32, (half, half), 1)
@@ -82,20 +115,24 @@
         o_ref, to = outs[i // per], slice(i % per * hd, (i % per + 1) * hd)
         down, across = cum[:, i : i + 1], cum_rows[i : i + 1, :]
         q, k, v = q_ref[:, cols], k_ref[:, cols], v_ref[:, cols]
-        parts = []
+        score = dot(q, k, (1, 1))
+        diagonal = []
         for first in (0, half):
             at = slice(first, first + half)
-            score = dot(q[at], k[at], (1, 1))
-            weights = jnp.where(causal, score * jnp.exp(down[at] - across[:, at]), 0.0).astype(BF16)
-            parts.append(dot(weights, v[at]))
-        o_ref[:half, to] = parts[0]
+            diagonal.append(jnp.where(causal, score[at, at] * jnp.exp(down[at] - across[:, at]), 0.0).astype(BF16))
         middle = across[:, half - 1 : half]
-        score = dot(q[half:], k[:half], (1, 1))
-        weights = (score * (jnp.exp(down[half:] - middle) * jnp.exp(middle - across[:, :half]))).astype(BF16)
-        o_ref[half:, to] = parts[1] + dot(weights, v[:half])
-
-
-def intra(place, query, key_rows, value_rows, log_decay, dep, slot, hd):
+        below = score[half:, :half] * (jnp.exp(down[half:] - middle) * jnp.exp(middle - across[:, :half]))
+        weights = jnp.concatenate(
+            [
+                jnp.concatenate([diagonal[0], jnp.zeros((half, half), BF16)], axis=1),
+                jnp.concatenate([below.astype(BF16), diagonal[1]], axis=1),
+            ],
+            axis=0,
+        )
+        o_ref[:, to] = dot(weights, v)
+
+
+def intra(place, query, key_rows, value_rows, cum, dep, slot, hd):
     tok, width = query.shape
     cw = width // SLOTS // CHUNKS
     return pl.pallas_call(
@@ -106,152 +143,146 @@
         compiler_params=pltpu.CompilerParams(vmem_limit_bytes=16 << 20),
         cost_estimate=BRIEF,
         name="intra",
-    )(place, query, key_rows, value_rows, log_decay, dep)
-
-
-def add_branch(hd, chunk, place, q_ref, gate_ref, ag_ref, ld_ref, own, there, ins, o_ref):
-    per = own.shape[1]
+    )(place, query, key_rows, value_rows, cum, dep)
+
+
+def add_branch(hd, chunk, slots, place, q_ref, gate_ref, ag_ref, cum_ref, states, ins, o_ref):
+    per = states[0].shape[1]
     cw = per * hd
     squares = 0.0
-    for slot in range(SLOTS):
+    grown = jnp.exp(cum_ref[...])
+    for n, slot in enumerate(slots):
         group = jnp.bitwise_xor(slot, place[0])
-        cum = running(ld_ref, group, per * CHUNKS)[chunk * per : (chunk + 1) * per]
-        grow = jnp.exp(cum).T
+        grow = group_rows(grown, group, chunk * per, per).T
         for i in range(per):
-            carried = (own if slot < 2 else there)[slot % 2, i]
+            carried = states[n // 2][slot % 2, i]
             high = carried.astype(BF16)
             low = (carried - high.astype(F32)).astype(BF16)
             where = pl.ds(pl.multiple_of((group * CHUNKS + chunk) * cw + i * hd, hd), hd)
             q = q_ref[:, where]
-            att = ins[slot][:, i * hd : (i + 1) * hd] + grow[:, i : i + 1] * (dot(q, high) + dot(q, low))
+            att = ins[n][:, i * hd : (i + 1) * hd] + grow[:, i : i + 1] * (dot(q, high) + dot(q, low))
             squares = squares + att * att
             opened = 0.5 * jnp.tanh(0.5 * gate_ref[:, where].astype(F32)) + 0.5
-            o_ref[:, slot * cw + i * hd : slot * cw + (i + 1) * hd] = att * (ag_ref[:, where] * opened)
+            o_ref[:, n * cw + i * hd : n * cw + (i + 1) * hd] = att * (ag_ref[:, where] * opened)
     return squares
 
 
-def branch_kernel(hd, chunk, place, q_ref, gate_ref, ag_ref, ld_ref, own, there, dep, *rest):
-    o_ref, sq_ref = rest[SLOTS:]
+def branch_kernel(hd, chunk, slots, place, q_ref, gate_ref, ag_ref, cum_ref, state, dep, *rest):
+    o_ref, sq_ref = rest[-2:]
     sq_ref[...] = add_branch(
-        hd, chunk, place, q_ref, gate_ref, ag_ref, ld_ref, own, there, rest[:SLOTS], o_ref
+        hd, chunk, slots, place, q_ref, gate_ref, ag_ref, cum_ref, (state,), rest[:-2], o_ref
     )
 
 
-def branch(place, query, gate, attn_gain, log_decay, states, intra_outs, dep, chunk, hd):
+def branch(place, query, gate, attn_gain, cum, states, intra_outs, dep, chunk, side, hd):
     tok, width = query.shape
-    return pl.pallas_call(
-        functools.partial(branch_kernel, hd, chunk),
-        in_specs=[SMEM] + [VMEM] * 6 + [ANY] + [VMEM] * SLOTS,
+    slots = (2 * side, 2 * side + 1)
+    return pl.pallas_call(
+        functools.partial(branch_kernel, hd, chunk, slots),
+        in_specs=[SMEM] + [VMEM] * 5 + [ANY] + [VMEM] * 2,
         out_specs=[VMEM] * 2,
         out_shape=[
-            jax.ShapeDtypeStruct((tok, width // CHUNKS), F32),
+            jax.ShapeDtypeStruct((tok, 2 * (width // SLOTS // CHUNKS)), F32),
             jax.ShapeDtypeStruct((tok, hd), F32),
         ],
         compiler_params=pltpu.CompilerParams(vmem_limit_bytes=16 << 20),
         cost_estimate=BRIEF,
         name="branch",
-    )(place, query, gate, attn_gain, log_decay, *states, dep, *intra_outs)
-
-
-def finish_kernel(hd, cap, place, q_ref, gate_ref, ag_ref, ld_ref, own, there, dep, *rest):
-    ins, rest = rest[:SLOTS], rest[SLOTS:]
-    early, rest = rest[: CHUNKS - 1], rest[CHUNKS - 1 :]
-    squares, rest = rest[: CHUNKS - 1], rest[CHUNKS - 1 :]
-    res_ref, mg_ref, ids_ref, o_hbm, late, sq, hidden, normed, target, staged, sems = rest
+    )(place, query, gate, attn_gain, cum, states[side], dep, *[intra_outs[j][chunk] for j in slots])
+
+
+def finish_kernel(hd, place, q_ref, gate_ref, ag_ref, cum_ref, there, dep, *rest):
+    ins, rest = rest[:2], rest[2:]
+    count = 2 * CHUNKS - 1
+    early, squares, rest = rest[:count], rest[count : 2 * count], rest[2 * count :]
+    res_ref, mg_ref, target, o_hbm, late, sq, sums, hidden, normed, pick, staged, sems = rest
     tok, width = normed.shape
-    per = own.shape[1]
+    per = there.shape[1]
     cw = per * hd
-
-    top = ids_ref.shape[0]
-    experts = o_hbm.shape[0] // cap
-    ids = ids_ref[...]
-    expert = lax.broadcasted_iota(jnp.int32, (experts, tok), 0)
-    hot = [(ids[k : k + 1, :] == expert).astype(F32) for k in range(top)]
-    row = lax.broadcasted_iota(jnp.int32, (tok, tok), 0)
-    col = lax.broadcasted_iota(jnp.int32, (tok, tok), 1)
-    count = dot(sum(hot).astype(BF16), (row < col).astype(F32).astype(BF16))
-    for k in range(top):
-        slot = jnp.sum(hot[k] * count, axis=0, keepdims=True).astype(jnp.int32)
-        target[k : k + 1, :] = ids[k : k + 1, :] * cap + slot
-        count = count + hot[k]
+    top = target.shape[0]
 
     part = add_branch(
-        hd, CHUNKS - 1, place, q_ref, gate_ref, ag_ref, ld_ref, own, there, ins, late
+        hd, CHUNKS - 1, (2, 3), place, q_ref, gate_ref, ag_ref, cum_ref, (there,), ins, late
     )
     for s in squares:
         part = part + s[...]
-    sq[...] = part
-
-    rows = hidden.shape[0]
+    rows = tok // 4
+    scale = lax.rsqrt(jnp.sum(part, axis=-1, keepdims=True) / width + 1e-06)
+    sq[...] = jnp.broadcast_to(scale, sq.shape)
 
     @pl.loop(0, tok // rows)
     def _(step):
         at = pl.ds(pl.multiple_of(step * rows, rows), rows)
-        scale = lax.rsqrt(jnp.sum(sq[at, :], axis=-1, keepdims=True) / width + 1e-06)
+        scale = sq[at, :]
         total = jnp.zeros((rows, LANES), F32)
         for slot in range(SLOTS):
             group = jnp.bitwise_xor(slot, place[0])
             for k in range(CHUNKS):
                 for n in range(cw // LANES):
-                    here = slice(slot * cw + n * LANES, slot * cw + (n + 1) * LANES)
+                    source = (*early, late)[2 * k + slot // 2]
+                    here = slice(slot % 2 * cw + n * LANES, slot % 2 * cw + (n + 1) * LANES)
                     where = pl.ds(pl.multiple_of((group * CHUNKS + k) * cw + n * LANES, LANES), LANES)
-                    value = (early[k] if k < CHUNKS - 1 else late)[at, here]
+                    value = source[at, here]
                     value = res_ref[at, where].astype(F32) + value * scale
                     total = total + value * value
-                    hidden[:, where] = value
-        scale = lax.rsqrt(jnp.sum(total, axis=-1, keepdims=True) / width + 1e-06)
+                    hidden[at, where] = value
+        sums[at, :] = total
+
+    scale = lax.rsqrt(jnp.sum(sums[...], axis=-1, keepdims=True) / width + 1e-06)
+    sq[...] = jnp.broadcast_to(scale, sq.shape)
+
+    @pl.loop(0, tok // rows)
+    def _(step):
+        at = pl.ds(pl.multiple_of(step * rows, rows), rows)
+        scale = sq[at, :]
         for n in range(width // LANES):
             cols = slice(n * LANES, (n + 1) * LANES)
-            normed[at, cols] = (hidden[:, cols] * scale * mg_ref[:, cols]).astype(BF16)
-
+            normed[at, cols] = (hidden[at, cols] * scale * mg_ref[:, cols]).astype(BF16)
+
+    row = lax.broadcasted_iota(jnp.int32, (o_hbm.shape[0], tok), 0)
+    hit = row == target[0:1, :]
+    for k in range(1, top):
+        hit = hit | (row == target[k : k + 1, :])
+    pick[...] = hit.astype(F32).astype(BF16)
     steps = sems.shape[0]
-    out_rows = o_hbm.shape[0] // steps
-
-    def copy(step):
-        at = pl.ds(pl.multiple_of(step * out_rows, out_rows), out_rows)
-        return pltpu.make_async_copy(staged.at[at], o_hbm.at[at], sems.at[step])
-
-    @pl.loop(0, steps)
-    def _(step):
-        at = pl.ds(pl.multiple_of(step * out_rows, out_rows), out_rows)
-        row = lax.broadcasted_iota(jnp.int32, (out_rows, tok), 0) + step * out_rows
-        hit = row == target[0:1, :]
-        for k in range(1, top):
-            hit = hit | (row == target[k : k + 1, :])
-        pick = hit.astype(F32).astype(BF16)
-        part = width // 4
-        for n in range(4):
-            cols = slice(n * part, (n + 1) * part)
-            staged[at, cols] = dot(pick, normed[:, cols]).astype(BF16)
-        copy(step).start()
-
+    block = width // steps
+    copies = []
     for step in range(steps):
-        copy(step).wait()
-
-
-def finish(
-    place, query, gate, attn_gain, log_decay, states, intra_outs, early, squares, residual, moe_gain, ids, dep, cap, experts, hd
-):
+        for n in range(step * block, (step + 1) * block, 2 * LANES):
+            cols = slice(n, n + 2 * LANES)
+            staged[:, cols] = dot(pick[...], normed[:, cols]).astype(BF16)
+        cols = pl.ds(step * block, block)
+        copies.append(pltpu.make_async_copy(staged.at[:, cols], o_hbm.at[:, cols], sems.at[step]))
+        copies[-1].start()
+    for c in copies:
+        c.wait()
+
+
+def finish(place, query, gate, attn_gain, cum, there, intra_outs, early, squares, residual, moe_gain, target, dep, rows, hd):
     tok, width = query.shape
     steps = 4
     return pl.pallas_call(
-        functools.partial(finish_kernel, hd, cap),
-        in_specs=[SMEM] + [VMEM] * 6 + [ANY] + [VMEM] * (SLOTS + 2 * (CHUNKS - 1) + 3),
+        functools.partial(finish_kernel, hd),
+        in_specs=[SMEM] + [VMEM] * 5 + [ANY] + [VMEM] * (2 + 2 * (2 * CHUNKS - 1) + 3),
         out_specs=pl.BlockSpec(memory_space=pl.ANY),
         scratch_shapes=[
-            pltpu.VMEM((tok, width // CHUNKS), F32),
-            pltpu.VMEM((tok, hd), F32),
-            pltpu.VMEM((tok // 4, width), F32),
+            pltpu.VMEM((tok, width // CHUNKS // 2), F32),
+            pltpu.VMEM((tok, LANES), F32),
+            pltpu.VMEM((tok, LANES), F32),
+            pltpu.VMEM((tok, width), F32),
             pltpu.VMEM((tok, width), BF16),
-            pltpu.VMEM((8, tok), jnp.int32),
-            pltpu.VMEM((experts * cap, width), BF16),
+            pltpu.VMEM((rows, tok), BF16),
+            pltpu.VMEM((rows, width), BF16),
             pltpu.SemaphoreType.DMA((steps,)),
         ],
-        out_shape=jax.ShapeDtypeStruct((experts * cap, width), BF16),
-        compiler_params=pltpu.CompilerParams(vmem_limit_bytes=24 << 20),
+        out_shape=jax.ShapeDtypeStruct((rows, width), BF16),
+        compiler_params=pltpu.CompilerParams(vmem_limit_bytes=28 << 20),
         cost_estimate=BRIEF,
         name="finish",
-    )(place, query, gate, attn_gain, log_decay, *states, dep, *intra_outs, *early, *squares, residual, moe_gain, ids)
+    )(
+        place, query, gate, attn_gain, cum, there, dep, *[o[-1] for o in intra_outs[2:]],
+        *early, *squares, residual, moe_gain, target,
+    )
 
 
 def land_kernel(i_ref, o_ref, sems):
@@ -398,6 +429,8 @@
     core, side = jnp.bitwise_and(index, 1), jnp.bitwise_and(lax.shift_right_logical(index, 1), 1)
     place = (2 * core + side)[None]
     flags = jnp.stack([2 * core + side, core, side])
+    expert_count = EXP_DEV * size
+    capacity = 5 * tok_rows * expert_ids.shape[1] // (4 * expert_count)
     ld = log_decay.T
     ag, mg = attn_gain[None], moe_gain[None]
     full, wire, plain = (per, hd + TAIL, hd), (per, hd + 2 * TAIL, hd), (per, hd, hd)
@@ -417,6 +450,9 @@
     for k in range(CHUNKS):
         dep = block_states(place, key_rows, value_rows, ld, dep, 2, k, hd)
         received.append(swap(dep, 1))
+        if k == 1:
+            cum, target = start(ld, expert_ids.T, dep, capacity, expert_count)
+            dep = cum
         if k:
             dep = chip(k - 1, dep)
         dep = block_states(place, key_rows, value_rows, ld, dep, 0, k, hd)
@@ -430,7 +466,7 @@
 
     def more_intra(dep):
         if len(intra_outs) < SLOTS:
-            intra_outs.append(intra(place, query, key_rows, value_rows, ld, dep, len(intra_outs), hd))
+            intra_outs.append(intra(place, query, key_rows, value_rows, cum, dep, len(intra_outs), hd))
             dep = intra_outs[-1][0]
         return dep
 
@@ -468,19 +504,15 @@
                 core_kernel, "core", flags, [keep[k], received[k], here[k], there[k]], dep, [((2,) + plain, F32)] * 2
             )
             states[k] = (own, swap(dep, 1))
+            for chunk, half in ((k - 1, 1), (k, 0)):
+                if chunk >= 0:
+                    dep, sq = branch(place, query, gate_input, ag, cum, states[chunk], intra_outs, dep, chunk, half, hd)
+                    early.append(dep)
+                    squares.append(sq)
         dep = more_intra(dep)
-    while len(intra_outs) < SLOTS:
-        dep = more_intra(dep)
-    for k in range(CHUNKS - 1):
-        dep, sq = branch(place, query, gate_input, ag, ld, states[k], [o[k] for o in intra_outs], dep, k, hd)
-        early.append(dep)
-        squares.append(sq)
-
-    expert_count = EXP_DEV * size
-    capacity = 5 * tok_rows * expert_ids.shape[1] // (4 * expert_count)
     outgoing = finish(
-        place, query, gate_input, ag, ld, states[-1], [o[-1] for o in intra_outs], early, squares,
-        residual, mg, expert_ids.T, dep, capacity, expert_count, hd,
+        place, query, gate_input, ag, cum, states[-1][1], intra_outs, early, squares,
+        residual, mg, target, dep, expert_count * capacity, hd,
     )
     return land(lax.all_to_all(outgoing, "ctx", split_axis=0, concat_axis=0, tiled=True))
 

time: 249 us -> 246 us (0.988)
  Pallas kernels: 40.3 us -> 33.8 us
  blocking collectives: 180 us -> 183 us
    pallas_call x4, Pallas kernels: 11.9 us -> 7.12 us  [intra(): pl.pallas_call(functools.partial(intra_kernel, hd, slot), in_specs=[SMEM]...]
    all_to_all x1, blocking collectives: 180 us -> 183 us  [body(): lax.all_to_all(outgoing, 'ctx', split_axis=0, concat_axis=0, tiled=True)]
    pallas_call x2 -> x5, Pallas kernels: 12.1 us -> 11.1 us  [the longest x1 7.64 us: finish(): pl.pallas_call(functools.partial(finish_kernel, hd), in_specs=[SMEM] + [V...]
    unnamed x24 -> x20, local copies, waits for them, and re-layouts: 4.63 us -> 5.4 us
  transfers between devices with their start and end apart: 16 -> 16, of which waited for: 1 -> 1; matrix products, arithmetic and copies ran while one was open for 0% -> 0% of each run, Pallas kernels for 11% -> 9%
where the time goes in v4:
time: 246 us; the launch traced here: 245 us
  blocking collectives  183 us (74%)
  Pallas kernels  33.8 us (14%)
  starting transfers between devices  19.9 us (8%)
  local copies, waits for them, and re-layouts  5.4 us (2%)
    all_to_all x1, blocking collectives, body(): lax.all_to_all(outgoing, 'ctx', split_axis=0, concat_axis=0, tiled=True)  183 us
    ppermute x10, starting transfers between devices, swap(): return lax.ppermute(value, 'ctx', [(i, i ^ bit) for i in range(size)])  12.4 us
    pallas_call x13, Pallas kernels, small(): pl.pallas_call(kernel, in_specs=[SMEM] + [VMEM] * len(ins) + [ANY], out_s...  9.21 us
    pallas_call x1, Pallas kernels, finish(): pl.pallas_call(functools.partial(finish_kernel, hd), in_specs=[SMEM] + [V...  7.64 us
    ppermute x6, starting transfers between devices, hop(): arrived[k].append(lax.ppermute(sent, 'ctx', pairs))  7.52 us
    pallas_call x4, Pallas kernels, intra(): pl.pallas_call(functools.partial(intra_kernel, hd, slot), in_specs=[SMEM]...  7.12 us
    unnamed x20, local copies, waits for them, and re-layouts  5.4 us
  transfers between devices with their start and end apart: 16, of which 1 were waited for; matrix products, arithmetic and copies ran while one was open for 0% of the time, Pallas kernels for 9%

profile of v4, /device:TPU:1, one launch (start us, length us, event | category | flops | bytes accessed | tf_op | source)
XLA Modules:
  0.0 245.5 jit_solution(4254110060376723018)
XLA Ops:
  0.0 1.9 copy-done
  1.9 1.9 copy-done.2
  3.8 0.8 copy-done.6
  4.6 0.8 block_states.4.dep
  5.4 0.1 collective-permute-start
  5.5 0.8 block_states.5.dep.keep
  6.3 0.0 copy-start.1
  6.3 0.8 block_states.6.dep
  7.1 0.5 collective-permute-start.1
  7.6 0.2 start.1
  7.9 0.1 pad_add_fusion.flags
  7.9 0.0 collective-permute-done.received
  7.9 0.8 chip.2
  8.7 2.3 collective-permute-start.4
  11.0 0.8 block_states.7.keep.dep
  11.8 0.0 collective-permute-done.1.received
  11.8 0.7 chip.3
  12.6 0.5 collective-permute-start.2
  13.0 1.8 intra.4
  14.8 0.6 late.1
  15.4 1.1 collective-permute-start.6
  16.5 0.0 collective-permute-done.4.other
  16.5 0.6 row.2.dep
  17.2 3.2 %collective-permute-start.7 = (bf16[6,128,128]{2,1,0:T(8,128)(2,1)S(1)}, bf16[6,128,128]{2,1,0:T(8,128)(2,1)S(1)}, u32[]{:S(2)}, u32[]{:S(2)}) collective-permute-start(bf16[6,128,128]{2,1,0:T(8,128)(2,1)S(1)} %row.2.dep), channel_id=1, source_target_pairs={{0,4},{1,5},{2,6},{3,7},{16,20},{17,21},{18,22},{19,23}} | collective-permute-start | bytes 589832 | tf_op jit(solution)/shard_map/ppermute | solution.py:476
  20.4 1.1 collective-permute-start.3
  21.5 1.8 intra.5
  23.2 0.0 collective-permute-done.2.other
  23.3 0.6 row.3.dep
  23.9 1.3 collective-permute-start.5
  25.2 1.8 intra.6
  27.0 0.0 collective-permute-done.6.rest
  27.0 0.0 collective-permute-done.7.more_0_
  27.0 0.7 hop.4.dep
  27.7 0.7 collective-permute-start.9
  28.4 1.8 intra.7
  30.2 0.0 collective-permute-done.5.more_0_
  30.2 0.7 hop.5.more_2_
  30.9 0.7 collective-permute-start.8
  31.6 0.7 hop.6.more_2_
  32.3 0.7 collective-permute-start.11
  33.0 0.7 hop.7.more_3_
  33.7 0.0 copy-start.4
  33.8 0.0 copy-start.7
  33.8 1.0 collective-permute-start.10
  34.8 0.0 collective-permute-done.11.more_2_
  34.8 0.8 side.2
  35.5 1.0 collective-permute-start.13
  36.5 0.0 collective-permute-done.10.more_2_
  36.5 0.7 side.3
  37.3 0.6 collective-permute-start.12
  37.9 2.2 collective-permute-done.13.there
  40.1 0.8 core.2
  40.9 5.0 %collective-permute-start.15 = (f32[2,6,128,128]{3,2,1,0:T(8,128)S(1)}, f32[2,6,128,128]{3,2,1,0:T(8,128)S(1)}, u32[]{:S(2)}, u32[]{:S(2)}) collective-permute-start(f32[2,6,128,128]{3,2,1,0:T(8,128)S(1)} %get-tuple-element.55.dep), channel_id=1, source_target_pairs={{0,1},{1,0},{2,3},{3,2},{4,5},{5,4},{6,7},{7,6},{8,9},{9,8},{10,11... | collective-permute-start | bytes 2359304 | tf_op jit(solution)/shard_map/ppermute | solution.py:318
  45.9 1.1 branch.3
  47.0 0.8 core.3
  47.7 0.2 collective-permute-start.14
  48.0 1.1 branch.4
  49.1 0.0 copy-start.5
  49.1 0.0 copy-start.8
  49.1 1.1 branch.5
  50.2 0.8 copy-done.5
  50.9 7.6 %finish.1 = bf16[640,6144]{1,0:T(8,128)(2,1)S(1)} custom-call(s32[1]{0:T(128)} %bitcast.place, bf16[256,6144]{1,0:T(8,128)(2,1)S(1)} %copy-done.3, bf16[256,6144]{1,0:T(8,128)(2,1)S(1)} %copy-done.4, f32[1,6144]{1,0:T(1,128)S(1)} %bitcast.20, f32[48,256]{1,0:T(8,128)S(1)} %get-tuple-element.37.dep.cum_ref, ...), custom_call_target="tpu_custom_call" | custom-call | flops 1 | bytes 1 | tf_op jit(solution)/shard_map/finish/pallas_call | solution.py:264
  58.6 183.5 %all_to_all.11 = bf16[16,40,6144]{2,1,0:T(8,128)(2,1)S(1)} all-to-all(bf16[16,40,6144]{2,1,0:T(8,128)(2,1)S(1)} %bitcast.9), channel_id=1, replica_groups=mesh['groups'=2,'ctx'=16] {'ctx'}, dimensions={0} | all-to-all | bytes 15728640 | tf_op jit(solution)/shard_map/all_to_all | solution.py:517
  242.1 3.2 %land.1 = bf16[1,640,6144]{2,1,0:T(8,128)(2,1)} custom-call(bf16[640,6144]{1,0:T(8,128)(2,1)S(1)} %bitcast.10), custom_call_target="tpu_custom_call" | custom-call | flops 1 | bytes 1 | tf_op jit(solution)/shard_map/land/pallas_call | solution.py:304
  (17 shorter events, 0.0 us)
Async XLA Ops:
  0.0 1.9 copy-start
  1.9 1.9 copy-start.2
  3.8 0.8 copy-start.6
  5.4 2.6 %collective-permute-start = (f32[2,6,136,128]{3,2,1,0:T(8,128)S(1)}, f32[2,6,136,128]{3,2,1,0:T(8,128)S(1)}, u32[]{:S(2)}, u32[]{:S(2)}) collective-permute-start(f32[2,6,136,128]{3,2,1,0:T(8,128)S(1)} %block_states.4.dep), channel_id=1, source_target_pairs={{0,1},{1,0},{2,3},{3,2},{4,5},{5,4},{6,7},{7,6},{8,9},{9,8},{10,11... | collective-permute-start | bytes 2506760 | tf_op jit(solution)/shard_map/ppermute | solution.py:318
  6.3 1.3 copy-start.9
  6.3 4.7 %copy-start.1 = (bf16[256,6144]{1,0:T(8,128)(2,1)S(1)}, bf16[256,6144]{1,0:T(8,128)(2,1)}, u32[]{:S(2)}) copy-start(bf16[256,6144]{1,0:T(8,128)(2,1)} %k_ref.15) | copy-start | bytes 9437188
  7.1 4.7 %collective-permute-start.1 = (f32[2,6,136,128]{3,2,1,0:T(8,128)S(1)}, f32[2,6,136,128]{3,2,1,0:T(8,128)S(1)}, u32[]{:S(2)}, u32[]{:S(2)}) collective-permute-start(f32[2,6,136,128]{3,2,1,0:T(8,128)S(1)} %block_states.6.dep), channel_id=1, source_target_pairs={{0,1},{1,0},{2,3},{3,2},{4,5},{5,4},{6,7},{7,6},{8,9},{9,8},{10,11... | collective-permute-start | bytes 2506760 | tf_op jit(solution)/shard_map/ppermute | solution.py:318
  8.7 7.8 %collective-permute-start.4 = (bf16[6,144,128]{2,1,0:T(8,128)(2,1)S(1)}, bf16[6,144,128]{2,1,0:T(8,128)(2,1)S(1)}, u32[]{:S(2)}, u32[]{:S(2)}) collective-permute-start(bf16[6,144,128]{2,1,0:T(8,128)(2,1)S(1)} %get-tuple-element.45), channel_id=1, source_target_pairs={{0,2},{1,3},{2,0},{3,1},{4,6},{5,7},{6,4},{7,5},{8,10},{9,11},{10,... | collective-permute-start | bytes 663560 | tf_op jit(solution)/shard_map/ppermute | solution.py:318
  11.0 2.0 copy-start.3
  12.6 10.7 %collective-permute-start.2 = (bf16[6,144,128]{2,1,0:T(8,128)(2,1)S(1)}, bf16[6,144,128]{2,1,0:T(8,128)(2,1)S(1)}, u32[]{:S(2)}, u32[]{:S(2)}) collective-permute-start(bf16[6,144,128]{2,1,0:T(8,128)(2,1)S(1)} %get-tuple-element.40), channel_id=1, source_target_pairs={{0,2},{1,3},{2,0},{3,1},{4,6},{5,7},{6,4},{7,5},{8,10},{9,11},{10,... | collective-permute-start | bytes 663560 | tf_op jit(solution)/shard_map/ppermute | solution.py:318
  15.4 11.6 %collective-permute-start.6 = (bf16[6,128,128]{2,1,0:T(8,128)(2,1)S(1)}, bf16[6,128,128]{2,1,0:T(8,128)(2,1)S(1)}, u32[]{:S(2)}, u32[]{:S(2)}) collective-permute-start(bf16[6,128,128]{2,1,0:T(8,128)(2,1)S(1)} %get-tuple-element.46.dep), channel_id=1, source_target_pairs={{0,2},{1,3},{2,0},{3,1},{4,6},{5,7},{6,4},{7,5},{8,10},{9,11},{10,... | collective-permute-start | bytes 589832 | tf_op jit(solution)/shard_map/ppermute | solution.py:318
  17.2 9.8 %collective-permute-start.7 = (bf16[6,128,128]{2,1,0:T(8,128)(2,1)S(1)}, bf16[6,128,128]{2,1,0:T(8,128)(2,1)S(1)}, u32[]{:S(2)}, u32[]{:S(2)}) collective-permute-start(bf16[6,128,128]{2,1,0:T(8,128)(2,1)S(1)} %row.2.dep), channel_id=1, source_target_pairs={{0,4},{1,5},{2,6},{3,7},{16,20},{17,21},{18,22},{19,23}} | collective-permute-start | bytes 589832 | tf_op jit(solution)/shard_map/ppermute | solution.py:476
  20.4 9.8 %collective-permute-start.3 = (bf16[6,128,128]{2,1,0:T(8,128)(2,1)S(1)}, bf16[6,128,128]{2,1,0:T(8,128)(2,1)S(1)}, u32[]{:S(2)}, u32[]{:S(2)}) collective-permute-start(bf16[6,128,128]{2,1,0:T(8,128)(2,1)S(1)} %get-tuple-element.44), channel_id=1, source_target_pairs={{0,2},{1,3},{2,0},{3,1},{4,6},{5,7},{6,4},{7,5},{8,10},{9,11},{10,... | collective-permute-start | bytes 589832 | tf_op jit(solution)/shard_map/ppermute | solution.py:318
  23.9 6.3 %collective-permute-start.5 = (bf16[6,128,128]{2,1,0:T(8,128)(2,1)S(1)}, bf16[6,128,128]{2,1,0:T(8,128)(2,1)S(1)}, u32[]{:S(2)}, u32[]{:S(2)}) collective-permute-start(bf16[6,128,128]{2,1,0:T(8,128)(2,1)S(1)} %row.3.dep), channel_id=1, source_target_pairs={{0,4},{1,5},{2,6},{3,7},{16,20},{17,21},{18,22},{19,23}} | collective-permute-start | bytes 589832 | tf_op jit(solution)/shard_map/ppermute | solution.py:476
  27.7 3.9 %collective-permute-start.9 = (bf16[6,128,128]{2,1,0:T(8,128)(2,1)S(1)}, bf16[6,128,128]{2,1,0:T(8,128)(2,1)S(1)}, u32[]{:S(2)}, u32[]{:S(2)}) collective-permute-start(bf16[6,128,128]{2,1,0:T(8,128)(2,1)S(1)} %hop.4.dep), channel_id=1, source_target_pairs={{4,8},{5,9},{6,10},{7,11},{20,24},{21,25},{22,26},{23,27}} | collective-permute-start | bytes 589832 | tf_op jit(solution)/shard_map/ppermute | solution.py:476
  30.9 2.1 collective-permute-start.8
  32.3 2.4 collective-permute-start.11
  33.7 12.1 %copy-start.4 = (bf16[256,6144]{1,0:T(8,128)(2,1)S(1)}, bf16[256,6144]{1,0:T(8,128)(2,1)}, u32[]{:S(2)}) copy-start(bf16[256,6144]{1,0:T(8,128)(2,1)} %gate_ref.7) | copy-start | bytes 9437188
  33.8 12.1 %copy-start.7 = (f32[6144]{0:T(1024)S(1)}, f32[6144]{0:T(1024)}, u32[]{:S(2)}) copy-start(f32[6144]{0:T(1024)} %param.15) | copy-start | bytes 73732
  33.8 2.8 %collective-permute-start.10 = (bf16[6,128,128]{2,1,0:T(8,128)(2,1)S(1)}, bf16[6,128,128]{2,1,0:T(8,128)(2,1)S(1)}, u32[]{:S(2)}, u32[]{:S(2)}) collective-permute-start(bf16[6,128,128]{2,1,0:T(8,128)(2,1)S(1)} %hop.7.more_3_), channel_id=1, source_target_pairs={{8,12},{9,13},{10,14},{11,15},{24,28},{25,29},{26,30},{27,31}} | collective-permute-start | bytes 589832 | tf_op jit(solution)/shard_map/ppermute | solution.py:476
  35.5 4.6 %collective-permute-start.13 = (bf16[6,128,128]{2,1,0:T(8,128)(2,1)S(1)}, bf16[6,128,128]{2,1,0:T(8,128)(2,1)S(1)}, u32[]{:S(2)}, u32[]{:S(2)}) collective-permute-start(bf16[6,128,128]{2,1,0:T(8,128)(2,1)S(1)} %get-tuple-element.50.more_3_), channel_id=1, source_target_pairs={{0,2},{1,3},{2,0},{3,1},{4,6},{5,7},{6,4},{7,5},{8,10},{9,11},{10,... | collective-permute-start | bytes 589832 | tf_op jit(solution)/shard_map/ppermute | solution.py:318
  37.3 9.7 %collective-permute-start.12 = (bf16[6,128,128]{2,1,0:T(8,128)(2,1)S(1)}, bf16[6,128,128]{2,1,0:T(8,128)(2,1)S(1)}, u32[]{:S(2)}, u32[]{:S(2)}) collective-permute-start(bf16[6,128,128]{2,1,0:T(8,128)(2,1)S(1)} %get-tuple-element.52.dep), channel_id=1, source_target_pairs={{0,2},{1,3},{2,0},{3,1},{4,6},{5,7},{6,4},{7,5},{8,10},{9,11},{10,... | collective-permute-start | bytes 589832 | tf_op jit(solution)/shard_map/ppermute | solution.py:318
  40.9 7.1 %collective-permute-start.15 = (f32[2,6,128,128]{3,2,1,0:T(8,128)S(1)}, f32[2,6,128,128]{3,2,1,0:T(8,128)S(1)}, u32[]{:S(2)}, u32[]{:S(2)}) collective-permute-start(f32[2,6,128,128]{3,2,1,0:T(8,128)S(1)} %get-tuple-element.55.dep), channel_id=1, source_target_pairs={{0,1},{1,0},{2,3},{3,2},{4,5},{5,4},{6,7},{7,6},{8,9},{9,8},{10,11... | collective-permute-start | bytes 2359304 | tf_op jit(solution)/shard_map/ppermute | solution.py:318
  47.7 2.4 collective-permute-start.14
  49.1 1.9 copy-start.5
  49.1 1.9 copy-start.8

commit v5 on v4

--- a/solution.py
+++ b/solution.py
@@ -195,7 +195,7 @@
     ins, rest = rest[:2], rest[2:]
     count = 2 * CHUNKS - 1
     early, squares, rest = rest[:count], rest[count : 2 * count], rest[2 * count :]
-    res_ref, mg_ref, target, o_hbm, late, sq, sums, hidden, normed, pick, staged, sems = rest
+    res_ref, mg_ref, target, o_ref, late, sq, sums, hidden, normed, pick = rest
     tok, width = normed.shape
     per = there.shape[1]
     cw = per * hd
@@ -231,40 +231,24 @@
     scale = lax.rsqrt(jnp.sum(sums[...], axis=-1, keepdims=True) / width + 1e-06)
     sq[...] = jnp.broadcast_to(scale, sq.shape)
 
-    @pl.loop(0, tok // rows)
-    def _(step):
-        at = pl.ds(pl.multiple_of(step * rows, rows), rows)
-        scale = sq[at, :]
-        for n in range(width // LANES):
-            cols = slice(n * LANES, (n + 1) * LANES)
-            normed[at, cols] = (hidden[at, cols] * scale * mg_ref[:, cols]).astype(BF16)
-
-    row = lax.broadcasted_iota(jnp.int32, (o_hbm.shape[0], tok), 0)
+    row = lax.broadcasted_iota(jnp.int32, (o_ref.shape[0], tok), 0)
     hit = row == target[0:1, :]
     for k in range(1, top):
         hit = hit | (row == target[k : k + 1, :])
     pick[...] = hit.astype(F32).astype(BF16)
-    steps = sems.shape[0]
-    block = width // steps
-    copies = []
-    for step in range(steps):
-        for n in range(step * block, (step + 1) * block, 2 * LANES):
-            cols = slice(n, n + 2 * LANES)
-            staged[:, cols] = dot(pick[...], normed[:, cols]).astype(BF16)
-        cols = pl.ds(step * block, block)
-        copies.append(pltpu.make_async_copy(staged.at[:, cols], o_hbm.at[:, cols], sems.at[step]))
-        copies[-1].start()
-    for c in copies:
-        c.wait()
+    for n in range(0, width, 2 * LANES):
+        cols = slice(n, n + 2 * LANES)
+        for at in (slice(n, n + LANES), slice(n + LANES, n + 2 * LANES)):
+            normed[:, at] = (hidden[:, at] * sq[...] * mg_ref[:, at]).astype(BF16)
+        o_ref[:, cols] = dot(pick[...], normed[:, cols]).astype(BF16)
 
 
 def finish(place, query, gate, attn_gain, cum, there, intra_outs, early, squares, residual, moe_gain, target, dep, rows, hd):
     tok, width = query.shape
-    steps = 4
     return pl.pallas_call(
         functools.partial(finish_kernel, hd),
         in_specs=[SMEM] + [VMEM] * 5 + [ANY] + [VMEM] * (2 + 2 * (2 * CHUNKS - 1) + 3),
-        out_specs=pl.BlockSpec(memory_space=pl.ANY),
+        out_specs=VMEM,
         scratch_shapes=[
             pltpu.VMEM((tok, width // CHUNKS // 2), F32),
             pltpu.VMEM((tok, LANES), F32),
@@ -272,8 +256,6 @@
             pltpu.VMEM((tok, width), F32),
             pltpu.VMEM((tok, width), BF16),
             pltpu.VMEM((rows, tok), BF16),
-            pltpu.VMEM((rows, width), BF16),
-            pltpu.SemaphoreType.DMA((steps,)),
         ],
         out_shape=jax.ShapeDtypeStruct((rows, width), BF16),
         compiler_params=pltpu.CompilerParams(vmem_limit_bytes=28 << 20),

time: 246 us -> 244 us (level)
  no operation moved by 1% of the time
where the time goes in v5:
time: 244 us; the launch traced here: 243 us
  blocking collectives  183 us (75%)
  Pallas kernels  31.6 us (13%)
  starting transfers between devices  19.9 us (8%)
  local copies, waits for them, and re-layouts  5.4 us (2%)
    all_to_all x1, blocking collectives, body(): lax.all_to_all(outgoing, 'ctx', split_axis=0, concat_axis=0, tiled=True)  183 us
    ppermute x10, starting transfers between devices, swap(): return lax.ppermute(value, 'ctx', [(i, i ^ bit) for i in range(size)])  12.4 us
    pallas_call x13, Pallas kernels, small(): pl.pallas_call(kernel, in_specs=[SMEM] + [VMEM] * len(ins) + [ANY], out_s...  9.21 us
    ppermute x6, starting transfers between devices, hop(): arrived[k].append(lax.ppermute(sent, 'ctx', pairs))  7.52 us
    pallas_call x4, Pallas kernels, intra(): pl.pallas_call(functools.partial(intra_kernel, hd, slot), in_specs=[SMEM]...  7.12 us
    pallas_call x1, Pallas kernels, finish(): pl.pallas_call(functools.partial(finish_kernel, hd), in_specs=[SMEM] + [V...  5.45 us
    unnamed x20, local copies, waits for them, and re-layouts  5.4 us
  transfers between devices with their start and end apart: 16, of which 1 were waited for; matrix products, arithmetic and copies ran while one was open for 0% of the time, Pallas kernels for 9%

profile of v5, /device:TPU:1, one launch (start us, length us, event | category | flops | bytes accessed | tf_op | source)
XLA Modules:
  0.0 243.3 jit_solution(10064624038532867274)
XLA Ops:
  0.0 1.9 copy-done
  1.9 1.9 copy-done.2
  3.8 0.8 copy-done.6
  4.6 0.8 block_states.4.dep
  5.4 0.1 collective-permute-start
  5.5 0.8 block_states.5.dep.keep
  6.3 0.0 copy-start.1
  6.3 0.8 block_states.6.dep
  7.1 0.5 collective-permute-start.1
  7.6 0.2 start.1
  7.9 0.1 pad_add_fusion.flags
  7.9 0.0 collective-permute-done.received
  7.9 0.8 chip.2
  8.7 2.3 collective-permute-start.4
  11.0 0.8 block_states.7.keep.dep
  11.8 0.0 collective-permute-done.1.received
  11.8 0.7 chip.3
  12.6 0.5 collective-permute-start.2
  13.0 1.8 intra.4
  14.8 0.6 late.1
  15.4 1.1 collective-permute-start.6
  16.5 0.0 collective-permute-done.4.other
  16.5 0.6 row.2.dep
  17.2 3.2 %collective-permute-start.7 = (bf16[6,128,128]{2,1,0:T(8,128)(2,1)S(1)}, bf16[6,128,128]{2,1,0:T(8,128)(2,1)S(1)}, u32[]{:S(2)}, u32[]{:S(2)}) collective-permute-start(bf16[6,128,128]{2,1,0:T(8,128)(2,1)S(1)} %row.2.dep), channel_id=1, source_target_pairs={{0,4},{1,5},{2,6},{3,7},{16,20},{17,21},{18,22},{19,23}} | collective-permute-start | bytes 589832 | tf_op jit(solution)/shard_map/ppermute | solution.py:458
  20.4 1.1 collective-permute-start.3
  21.5 1.8 intra.5
  23.2 0.0 collective-permute-done.2.other
  23.3 0.6 row.3.dep
  23.9 1.3 collective-permute-start.5
  25.2 1.8 intra.6
  27.0 0.0 collective-permute-done.6.rest
  27.0 0.0 collective-permute-done.7.more_0_
  27.0 0.7 hop.4.dep
  27.7 0.7 collective-permute-start.9
  28.4 1.8 intra.7
  30.2 0.0 collective-permute-done.5.more_0_
  30.2 0.7 hop.5.more_2_
  30.9 0.7 collective-permute-start.8
  31.6 0.7 hop.6.more_2_
  32.3 0.7 collective-permute-start.11
  33.0 0.7 hop.7.more_3_
  33.7 0.0 copy-start.4
  33.8 0.0 copy-start.7
  33.8 1.0 collective-permute-start.10
  34.8 0.0 collective-permute-done.11.more_2_
  34.8 0.8 side.2
  35.5 1.0 collective-permute-start.13
  36.5 0.0 collective-permute-done.10.more_2_
  36.5 0.7 side.3
  37.3 0.6 collective-permute-start.12
  37.9 2.2 collective-permute-done.13.there
  40.1 0.8 core.2
  40.9 5.0 %collective-permute-start.15 = (f32[2,6,128,128]{3,2,1,0:T(8,128)S(1)}, f32[2,6,128,128]{3,2,1,0:T(8,128)S(1)}, u32[]{:S(2)}, u32[]{:S(2)}) collective-permute-start(f32[2,6,128,128]{3,2,1,0:T(8,128)S(1)} %get-tuple-element.55.dep), channel_id=1, source_target_pairs={{0,1},{1,0},{2,3},{3,2},{4,5},{5,4},{6,7},{7,6},{8,9},{9,8},{10,11... | collective-permute-start | bytes 2359304 | tf_op jit(solution)/shard_map/ppermute | solution.py:300
  45.9 1.1 branch.3
  47.0 0.8 core.3
  47.7 0.2 collective-permute-start.14
  48.0 1.1 branch.4
  49.1 0.0 copy-start.5
  49.1 0.0 copy-start.8
  49.1 1.1 branch.5
  50.2 0.8 copy-done.5
  50.9 5.4 %finish.1 = bf16[640,6144]{1,0:T(8,128)(2,1)S(1)} custom-call(s32[1]{0:T(128)} %bitcast.place, bf16[256,6144]{1,0:T(8,128)(2,1)S(1)} %copy-done.3, bf16[256,6144]{1,0:T(8,128)(2,1)S(1)} %copy-done.4, f32[1,6144]{1,0:T(1,128)S(1)} %bitcast.20, f32[48,256]{1,0:T(8,128)S(1)} %get-tuple-element.37.dep.cum_ref, ...), custom_call_target="tpu_custom_call" | custom-call | flops 1 | bytes 1 | tf_op jit(solution)/shard_map/finish/pallas_call | solution.py:248
  56.4 183.5 %all_to_all.11 = bf16[16,40,6144]{2,1,0:T(8,128)(2,1)S(1)} all-to-all(bf16[16,40,6144]{2,1,0:T(8,128)(2,1)S(1)} %bitcast.9), channel_id=1, replica_groups=mesh['groups'=2,'ctx'=16] {'ctx'}, dimensions={0} | all-to-all | bytes 15728640 | tf_op jit(solution)/shard_map/all_to_all | solution.py:499
  239.9 3.2 %land.1 = bf16[1,640,6144]{2,1,0:T(8,128)(2,1)} custom-call(bf16[640,6144]{1,0:T(8,128)(2,1)S(1)} %bitcast.10), custom_call_target="tpu_custom_call" | custom-call | flops 1 | bytes 1 | tf_op jit(solution)/shard_map/land/pallas_call | solution.py:286
  (17 shorter events, 0.0 us)
Async XLA Ops:
  0.0 1.9 copy-start
  1.9 1.9 copy-start.2
  3.8 0.8 copy-start.6
  5.4 2.6 %collective-permute-start = (f32[2,6,136,128]{3,2,1,0:T(8,128)S(1)}, f32[2,6,136,128]{3,2,1,0:T(8,128)S(1)}, u32[]{:S(2)}, u32[]{:S(2)}) collective-permute-start(f32[2,6,136,128]{3,2,1,0:T(8,128)S(1)} %block_states.4.dep), channel_id=1, source_target_pairs={{0,1},{1,0},{2,3},{3,2},{4,5},{5,4},{6,7},{7,6},{8,9},{9,8},{10,11... | collective-permute-start | bytes 2506760 | tf_op jit(solution)/shard_map/ppermute | solution.py:300
  6.3 1.3 copy-start.9
  6.3 4.7 %copy-start.1 = (bf16[256,6144]{1,0:T(8,128)(2,1)S(1)}, bf16[256,6144]{1,0:T(8,128)(2,1)}, u32[]{:S(2)}) copy-start(bf16[256,6144]{1,0:T(8,128)(2,1)} %k_ref.15) | copy-start | bytes 9437188
  7.1 4.7 %collective-permute-start.1 = (f32[2,6,136,128]{3,2,1,0:T(8,128)S(1)}, f32[2,6,136,128]{3,2,1,0:T(8,128)S(1)}, u32[]{:S(2)}, u32[]{:S(2)}) collective-permute-start(f32[2,6,136,128]{3,2,1,0:T(8,128)S(1)} %block_states.6.dep), channel_id=1, source_target_pairs={{0,1},{1,0},{2,3},{3,2},{4,5},{5,4},{6,7},{7,6},{8,9},{9,8},{10,11... | collective-permute-start | bytes 2506760 | tf_op jit(solution)/shard_map/ppermute | solution.py:300
  8.7 7.8 %collective-permute-start.4 = (bf16[6,144,128]{2,1,0:T(8,128)(2,1)S(1)}, bf16[6,144,128]{2,1,0:T(8,128)(2,1)S(1)}, u32[]{:S(2)}, u32[]{:S(2)}) collective-permute-start(bf16[6,144,128]{2,1,0:T(8,128)(2,1)S(1)} %get-tuple-element.45), channel_id=1, source_target_pairs={{0,2},{1,3},{2,0},{3,1},{4,6},{5,7},{6,4},{7,5},{8,10},{9,11},{10,... | collective-permute-start | bytes 663560 | tf_op jit(solution)/shard_map/ppermute | solution.py:300
  11.0 2.0 copy-start.3
  12.6 10.7 %collective-permute-start.2 = (bf16[6,144,128]{2,1,0:T(8,128)(2,1)S(1)}, bf16[6,144,128]{2,1,0:T(8,128)(2,1)S(1)}, u32[]{:S(2)}, u32[]{:S(2)}) collective-permute-start(bf16[6,144,128]{2,1,0:T(8,128)(2,1)S(1)} %get-tuple-element.40), channel_id=1, source_target_pairs={{0,2},{1,3},{2,0},{3,1},{4,6},{5,7},{6,4},{7,5},{8,10},{9,11},{10,... | collective-permute-start | bytes 663560 | tf_op jit(solution)/shard_map/ppermute | solution.py:300
  15.4 11.6 %collective-permute-start.6 = (bf16[6,128,128]{2,1,0:T(8,128)(2,1)S(1)}, bf16[6,128,128]{2,1,0:T(8,128)(2,1)S(1)}, u32[]{:S(2)}, u32[]{:S(2)}) collective-permute-start(bf16[6,128,128]{2,1,0:T(8,128)(2,1)S(1)} %get-tuple-element.46.dep), channel_id=1, source_target_pairs={{0,2},{1,3},{2,0},{3,1},{4,6},{5,7},{6,4},{7,5},{8,10},{9,11},{10,... | collective-permute-start | bytes 589832 | tf_op jit(solution)/shard_map/ppermute | solution.py:300
  17.2 9.8 %collective-permute-start.7 = (bf16[6,128,128]{2,1,0:T(8,128)(2,1)S(1)}, bf16[6,128,128]{2,1,0:T(8,128)(2,1)S(1)}, u32[]{:S(2)}, u32[]{:S(2)}) collective-permute-start(bf16[6,128,128]{2,1,0:T(8,128)(2,1)S(1)} %row.2.dep), channel_id=1, source_target_pairs={{0,4},{1,5},{2,6},{3,7},{16,20},{17,21},{18,22},{19,23}} | collective-permute-start | bytes 589832 | tf_op jit(solution)/shard_map/ppermute | solution.py:458
  20.4 9.8 %collective-permute-start.3 = (bf16[6,128,128]{2,1,0:T(8,128)(2,1)S(1)}, bf16[6,128,128]{2,1,0:T(8,128)(2,1)S(1)}, u32[]{:S(2)}, u32[]{:S(2)}) collective-permute-start(bf16[6,128,128]{2,1,0:T(8,128)(2,1)S(1)} %get-tuple-element.44), channel_id=1, source_target_pairs={{0,2},{1,3},{2,0},{3,1},{4,6},{5,7},{6,4},{7,5},{8,10},{9,11},{10,... | collective-permute-start | bytes 589832 | tf_op jit(solution)/shard_map/ppermute | solution.py:300
  23.9 6.3 %collective-permute-start.5 = (bf16[6,128,128]{2,1,0:T(8,128)(2,1)S(1)}, bf16[6,128,128]{2,1,0:T(8,128)(2,1)S(1)}, u32[]{:S(2)}, u32[]{:S(2)}) collective-permute-start(bf16[6,128,128]{2,1,0:T(8,128)(2,1)S(1)} %row.3.dep), channel_id=1, source_target_pairs={{0,4},{1,5},{2,6},{3,7},{16,20},{17,21},{18,22},{19,23}} | collective-permute-start | bytes 589832 | tf_op jit(solution)/shard_map/ppermute | solution.py:458
  27.7 3.9 %collective-permute-start.9 = (bf16[6,128,128]{2,1,0:T(8,128)(2,1)S(1)}, bf16[6,128,128]{2,1,0:T(8,128)(2,1)S(1)}, u32[]{:S(2)}, u32[]{:S(2)}) collective-permute-start(bf16[6,128,128]{2,1,0:T(8,128)(2,1)S(1)} %hop.4.dep), channel_id=1, source_target_pairs={{4,8},{5,9},{6,10},{7,11},{20,24},{21,25},{22,26},{23,27}} | collective-permute-start | bytes 589832 | tf_op jit(solution)/shard_map/ppermute | solution.py:458
  30.9 2.1 collective-permute-start.8
  32.3 2.4 %collective-permute-start.11 = (bf16[6,128,128]{2,1,0:T(8,128)(2,1)S(1)}, bf16[6,128,128]{2,1,0:T(8,128)(2,1)S(1)}, u32[]{:S(2)}, u32[]{:S(2)}) collective-permute-start(bf16[6,128,128]{2,1,0:T(8,128)(2,1)S(1)} %hop.6.more_2_), channel_id=1, source_target_pairs={{8,12},{9,13},{10,14},{11,15},{24,28},{25,29},{26,30},{27,31}} | collective-permute-start | bytes 589832 | tf_op jit(solution)/shard_map/ppermute | solution.py:458
  33.7 12.1 %copy-start.4 = (bf16[256,6144]{1,0:T(8,128)(2,1)S(1)}, bf16[256,6144]{1,0:T(8,128)(2,1)}, u32[]{:S(2)}) copy-start(bf16[256,6144]{1,0:T(8,128)(2,1)} %gate_ref.7) | copy-start | bytes 9437188
  33.8 12.1 %copy-start.7 = (f32[6144]{0:T(1024)S(1)}, f32[6144]{0:T(1024)}, u32[]{:S(2)}) copy-start(f32[6144]{0:T(1024)} %param.15) | copy-start | bytes 73732
  33.8 2.8 %collective-permute-start.10 = (bf16[6,128,128]{2,1,0:T(8,128)(2,1)S(1)}, bf16[6,128,128]{2,1,0:T(8,128)(2,1)S(1)}, u32[]{:S(2)}, u32[]{:S(2)}) collective-permute-start(bf16[6,128,128]{2,1,0:T(8,128)(2,1)S(1)} %hop.7.more_3_), channel_id=1, source_target_pairs={{8,12},{9,13},{10,14},{11,15},{24,28},{25,29},{26,30},{27,31}} | collective-permute-start | bytes 589832 | tf_op jit(solution)/shard_map/ppermute | solution.py:458
  35.5 4.6 %collective-permute-start.13 = (bf16[6,128,128]{2,1,0:T(8,128)(2,1)S(1)}, bf16[6,128,128]{2,1,0:T(8,128)(2,1)S(1)}, u32[]{:S(2)}, u32[]{:S(2)}) collective-permute-start(bf16[6,128,128]{2,1,0:T(8,128)(2,1)S(1)} %get-tuple-element.50.more_3_), channel_id=1, source_target_pairs={{0,2},{1,3},{2,0},{3,1},{4,6},{5,7},{6,4},{7,5},{8,10},{9,11},{10,... | collective-permute-start | bytes 589832 | tf_op jit(solution)/shard_map/ppermute | solution.py:300
  37.3 9.7 %collective-permute-start.12 = (bf16[6,128,128]{2,1,0:T(8,128)(2,1)S(1)}, bf16[6,128,128]{2,1,0:T(8,128)(2,1)S(1)}, u32[]{:S(2)}, u32[]{:S(2)}) collective-permute-start(bf16[6,128,128]{2,1,0:T(8,128)(2,1)S(1)} %get-tuple-element.52.dep), channel_id=1, source_target_pairs={{0,2},{1,3},{2,0},{3,1},{4,6},{5,7},{6,4},{7,5},{8,10},{9,11},{10,... | collective-permute-start | bytes 589832 | tf_op jit(solution)/shard_map/ppermute | solution.py:300
  40.9 7.1 %collective-permute-start.15 = (f32[2,6,128,128]{3,2,1,0:T(8,128)S(1)}, f32[2,6,128,128]{3,2,1,0:T(8,128)S(1)}, u32[]{:S(2)}, u32[]{:S(2)}) collective-permute-start(f32[2,6,128,128]{3,2,1,0:T(8,128)S(1)} %get-tuple-element.55.dep), channel_id=1, source_target_pairs={{0,1},{1,0},{2,3},{3,2},{4,5},{5,4},{6,7},{7,6},{8,9},{9,8},{10,11... | collective-permute-start | bytes 2359304 | tf_op jit(solution)/shard_map/ppermute | solution.py:300
  47.7 2.4 collective-permute-start.14
  49.1 1.9 copy-start.5
  49.1 1.9 copy-start.8

commit v6 on v5

--- a/solution.py
+++ b/solution.py
@@ -316,12 +316,15 @@
     return decay * before + state
 
 
-def decay_rows(decay, rows):
-    high = decay.astype(BF16).astype(F32)
-    mid = (decay - high).astype(BF16).astype(F32)
-    low = decay - high - mid
-    row = lax.broadcasted_iota(jnp.int32, (decay.shape[0], rows, decay.shape[2]), 1)
-    return jnp.where(row == 0, high, jnp.where(row == 1, mid, jnp.where(row == 2, low, 0.0)))
+def decay_rows(decays, rows):
+    row = lax.broadcasted_iota(jnp.int32, (rows, decays[0].shape[1]), 0)
+    out = jnp.zeros(row.shape, F32)
+    for i, decay in enumerate(decays):
+        high = decay.astype(BF16).astype(F32)
+        mid = (decay - high).astype(BF16).astype(F32)
+        for n, part in enumerate((high, mid, decay - high - mid)):
+            out = jnp.where(row == 3 * i + n, part, out)
+    return out
 
 
 def chip_kernel(flags, keep, received, dep, mine, sent, rest):
@@ -337,25 +340,25 @@
             mine[:, hd:, :] = decay
         else:
             high = state.astype(BF16)
-            sent[:, :hd, :] = high
-            sent[:, hd:, :] = decay_rows(decay[:, :1, :], 2 * TAIL).astype(BF16)
+            per = high.shape[0]
+            for i in range(per):
+                sent[i * hd : (i + 1) * hd, :] = high[i]
+            decays = [decay[i, :1, :] for i in range(per)]
+            sent[per * hd :, :] = decay_rows(decays, sent.shape[0] - per * hd).astype(BF16)
             rest[...] = (state - high.astype(F32)).astype(BF16)
-
-
-def late_kernel(flags, *refs):
-    count = len(refs) // 2
-    for i_ref, o_ref in zip(refs[:count], refs[count + 1 :]):
-        o_ref[...] = i_ref[...]
 
 
 def row_parts(flags, mine, other, rest=None):
     hd = mine.shape[-1]
     low = flags[2] == 0
     a = (mine[:, :hd, :], mine[:, hd : hd + 1, :])
-    state = other[:, :hd, :].astype(F32)
+    per = mine.shape[0]
+    state = other[: per * hd, :].astype(F32).reshape(per, hd, hd)
     if rest is not None:
         state = state + rest[...].astype(F32)
-    b = (state, jnp.sum(other[:, hd:, :].astype(F32), axis=1, keepdims=True))
+    tail = other[per * hd :, :].astype(F32)
+    decays = [tail[i : i + 1] + tail[i + 1 : i + 2] + tail[i + 2 : i + 3] for i in range(0, 3 * per, 3)]
+    b = (state, jnp.stack(decays))
     first = tuple(jnp.where(low, x, y) for x, y in zip(a, b))
     second = tuple(jnp.where(low, y, x) for x, y in zip(a, b))
     return first, second
@@ -415,7 +418,7 @@
     capacity = 5 * tok_rows * expert_ids.shape[1] // (4 * expert_count)
     ld = log_decay.T
     ag, mg = attn_gain[None], moe_gain[None]
-    full, wire, plain = (per, hd + TAIL, hd), (per, hd + 2 * TAIL, hd), (per, hd, hd)
+    full, wire, plain = (per, hd + TAIL, hd), (per * hd + (3 * per + 15) // 16 * 16, hd), (per, hd, hd)
 
     received, keep, mine, other, rest = [], [], [], [], []
     dep = ld
@@ -458,8 +461,6 @@
         arrived[k].append(lax.ppermute(sent, "ctx", pairs))
 
     dep = more_intra(dep)
-    rest = small(late_kernel, "late", flags, rest, dep, [(plain, BF16)] * CHUNKS)
-    dep = rest[0]
     rest = [swap(r, 2) for r in rest]
     order = sorted(((k, stage) for k in range(CHUNKS) for stage in range(hops + 2)), key=lambda r: r[1] + 0.6 * r[0])
     for k, stage in order:

time: 244 us -> 243 us (level)
    pallas_call x13 -> x12, Pallas kernels: 9.21 us -> 8.57 us  [small(): pl.pallas_call(kernel, in_specs=[SMEM] + [VMEM] * len(ins) + [ANY], out_s...]
  transfers between devices with their start and end apart: 16 -> 16, of which waited for: 1 -> 2; matrix products, arithmetic and copies ran while one was open for 0% -> 0% of each run, Pallas kernels for 9% -> 9%
where the time goes in v6:
time: 243 us; the launch traced here: 242 us
  blocking collectives  183 us (75%)
  Pallas kernels  31 us (13%)
  starting transfers between devices  20 us (8%)
  local copies, waits for them, and re-layouts  5.4 us (2%)
  waiting for transfers between devices  2.44 us (1%)
    all_to_all x1, blocking collectives, body(): lax.all_to_all(outgoing, 'ctx', split_axis=0, concat_axis=0, tiled=True)  183 us
    ppermute x10, starting transfers between devices, swap(): return lax.ppermute(value, 'ctx', [(i, i ^ bit) for i in range(size)])  12.6 us
    pallas_call x12, Pallas kernels, small(): pl.pallas_call(kernel, in_specs=[SMEM] + [VMEM] * len(ins) + [ANY], out_s...  8.57 us
    ppermute x6, starting transfers between devices, hop(): arrived[k].append(lax.ppermute(sent, 'ctx', pairs))  7.42 us
    pallas_call x4, Pallas kernels, intra(): pl.pallas_call(functools.partial(intra_kernel, hd, slot), in_specs=[SMEM]...  7.12 us
    pallas_call x1, Pallas kernels, finish(): pl.pallas_call(functools.partial(finish_kernel, hd), in_specs=[SMEM] + [V...  5.43 us
    unnamed x20, local copies, waits for them, and re-layouts  5.4 us
  transfers between devices with their start and end apart: 16, of which 2 were waited for; matrix products, arithmetic and copies ran while one was open for 0% of the time, Pallas kernels for 9%

profile of v6, /device:TPU:1, one launch (start us, length us, event | category | flops | bytes accessed | tf_op | source)
XLA Modules:
  0.0 242.5 jit_solution(5300051692768099376)
XLA Ops:
  0.0 1.9 copy-done
  1.9 1.9 copy-done.2
  3.8 0.8 copy-done.6
  4.6 0.8 block_states.4.dep
  5.4 0.1 collective-permute-start
  5.5 0.8 block_states.5.dep.keep
  6.3 0.0 copy-start.1
  6.3 0.8 block_states.6.dep
  7.1 0.5 collective-permute-start.1
  7.6 0.2 start.1
  7.9 0.1 pad_add_fusion.flags
  7.9 0.0 collective-permute-done.received
  7.9 0.8 chip.2
  8.7 2.3 collective-permute-start.4
  11.0 0.8 block_states.7.keep.dep
  11.8 0.0 collective-permute-done.1.received
  11.8 0.7 chip.3
  12.6 0.5 collective-permute-start.2
  13.0 1.1 collective-permute-start.6
  14.1 1.8 intra.4
  15.9 0.2 collective-permute-done.4.other
  16.0 0.6 row.2.dep
  16.7 3.1 %collective-permute-start.7 = (bf16[6,128,128]{2,1,0:T(8,128)(2,1)S(1)}, bf16[6,128,128]{2,1,0:T(8,128)(2,1)S(1)}, u32[]{:S(2)}, u32[]{:S(2)}) collective-permute-start(bf16[6,128,128]{2,1,0:T(8,128)(2,1)S(1)} %row.2.dep), channel_id=1, source_target_pairs={{0,4},{1,5},{2,6},{3,7},{16,20},{17,21},{18,22},{19,23}} | collective-permute-start | bytes 589832 | tf_op jit(solution)/shard_map/ppermute | solution.py:461
  19.8 1.3 collective-permute-start.3
  21.1 1.8 intra.5
  22.9 0.0 collective-permute-done.2.other
  22.9 0.6 row.3.dep
  23.5 1.3 collective-permute-start.5
  24.8 1.8 intra.6
  26.6 0.0 collective-permute-done.6.rest
  26.6 0.7 hop.4.dep
  27.3 0.7 collective-permute-start.9
  28.0 1.8 intra.7
  29.8 0.0 collective-permute-done.5.more_0_
  29.8 0.7 hop.5.more_2_
  30.5 0.7 collective-permute-start.8
  31.2 0.7 hop.6.more_2_
  31.9 0.7 collective-permute-start.11
  32.6 0.0 collective-permute-done.8.more_1_
  32.6 0.7 hop.7.more_3_
  33.3 0.0 copy-start.4
  33.4 0.0 copy-start.7
  33.4 1.0 collective-permute-start.10
  34.4 0.0 collective-permute-done.11.more_2_
  34.4 0.7 side.2
  35.1 0.7 collective-permute-start.13
  35.8 0.0 collective-permute-done.10.more_2_
  35.8 0.7 side.3
  36.5 0.9 collective-permute-start.12
  37.5 2.3 collective-permute-done.13.there
  39.7 0.8 core.2
  40.5 5.0 %collective-permute-start.15 = (f32[2,6,128,128]{3,2,1,0:T(8,128)S(1)}, f32[2,6,128,128]{3,2,1,0:T(8,128)S(1)}, u32[]{:S(2)}, u32[]{:S(2)}) collective-permute-start(f32[2,6,128,128]{3,2,1,0:T(8,128)S(1)} %get-tuple-element.51.dep), channel_id=1, source_target_pairs={{0,1},{1,0},{2,3},{3,2},{4,5},{5,4},{6,7},{7,6},{8,9},{9,8},{10,11... | collective-permute-start | bytes 2359304 | tf_op jit(solution)/shard_map/ppermute | solution.py:300
  45.5 1.1 branch.3
  46.6 0.8 core.3
  47.3 0.2 collective-permute-start.14
  47.6 1.1 branch.4
  48.6 0.0 copy-start.5
  48.7 0.0 copy-start.8
  48.7 1.1 branch.5
  49.7 0.0 collective-permute-done.14.there
  49.8 0.8 copy-done.5
  50.5 5.4 %finish.1 = bf16[640,6144]{1,0:T(8,128)(2,1)S(1)} custom-call(s32[1]{0:T(128)} %bitcast.place, bf16[256,6144]{1,0:T(8,128)(2,1)S(1)} %copy-done.3, bf16[256,6144]{1,0:T(8,128)(2,1)S(1)} %copy-done.4, f32[1,6144]{1,0:T(1,128)S(1)} %bitcast.20, f32[48,256]{1,0:T(8,128)S(1)} %get-tuple-element.35.dep.cum_ref, ...), custom_call_target="tpu_custom_call" | custom-call | flops 1 | bytes 1 | tf_op jit(solution)/shard_map/finish/pallas_call | solution.py:248
  56.0 183.1 %all_to_all.11 = bf16[16,40,6144]{2,1,0:T(8,128)(2,1)S(1)} all-to-all(bf16[16,40,6144]{2,1,0:T(8,128)(2,1)S(1)} %bitcast.9), channel_id=1, replica_groups=mesh['groups'=2,'ctx'=16] {'ctx'}, dimensions={0} | all-to-all | bytes 15728640 | tf_op jit(solution)/shard_map/all_to_all | solution.py:500
  239.1 3.2 %land.1 = bf16[1,640,6144]{2,1,0:T(8,128)(2,1)} custom-call(bf16[640,6144]{1,0:T(8,128)(2,1)S(1)} %bitcast.10), custom_call_target="tpu_custom_call" | custom-call | flops 1 | bytes 1 | tf_op jit(solution)/shard_map/land/pallas_call | solution.py:286
  (16 shorter events, 0.0 us)
Async XLA Ops:
  0.0 1.9 copy-start
  1.9 1.9 copy-start.2
  3.8 0.8 copy-start.6
  5.4 2.6 %collective-permute-start = (f32[2,6,136,128]{3,2,1,0:T(8,128)S(1)}, f32[2,6,136,128]{3,2,1,0:T(8,128)S(1)}, u32[]{:S(2)}, u32[]{:S(2)}) collective-permute-start(f32[2,6,136,128]{3,2,1,0:T(8,128)S(1)} %block_states.4.dep), channel_id=1, source_target_pairs={{0,1},{1,0},{2,3},{3,2},{4,5},{5,4},{6,7},{7,6},{8,9},{9,8},{10,11... | collective-permute-start | bytes 2506760 | tf_op jit(solution)/shard_map/ppermute | solution.py:300
  6.3 1.3 copy-start.9
  6.3 4.7 %copy-start.1 = (bf16[256,6144]{1,0:T(8,128)(2,1)S(1)}, bf16[256,6144]{1,0:T(8,128)(2,1)}, u32[]{:S(2)}) copy-start(bf16[256,6144]{1,0:T(8,128)(2,1)} %k_ref.15) | copy-start | bytes 9437188
  7.1 4.7 %collective-permute-start.1 = (f32[2,6,136,128]{3,2,1,0:T(8,128)S(1)}, f32[2,6,136,128]{3,2,1,0:T(8,128)S(1)}, u32[]{:S(2)}, u32[]{:S(2)}) collective-permute-start(f32[2,6,136,128]{3,2,1,0:T(8,128)S(1)} %block_states.6.dep), channel_id=1, source_target_pairs={{0,1},{1,0},{2,3},{3,2},{4,5},{5,4},{6,7},{7,6},{8,9},{9,8},{10,11... | collective-permute-start | bytes 2506760 | tf_op jit(solution)/shard_map/ppermute | solution.py:300
  8.7 7.3 %collective-permute-start.4 = (bf16[800,128]{1,0:T(8,128)(2,1)S(1)}, bf16[800,128]{1,0:T(8,128)(2,1)S(1)}, u32[]{:S(2)}, u32[]{:S(2)}) collective-permute-start(bf16[800,128]{1,0:T(8,128)(2,1)S(1)} %get-tuple-element.40), channel_id=1, source_target_pairs={{0,2},{1,3},{2,0},{3,1},{4,6},{5,7},{6,4},{7,5},{8,10},{9,11},{10,... | collective-permute-start | bytes 614408 | tf_op jit(solution)/shard_map/ppermute | solution.py:300
  11.0 3.1 %copy-start.3 = (bf16[256,6144]{1,0:T(8,128)(2,1)S(1)}, bf16[256,6144]{1,0:T(8,128)(2,1)}, u32[]{:S(2)}) copy-start(bf16[256,6144]{1,0:T(8,128)(2,1)} %q_ref.15) | copy-start | bytes 9437188
  12.6 10.3 %collective-permute-start.2 = (bf16[800,128]{1,0:T(8,128)(2,1)S(1)}, bf16[800,128]{1,0:T(8,128)(2,1)S(1)}, u32[]{:S(2)}, u32[]{:S(2)}) collective-permute-start(bf16[800,128]{1,0:T(8,128)(2,1)S(1)} %get-tuple-element.38), channel_id=1, source_target_pairs={{0,2},{1,3},{2,0},{3,1},{4,6},{5,7},{6,4},{7,5},{8,10},{9,11},{10,... | collective-permute-start | bytes 614408 | tf_op jit(solution)/shard_map/ppermute | solution.py:300
  13.0 13.6 %collective-permute-start.6 = (bf16[6,128,128]{2,1,0:T(8,128)(2,1)S(1)}, bf16[6,128,128]{2,1,0:T(8,128)(2,1)S(1)}, u32[]{:S(2)}, u32[]{:S(2)}) collective-permute-start(bf16[6,128,128]{2,1,0:T(8,128)(2,1)S(1)} %get-tuple-element.43), channel_id=1, source_target_pairs={{0,2},{1,3},{2,0},{3,1},{4,6},{5,7},{6,4},{7,5},{8,10},{9,11},{10,... | collective-permute-start | bytes 589832 | tf_op jit(solution)/shard_map/ppermute | solution.py:300
  16.7 10.0 %collective-permute-start.7 = (bf16[6,128,128]{2,1,0:T(8,128)(2,1)S(1)}, bf16[6,128,128]{2,1,0:T(8,128)(2,1)S(1)}, u32[]{:S(2)}, u32[]{:S(2)}) collective-permute-start(bf16[6,128,128]{2,1,0:T(8,128)(2,1)S(1)} %row.2.dep), channel_id=1, source_target_pairs={{0,4},{1,5},{2,6},{3,7},{16,20},{17,21},{18,22},{19,23}} | collective-permute-start | bytes 589832 | tf_op jit(solution)/shard_map/ppermute | solution.py:461
  19.8 10.0 %collective-permute-start.3 = (bf16[6,128,128]{2,1,0:T(8,128)(2,1)S(1)}, bf16[6,128,128]{2,1,0:T(8,128)(2,1)S(1)}, u32[]{:S(2)}, u32[]{:S(2)}) collective-permute-start(bf16[6,128,128]{2,1,0:T(8,128)(2,1)S(1)} %get-tuple-element.39), channel_id=1, source_target_pairs={{0,2},{1,3},{2,0},{3,1},{4,6},{5,7},{6,4},{7,5},{8,10},{9,11},{10,... | collective-permute-start | bytes 589832 | tf_op jit(solution)/shard_map/ppermute | solution.py:300
  23.5 6.3 %collective-permute-start.5 = (bf16[6,128,128]{2,1,0:T(8,128)(2,1)S(1)}, bf16[6,128,128]{2,1,0:T(8,128)(2,1)S(1)}, u32[]{:S(2)}, u32[]{:S(2)}) collective-permute-start(bf16[6,128,128]{2,1,0:T(8,128)(2,1)S(1)} %row.3.dep), channel_id=1, source_target_pairs={{0,4},{1,5},{2,6},{3,7},{16,20},{17,21},{18,22},{19,23}} | collective-permute-start | bytes 589832 | tf_op jit(solution)/shard_map/ppermute | solution.py:461
  27.3 3.9 %collective-permute-start.9 = (bf16[6,128,128]{2,1,0:T(8,128)(2,1)S(1)}, bf16[6,128,128]{2,1,0:T(8,128)(2,1)S(1)}, u32[]{:S(2)}, u32[]{:S(2)}) collective-permute-start(bf16[6,128,128]{2,1,0:T(8,128)(2,1)S(1)} %hop.4.dep), channel_id=1, source_target_pairs={{4,8},{5,9},{6,10},{7,11},{20,24},{21,25},{22,26},{23,27}} | collective-permute-start | bytes 589832 | tf_op jit(solution)/shard_map/ppermute | solution.py:461
  30.5 2.1 collective-permute-start.8
  31.9 2.4 %collective-permute-start.11 = (bf16[6,128,128]{2,1,0:T(8,128)(2,1)S(1)}, bf16[6,128,128]{2,1,0:T(8,128)(2,1)S(1)}, u32[]{:S(2)}, u32[]{:S(2)}) collective-permute-start(bf16[6,128,128]{2,1,0:T(8,128)(2,1)S(1)} %hop.6.more_2_), channel_id=1, source_target_pairs={{8,12},{9,13},{10,14},{11,15},{24,28},{25,29},{26,30},{27,31}} | collective-permute-start | bytes 589832 | tf_op jit(solution)/shard_map/ppermute | solution.py:461
  33.3 12.1 %copy-start.4 = (bf16[256,6144]{1,0:T(8,128)(2,1)S(1)}, bf16[256,6144]{1,0:T(8,128)(2,1)}, u32[]{:S(2)}) copy-start(bf16[256,6144]{1,0:T(8,128)(2,1)} %gate_ref.7) | copy-start | bytes 9437188
  33.4 12.1 %copy-start.7 = (f32[6144]{0:T(1024)S(1)}, f32[6144]{0:T(1024)}, u32[]{:S(2)}) copy-start(f32[6144]{0:T(1024)} %param.15) | copy-start | bytes 73732
  33.4 2.4 collective-permute-start.10
  35.1 4.6 %collective-permute-start.13 = (bf16[6,128,128]{2,1,0:T(8,128)(2,1)S(1)}, bf16[6,128,128]{2,1,0:T(8,128)(2,1)S(1)}, u32[]{:S(2)}, u32[]{:S(2)}) collective-permute-start(bf16[6,128,128]{2,1,0:T(8,128)(2,1)S(1)} %get-tuple-element.46.more_3_), channel_id=1, source_target_pairs={{0,2},{1,3},{2,0},{3,1},{4,6},{5,7},{6,4},{7,5},{8,10},{9,11},{10,... | collective-permute-start | bytes 589832 | tf_op jit(solution)/shard_map/ppermute | solution.py:300
  36.5 10.0 %collective-permute-start.12 = (bf16[6,128,128]{2,1,0:T(8,128)(2,1)S(1)}, bf16[6,128,128]{2,1,0:T(8,128)(2,1)S(1)}, u32[]{:S(2)}, u32[]{:S(2)}) collective-permute-start(bf16[6,128,128]{2,1,0:T(8,128)(2,1)S(1)} %get-tuple-element.48.dep), channel_id=1, source_target_pairs={{0,2},{1,3},{2,0},{3,1},{4,6},{5,7},{6,4},{7,5},{8,10},{9,11},{10,... | collective-permute-start | bytes 589832 | tf_op jit(solution)/shard_map/ppermute | solution.py:300
  40.5 7.1 %collective-permute-start.15 = (f32[2,6,128,128]{3,2,1,0:T(8,128)S(1)}, f32[2,6,128,128]{3,2,1,0:T(8,128)S(1)}, u32[]{:S(2)}, u32[]{:S(2)}) collective-permute-start(f32[2,6,128,128]{3,2,1,0:T(8,128)S(1)} %get-tuple-element.51.dep), channel_id=1, source_target_pairs={{0,1},{1,0},{2,3},{3,2},{4,5},{5,4},{6,7},{7,6},{8,9},{9,8},{10,11... | collective-permute-start | bytes 2359304 | tf_op jit(solution)/shard_map/ppermute | solution.py:300
  47.3 2.4 collective-permute-start.14
  48.6 1.9 copy-start.5
  48.7 1.9 copy-start.8

commit v7 on v6

--- a/solution.py
+++ b/solution.py
@@ -435,9 +435,9 @@
     for k in range(CHUNKS):
         dep = block_states(place, key_rows, value_rows, ld, dep, 2, k, hd)
         received.append(swap(dep, 1))
-        if k == 1:
-            cum, target = start(ld, expert_ids.T, dep, capacity, expert_count)
-            dep = cum
+    cum, target = start(ld, expert_ids.T, dep, capacity, expert_count)
+    dep = cum
+    for k in range(CHUNKS):
         if k:
             dep = chip(k - 1, dep)
         dep = block_states(place, key_rows, value_rows, ld, dep, 0, k, hd)

time: 243 us -> 244 us (level)
  transfers between devices with their start and end apart: 16 -> 16, of which waited for: 2 -> 1; matrix products, arithmetic and copies ran while one was open for 0% -> 0% of each run, Pallas kernels for 9% -> 9%
where the time goes in v7:
time: 244 us
  blocking collectives  185 us (76%)
  Pallas kernels  31 us (13%)
  starting transfers between devices  19.7 us (8%)
  local copies, waits for them, and re-layouts  5.64 us (2%)
    all_to_all x1, blocking collectives, body(): lax.all_to_all(outgoing, 'ctx', split_axis=0, concat_axis=0, tiled=True)  185 us
    ppermute x10, starting transfers between devices, swap(): return lax.ppermute(value, 'ctx', [(i, i ^ bit) for i in range(size)])  12.2 us
    pallas_call x12, Pallas kernels, small(): pl.pallas_call(kernel, in_specs=[SMEM] + [VMEM] * len(ins) + [ANY], out_s...  8.53 us
    ppermute x6, starting transfers between devices, hop(): arrived[k].append(lax.ppermute(sent, 'ctx', pairs))  7.51 us
    pallas_call x4, Pallas kernels, intra(): pl.pallas_call(functools.partial(intra_kernel, hd, slot), in_specs=[SMEM]...  7.13 us
    unnamed x20, local copies, waits for them, and re-layouts  5.64 us
    pallas_call x1, Pallas kernels, finish(): pl.pallas_call(functools.partial(finish_kernel, hd), in_specs=[SMEM] + [V...  5.43 us
  transfers between devices with their start and end apart: 16, of which 1 were waited for; matrix products, arithmetic and copies ran while one was open for 0% of the time, Pallas kernels for 9%

profile of v7, /device:TPU:1, one launch (start us, length us, event | category | flops | bytes accessed | tf_op | source)
XLA Modules:
  0.0 243.7 jit_solution(14996988094352224954)
XLA Ops:
  0.0 1.9 copy-done
  1.9 1.9 copy-done.2
  3.8 0.8 copy-done.6
  4.6 0.8 block_states.4.dep
  5.4 0.0 copy-start.1
  5.4 0.1 collective-permute-start
  5.5 0.8 block_states.5.dep
  6.3 0.5 collective-permute-start.1
  6.8 0.2 start.1
  7.1 0.2 copy-done.1
  7.3 0.8 block_states.6.keep.dep
  8.1 0.1 pad_add_fusion.flags
  8.2 0.0 collective-permute-done.received
  8.2 0.7 chip.2
  8.9 2.1 collective-permute-start.4
  11.0 0.8 block_states.7.keep.dep
  11.8 0.0 collective-permute-done.1.received
  11.8 0.7 chip.3
  12.6 0.1 collective-permute-start.2
  12.7 1.4 collective-permute-start.6
  14.1 1.8 intra.4
  15.9 0.0 collective-permute-done.4.other
  15.9 0.6 row.2.dep
  16.5 3.2 %collective-permute-start.7 = (bf16[6,128,128]{2,1,0:T(8,128)(2,1)S(1)}, bf16[6,128,128]{2,1,0:T(8,128)(2,1)S(1)}, u32[]{:S(2)}, u32[]{:S(2)}) collective-permute-start(bf16[6,128,128]{2,1,0:T(8,128)(2,1)S(1)} %row.2.dep), channel_id=1, source_target_pairs={{0,4},{1,5},{2,6},{3,7},{16,20},{17,21},{18,22},{19,23}} | collective-permute-start | bytes 589832 | tf_op jit(solution)/shard_map/ppermute | solution.py:461
  19.8 1.1 collective-permute-start.3
  20.9 1.8 intra.5
  22.7 0.0 collective-permute-done.2.other
  22.7 0.6 row.3.dep
  23.3 1.3 collective-permute-start.5
  24.6 1.8 intra.6
  26.4 0.0 collective-permute-done.6.rest
  26.5 0.7 hop.4.dep
  27.1 0.7 collective-permute-start.9
  27.8 1.8 intra.7
  29.6 0.0 collective-permute-done.3.rest
  29.6 0.7 hop.5.more_2_
  30.3 0.7 collective-permute-start.8
  31.0 0.7 hop.6.more_2_
  31.7 0.7 collective-permute-start.11
  32.4 0.0 collective-permute-done.8.more_1_
  32.4 0.7 hop.7.more_3_
  33.2 0.0 copy-start.4
  33.2 0.0 copy-start.7
  33.2 1.0 collective-permute-start.10
  34.2 0.0 collective-permute-done.11.more_2_
  34.2 0.7 side.2
  34.9 0.7 collective-permute-start.13
  35.6 0.7 side.3
  36.3 0.9 collective-permute-start.12
  37.3 2.3 collective-permute-done.13.there
  39.5 0.8 core.2
  40.3 5.0 %collective-permute-start.15 = (f32[2,6,128,128]{3,2,1,0:T(8,128)S(1)}, f32[2,6,128,128]{3,2,1,0:T(8,128)S(1)}, u32[]{:S(2)}, u32[]{:S(2)}) collective-permute-start(f32[2,6,128,128]{3,2,1,0:T(8,128)S(1)} %get-tuple-element.51.dep), channel_id=1, source_target_pairs={{0,1},{1,0},{2,3},{3,2},{4,5},{5,4},{6,7},{7,6},{8,9},{9,8},{10,11... | collective-permute-start | bytes 2359304 | tf_op jit(solution)/shard_map/ppermute | solution.py:300
  45.3 1.1 branch.3
  46.4 0.0 collective-permute-done.12.there
  46.4 0.8 core.3
  47.2 0.2 collective-permute-start.14
  47.3 1.1 branch.4
  48.4 0.0 copy-start.5
  48.5 0.0 copy-start.8
  48.5 1.1 branch.5
  49.5 0.8 copy-done.5
  50.3 5.4 %finish.1 = bf16[640,6144]{1,0:T(8,128)(2,1)S(1)} custom-call(s32[1]{0:T(128)} %bitcast.place, bf16[256,6144]{1,0:T(8,128)(2,1)S(1)} %copy-done.3, bf16[256,6144]{1,0:T(8,128)(2,1)S(1)} %copy-done.4, f32[1,6144]{1,0:T(1,128)S(1)} %bitcast.20, f32[48,256]{1,0:T(8,128)S(1)} %get-tuple-element.35.dep.cum_ref, ...), custom_call_target="tpu_custom_call" | custom-call | flops 1 | bytes 1 | tf_op jit(solution)/shard_map/finish/pallas_call | solution.py:248
  55.8 184.6 %all_to_all.11 = bf16[16,40,6144]{2,1,0:T(8,128)(2,1)S(1)} all-to-all(bf16[16,40,6144]{2,1,0:T(8,128)(2,1)S(1)} %bitcast.9), channel_id=1, replica_groups=mesh['groups'=2,'ctx'=16] {'ctx'}, dimensions={0} | all-to-all | bytes 15728640 | tf_op jit(solution)/shard_map/all_to_all | solution.py:500
  240.3 3.2 %land.1 = bf16[1,640,6144]{2,1,0:T(8,128)(2,1)} custom-call(bf16[640,6144]{1,0:T(8,128)(2,1)S(1)} %bitcast.10), custom_call_target="tpu_custom_call" | custom-call | flops 1 | bytes 1 | tf_op jit(solution)/shard_map/land/pallas_call | solution.py:286
  (16 shorter events, 0.0 us)
Async XLA Ops:
  0.0 1.9 copy-start
  1.9 1.9 copy-start.2
  3.8 0.8 copy-start.6
  5.4 1.5 copy-start.9
  5.4 1.9 copy-start.1
  5.4 2.8 %collective-permute-start = (f32[2,6,136,128]{3,2,1,0:T(8,128)S(1)}, f32[2,6,136,128]{3,2,1,0:T(8,128)S(1)}, u32[]{:S(2)}, u32[]{:S(2)}) collective-permute-start(f32[2,6,136,128]{3,2,1,0:T(8,128)S(1)} %block_states.4.dep), channel_id=1, source_target_pairs={{0,1},{1,0},{2,3},{3,2},{4,5},{5,4},{6,7},{7,6},{8,9},{9,8},{10,11... | collective-permute-start | bytes 2506760 | tf_op jit(solution)/shard_map/ppermute | solution.py:300
  6.3 5.5 %collective-permute-start.1 = (f32[2,6,136,128]{3,2,1,0:T(8,128)S(1)}, f32[2,6,136,128]{3,2,1,0:T(8,128)S(1)}, u32[]{:S(2)}, u32[]{:S(2)}) collective-permute-start(f32[2,6,136,128]{3,2,1,0:T(8,128)S(1)} %block_states.5.dep), channel_id=1, source_target_pairs={{0,1},{1,0},{2,3},{3,2},{4,5},{5,4},{6,7},{7,6},{8,9},{9,8},{10,11... | collective-permute-start | bytes 2506760 | tf_op jit(solution)/shard_map/ppermute | solution.py:300
  8.9 7.0 %collective-permute-start.4 = (bf16[800,128]{1,0:T(8,128)(2,1)S(1)}, bf16[800,128]{1,0:T(8,128)(2,1)S(1)}, u32[]{:S(2)}, u32[]{:S(2)}) collective-permute-start(bf16[800,128]{1,0:T(8,128)(2,1)S(1)} %get-tuple-element.40), channel_id=1, source_target_pairs={{0,2},{1,3},{2,0},{3,1},{4,6},{5,7},{6,4},{7,5},{8,10},{9,11},{10,... | collective-permute-start | bytes 614408 | tf_op jit(solution)/shard_map/ppermute | solution.py:300
  11.0 3.1 %copy-start.3 = (bf16[256,6144]{1,0:T(8,128)(2,1)S(1)}, bf16[256,6144]{1,0:T(8,128)(2,1)}, u32[]{:S(2)}) copy-start(bf16[256,6144]{1,0:T(8,128)(2,1)} %q_ref.15) | copy-start | bytes 9437188
  12.6 10.1 %collective-permute-start.2 = (bf16[800,128]{1,0:T(8,128)(2,1)S(1)}, bf16[800,128]{1,0:T(8,128)(2,1)S(1)}, u32[]{:S(2)}, u32[]{:S(2)}) collective-permute-start(bf16[800,128]{1,0:T(8,128)(2,1)S(1)} %get-tuple-element.38), channel_id=1, source_target_pairs={{0,2},{1,3},{2,0},{3,1},{4,6},{5,7},{6,4},{7,5},{8,10},{9,11},{10,... | collective-permute-start | bytes 614408 | tf_op jit(solution)/shard_map/ppermute | solution.py:300
  12.7 13.8 %collective-permute-start.6 = (bf16[6,128,128]{2,1,0:T(8,128)(2,1)S(1)}, bf16[6,128,128]{2,1,0:T(8,128)(2,1)S(1)}, u32[]{:S(2)}, u32[]{:S(2)}) collective-permute-start(bf16[6,128,128]{2,1,0:T(8,128)(2,1)S(1)} %get-tuple-element.43), channel_id=1, source_target_pairs={{0,2},{1,3},{2,0},{3,1},{4,6},{5,7},{6,4},{7,5},{8,10},{9,11},{10,... | collective-permute-start | bytes 589832 | tf_op jit(solution)/shard_map/ppermute | solution.py:300
  16.5 9.9 %collective-permute-start.7 = (bf16[6,128,128]{2,1,0:T(8,128)(2,1)S(1)}, bf16[6,128,128]{2,1,0:T(8,128)(2,1)S(1)}, u32[]{:S(2)}, u32[]{:S(2)}) collective-permute-start(bf16[6,128,128]{2,1,0:T(8,128)(2,1)S(1)} %row.2.dep), channel_id=1, source_target_pairs={{0,4},{1,5},{2,6},{3,7},{16,20},{17,21},{18,22},{19,23}} | collective-permute-start | bytes 589832 | tf_op jit(solution)/shard_map/ppermute | solution.py:461
  19.8 9.9 %collective-permute-start.3 = (bf16[6,128,128]{2,1,0:T(8,128)(2,1)S(1)}, bf16[6,128,128]{2,1,0:T(8,128)(2,1)S(1)}, u32[]{:S(2)}, u32[]{:S(2)}) collective-permute-start(bf16[6,128,128]{2,1,0:T(8,128)(2,1)S(1)} %get-tuple-element.39), channel_id=1, source_target_pairs={{0,2},{1,3},{2,0},{3,1},{4,6},{5,7},{6,4},{7,5},{8,10},{9,11},{10,... | collective-permute-start | bytes 589832 | tf_op jit(solution)/shard_map/ppermute | solution.py:300
  23.3 6.3 %collective-permute-start.5 = (bf16[6,128,128]{2,1,0:T(8,128)(2,1)S(1)}, bf16[6,128,128]{2,1,0:T(8,128)(2,1)S(1)}, u32[]{:S(2)}, u32[]{:S(2)}) collective-permute-start(bf16[6,128,128]{2,1,0:T(8,128)(2,1)S(1)} %row.3.dep), channel_id=1, source_target_pairs={{0,4},{1,5},{2,6},{3,7},{16,20},{17,21},{18,22},{19,23}} | collective-permute-start | bytes 589832 | tf_op jit(solution)/shard_map/ppermute | solution.py:461
  27.1 3.9 %collective-permute-start.9 = (bf16[6,128,128]{2,1,0:T(8,128)(2,1)S(1)}, bf16[6,128,128]{2,1,0:T(8,128)(2,1)S(1)}, u32[]{:S(2)}, u32[]{:S(2)}) collective-permute-start(bf16[6,128,128]{2,1,0:T(8,128)(2,1)S(1)} %hop.4.dep), channel_id=1, source_target_pairs={{4,8},{5,9},{6,10},{7,11},{20,24},{21,25},{22,26},{23,27}} | collective-permute-start | bytes 589832 | tf_op jit(solution)/shard_map/ppermute | solution.py:461
  30.3 2.1 collective-permute-start.8
  31.7 2.4 collective-permute-start.11
  33.2 12.1 %copy-start.4 = (bf16[256,6144]{1,0:T(8,128)(2,1)S(1)}, bf16[256,6144]{1,0:T(8,128)(2,1)}, u32[]{:S(2)}) copy-start(bf16[256,6144]{1,0:T(8,128)(2,1)} %gate_ref.7) | copy-start | bytes 9437188
  33.2 12.1 %copy-start.7 = (f32[6144]{0:T(1024)S(1)}, f32[6144]{0:T(1024)}, u32[]{:S(2)}) copy-start(f32[6144]{0:T(1024)} %param.15) | copy-start | bytes 73732
  33.2 2.4 collective-permute-start.10
  34.9 4.6 %collective-permute-start.13 = (bf16[6,128,128]{2,1,0:T(8,128)(2,1)S(1)}, bf16[6,128,128]{2,1,0:T(8,128)(2,1)S(1)}, u32[]{:S(2)}, u32[]{:S(2)}) collective-permute-start(bf16[6,128,128]{2,1,0:T(8,128)(2,1)S(1)} %get-tuple-element.46.more_3_), channel_id=1, source_target_pairs={{0,2},{1,3},{2,0},{3,1},{4,6},{5,7},{6,4},{7,5},{8,10},{9,11},{10,... | collective-permute-start | bytes 589832 | tf_op jit(solution)/shard_map/ppermute | solution.py:300
  36.3 10.1 %collective-permute-start.12 = (bf16[6,128,128]{2,1,0:T(8,128)(2,1)S(1)}, bf16[6,128,128]{2,1,0:T(8,128)(2,1)S(1)}, u32[]{:S(2)}, u32[]{:S(2)}) collective-permute-start(bf16[6,128,128]{2,1,0:T(8,128)(2,1)S(1)} %get-tuple-element.48.dep), channel_id=1, source_target_pairs={{0,2},{1,3},{2,0},{3,1},{4,6},{5,7},{6,4},{7,5},{8,10},{9,11},{10,... | collective-permute-start | bytes 589832 | tf_op jit(solution)/shard_map/ppermute | solution.py:300
  40.3 7.1 %collective-permute-start.15 = (f32[2,6,128,128]{3,2,1,0:T(8,128)S(1)}, f32[2,6,128,128]{3,2,1,0:T(8,128)S(1)}, u32[]{:S(2)}, u32[]{:S(2)}) collective-permute-start(f32[2,6,128,128]{3,2,1,0:T(8,128)S(1)} %get-tuple-element.51.dep), channel_id=1, source_target_pairs={{0,1},{1,0},{2,3},{3,2},{4,5},{5,4},{6,7},{7,6},{8,9},{9,8},{10,11... | collective-permute-start | bytes 2359304 | tf_op jit(solution)/shard_map/ppermute | solution.py:300
  47.2 2.4 collective-permute-start.14
  48.4 1.9 copy-start.5
  48.5 1.9 copy-start.8
